TPU v7x, 128 devices: a whole 4x4x4 slice. The times are simulated.
128 devices in a mesh: dp: 8 (over x, core), fsdp: 16 (over z, y).
Axes of the slice: x: 4, y: 4, z: 4, core: 2. Of those that a mesh axis runs over, the one named last changes fastest.
Arguments:
- tokens: bfloat16 [512, 256, 768], P('fsdp', 'dp'), may hold values from -6 to 6
- cotangent: bfloat16 [512, 256, 768], P('fsdp', 'dp'), may hold values from -6 to 6
- perm: int32 [512], replicated, may hold values from 0 to 511, as said below
- lengths: int32 [512], P(('dp', 'fsdp')), may hold values from 32 to 256, as said below
- drop: int32 [512], P(('dp', 'fsdp')), may hold values 0 or 1
- w_query: bfloat16 [768, 768], P(('dp', 'fsdp')), may hold values from -0.21875 to 0.21875
- b_query: bfloat16 [768], P(('dp', 'fsdp')), may hold values from -3 to 3
- w_key: bfloat16 [768, 768], P(('dp', 'fsdp')), may hold values from -0.21875 to 0.21875
- w_value: bfloat16 [768, 768], P(('dp', 'fsdp')), may hold values from -0.21875 to 0.21875
- b_value: bfloat16 [768], P(('dp', 'fsdp')), may hold values from -3 to 3
- w_out: bfloat16 [768, 768], P(('dp', 'fsdp')), may hold values from -2 to 2
- b_out: bfloat16 [768], P(('dp', 'fsdp')), may hold values from -3 to 3
- norm1_gain: bfloat16 [768], P(('dp', 'fsdp')), may hold values from 0.5 to 1.5
- norm1_bias: bfloat16 [768], P(('dp', 'fsdp')), may hold values from -3 to 3
- w_inner: bfloat16 [768, 3072], P(('dp', 'fsdp')), may hold values from -0.21875 to 0.21875
- b_inner: bfloat16 [3072], P(('dp', 'fsdp')), may hold values from -3 to 3
- w_outer: bfloat16 [3072, 768], P(('dp', 'fsdp')), may hold values from -0.109375 to 0.109375
- b_outer: bfloat16 [768], P(('dp', 'fsdp')), may hold values from -3 to 3
- norm2_gain: bfloat16 [768], P(('dp', 'fsdp')), may hold values from 0.5 to 1.5
- norm2_bias: bfloat16 [768], P(('dp', 'fsdp')), may hold values from -3 to 3
Outputs:
- layer_out: bfloat16 [512, 256, 768], P('fsdp', 'dp')
- grad_tokens: bfloat16 [512, 256, 768], P('fsdp', 'dp')
- grad_w_query: float32 [768, 768], P(('dp', 'fsdp'))
- grad_b_query: float32 [768], P(('dp', 'fsdp'))
- grad_w_key: float32 [768, 768], P(('dp', 'fsdp'))
- grad_w_value: float32 [768, 768], P(('dp', 'fsdp'))
- grad_b_value: float32 [768], P(('dp', 'fsdp'))
- grad_w_out: float32 [768, 768], P(('dp', 'fsdp'))
- grad_b_out: float32 [768], P(('dp', 'fsdp'))
- grad_norm1_gain: float32 [768], P(('dp', 'fsdp'))
- grad_norm1_bias: float32 [768], P(('dp', 'fsdp'))
- grad_w_inner: float32 [768, 3072], P(('dp', 'fsdp'))
- grad_b_inner: float32 [3072], P(('dp', 'fsdp'))
- grad_w_outer: float32 [3072, 768], P(('dp', 'fsdp'))
- grad_b_outer: float32 [768], P(('dp', 'fsdp'))
- grad_norm2_gain: float32 [768], P(('dp', 'fsdp'))
- grad_norm2_bias: float32 [768], P(('dp', 'fsdp'))
Inputs may be any that keep to these rules, and one draw needn't show every extreme that they name: `perm`: A permutation of the sequences. Dealt slot q = (a * 16 + b) * 4 + j, for dp index a and fsdp index b, holds an input sequence of b's range b * 32 to (b + 1) * 32 - 1. `lengths`: some sequence has 256 tokens and some has 32.
All inputs are finite; a program needn't handle non-finite values. No bound on the sum of `drop` on one device may be relied on, other than what follows from the above.
Results may differ from a plain program's by a relative error of at most 0.02.
Values may be sent and summed in bfloat16 or wider, within the bound.
No kernel may reach another device: no remote copies, remote signals or barrier semaphores. Data moves between devices by JAX's collectives and lax.ppermute only.
A program may use at most 256 MiB of HBM per device.

v0:
```python
import functools
import jax
import jax.numpy as jnp
from jax import lax
from jax.experimental import pallas as pl
from jax.experimental.pallas import tpu as pltpu
from jax.sharding import Mesh
from jax.sharding import PartitionSpec as P

HEADS = 12
HEAD = 64
WIDTH = 768
FF = 3072
SLOT = 256
SEQ_DEV = 4
RING = 4
CORES = 2
PIECE = 32
GROUP = RING * CORES
ROWS = SEQ_DEV * SLOT
PAIR = 2 * HEAD
PACKED = 3 * WIDTH + 512
MIXED = WIDTH + FF

epsilon = 1e-05
bf16 = jnp.bfloat16
f32 = jnp.float32
VMEM_LIMIT = 58 * 1024 * 1024

TN = (((0,), (0,)), ((), ()))
NT = (((1,), (1,)), ((), ()))


def mm(a, b):
    return jnp.dot(a, b, preferred_element_type=f32)


def mm_nt(a, b):
    return lax.dot_general(a, b, NT, preferred_element_type=f32)


def mm_tn(a, b):
    return lax.dot_general(a, b, TN, preferred_element_type=f32)


def joined(ref):
    return ref[...].reshape(SLOT, WIDTH)


def spread(extras, start, width):
    total = 128 * width
    group = lax.broadcasted_iota(jnp.int32, (32, total), 0)
    owner = lax.broadcasted_iota(jnp.int32, (32, total), 1) // width
    pick = lax.broadcasted_iota(jnp.int32, (width, total), 0)
    within = lax.rem(lax.broadcasted_iota(jnp.int32, (width, total), 1), width)
    chosen = (pick == within).astype(bf16)
    out = jnp.zeros((32, total), f32)
    for y in range(RING):
        values = extras[:, 128 * y + start : 128 * y + start + width].astype(bf16)
        out += jnp.where(owner == group * RING + y, mm(values, chosen), 0.0)
    return jnp.sum(out, axis=0, keepdims=True)


def gather_back(vectors):
    values = jnp.zeros((128, 128), f32)
    start = 0
    for vector in vectors:
        total = vector.shape[1]
        width = total // 128
        owner = lax.broadcasted_iota(jnp.int32, (128, total), 1) // width
        mine = owner == lax.broadcasted_iota(jnp.int32, (128, total), 0)
        within = lax.rem(lax.broadcasted_iota(jnp.int32, (total, 128), 0), width)
        column = lax.broadcasted_iota(jnp.int32, (total, 128), 1)
        spots = (column == within + start).astype(bf16)
        values += mm(jnp.where(mine, vector, 0.0).astype(bf16), spots)
        start += width
    row = lax.broadcasted_iota(jnp.int32, (WIDTH, 128), 0)
    device = lax.broadcasted_iota(jnp.int32, (WIDTH, 128), 1)
    within = lax.rem(row, 24)
    picks = (within < RING) & (row // 24 * RING + within == device)
    return mm(picks.astype(bf16), values.astype(bf16)).astype(bf16)


def attention_copies(ids, pieces, w, sems):
    copies = []
    for i, piece in enumerate(pieces):
        x = lax.rem(ids[8] + RING - i // 2, RING)
        c = ids[9] if i % 2 == 0 else 1 - ids[9]
        copies.append(pltpu.make_async_copy(piece, w.at[x, c], sems.at[i]))
    return copies


def half_of(ids, i):
    c = ids[9] if i % 2 == 0 else 1 - ids[9]
    return c, ids[11] // 2 if i // 2 == 0 else 1 - ids[11] // 2


def columns(w, start, end):
    return w[:, :, :, start:end].reshape(WIDTH, end - start)


def attention_forward(
    ids, x_in, p0, p1, p2, p3, p4, p5, p6, p7, perm,
    xt_out, qkv_out, exp_out, norm_out, ctxt_out, vec, bias_out, info,
    w, extras, sems,
):
    s = pl.program_id(0)

    @pl.when(s == 0)
    def _():
        copies = attention_copies(ids, (p0, p1, p2, p3, p4, p5, p6, p7), w, sems)
        for copy in copies:
            copy.start()
        for copy in copies:
            copy.wait()
        rows = columns(w, 3 * WIDTH, PACKED).astype(f32).reshape(32, 24, PACKED - 3 * WIDTH)
        extras[...] = jnp.sum(rows, axis=1)
        for i in range(8):
            vec[i : i + 1] = spread(extras, 6 * i, 6)
        bias_out[...] = spread(extras, 48, 24)

    length = jnp.zeros((1, 1), f32)
    dropped = jnp.zeros((1, 1), f32)
    for y in range(RING):
        hit = perm[:, RING * y : RING * y + 4] == ids[10] + s
        length += jnp.sum(jnp.where(hit, extras[:, 128 * y + 72 : 128 * y + 76], 0.0), keepdims=True)
        dropped += jnp.sum(jnp.where(hit, extras[:, 128 * y + 76 : 128 * y + 80], 0.0), keepdims=True)
    line = lax.broadcasted_iota(jnp.int32, (8, 128), 0)
    info[...] = jnp.where(line == s, length, jnp.where(line == s + 4, dropped, info[...]))

    x = joined(x_in)
    xt_out[...] = x.T
    q = ((mm(x, columns(w, 0, WIDTH)) + vec[0:1]).astype(bf16).astype(f32) * HEAD**-0.5).astype(bf16)
    k = mm(x, columns(w, WIDTH, 2 * WIDTH)).astype(bf16)
    v = (mm(x, columns(w, 2 * WIDTH, 3 * WIDTH)) + vec[1:2]).astype(bf16)
    qkv_out[:, :WIDTH] = q
    qkv_out[:, WIDTH : 2 * WIDTH] = k
    qkv_out[:, 2 * WIDTH :] = v
    q_t = q.T
    v_t = v.T
    keys = lax.broadcasted_iota(jnp.int32, (SLOT, 1), 0).astype(f32)
    bias = jnp.where(keys < length, 0.0, -1e30)
    low = lax.broadcasted_iota(jnp.int32, (SLOT, PAIR), 1) < HEAD
    ctx_t = []
    for h in range(HEADS):
        p = h // 2 * PAIR
        k_pair = k[:, p : p + PAIR]
        k_one = jnp.where(low if h % 2 == 0 else ~low, k_pair, jnp.zeros_like(k_pair))
        scores = mm(k_one, q_t[p : p + PAIR]) + bias
        top = jnp.max(scores, axis=0, keepdims=True)
        expo = jnp.exp(scores - top)
        inverse = 1.0 / jnp.sum(expo, axis=0, keepdims=True)
        norm_out[0, h : h + 1, :] = inverse
        expo = expo.astype(bf16)
        exp_out[0, h] = expo
        ctx_t.append(mm(v_t[h * HEAD : (h + 1) * HEAD], expo) * inverse)
    ctx_t = jnp.concatenate(ctx_t, axis=0).astype(bf16)
    ctxt_out[...] = ctx_t


def row_mean(v):
    return jnp.mean(v, axis=-1, keepdims=True)


def normalised(z):
    center = z - row_mean(z)
    r = lax.rsqrt(row_mean(center * center) + epsilon)
    return center * r, r


def norm_back(dy, zhat, r, gain):
    e = dy * gain
    return r * (e - row_mean(e) - zhat * row_mean(e * zhat))


def col_sum(v):
    return jnp.sum(v, axis=0, keepdims=True)


FF_STEP = 768
FF_STEPS = FF // FF_STEP


def cut_cores(ids, value, away, mine):
    blocks, rows, _ = away.shape
    first = ids[9] == 0
    for x in range(blocks):
        even = value[2 * x * rows : (2 * x + 1) * rows]
        odd = value[(2 * x + 1) * rows : (2 * x + 2) * rows]
        away[x] = jnp.where(first, odd, even)
        mine[x] = jnp.where(first, even, odd)


def feed_forward(
    ids, x_in, c_in, ctx_t, i0, i1, i2, i3, j0, j1, j2, j3, vec, bias_in,
    layer_out, dsum_out, dattn_out, outer_away, outer_mine, inner_away, inner_mine, out_away, out_mine,
    slope, vec_grad, bias_grad, w_in, w_out, hid_t, act_t, d_branches, d_inners, d_attns, in_sems, out_sems,
):
    s = pl.program_id(0)

    @pl.when(s == 0)
    def _():
        vec_grad[...] = jnp.zeros_like(vec_grad)
        bias_grad[...] = jnp.zeros_like(bias_grad)
        copies = []
        for i, (piece, late) in enumerate(zip((i0, i1, i2, i3), (j0, j1, j2, j3))):
            c, z_half = half_of(ids, i)
            y_half = ids[12] // 2 if i // 2 == 0 else 1 - ids[12] // 2
            for d in range(RING):
                x = lax.rem(ids[8] + RING - d, RING)
                copies.append(pltpu.make_async_copy(piece.at[d], w_in.at[x, c, z_half], in_sems.at[i, d]))
                for n in range(RING):
                    target = w_out.at[x, c, n, y_half]
                    copies.append(pltpu.make_async_copy(late.at[n, d], target, out_sems.at[i, d, n]))
        for copy in copies:
            copy.start()
        for copy in copies:
            copy.wait()

    def inner_columns(n):
        return w_in[:, :, :, :, WIDTH + n * FF_STEP : WIDTH + (n + 1) * FF_STEP].reshape(WIDTH, FF_STEP)

    def outer_rows(n):
        return w_out[n].reshape(FF_STEP, WIDTH)

    @pl.when(s < SEQ_DEV)
    def _():
        x = joined(x_in).astype(f32)
        context = ctx_t[:, pl.ds(pl.multiple_of(s * SLOT, SLOT), SLOT)].T
        attn_out = mm(context, w_in[:, :, :, :, :WIDTH].reshape(WIDTH, WIDTH)) + vec[2:3]
        zhat1, r1 = normalised(x + attn_out)
        hidden = zhat1 * vec[3:4] + vec[4:5]
        hid_low = hidden.astype(bf16)
        hid_t[s] = hid_low.T
        branch = jnp.broadcast_to(vec[5:6], (SLOT, WIDTH))
        for n in range(FF_STEPS):
            cols = slice(n * FF_STEP, (n + 1) * FF_STEP)
            inner = mm(hid_low, inner_columns(n)) + bias_in[0:1, cols]
            half = 0.5 * lax.erf(inner * 0.7071067811865476) + 0.5
            bell = 0.3989422804014327 * jnp.exp(-0.5 * (inner * inner))
            act = (inner * half).astype(bf16)
            act_t[s, cols, :] = act.T
            slope[:, cols] = (half + inner * bell).astype(bf16)
            branch += mm(act, outer_rows(n))
        zhat2, r2 = normalised(hidden + branch)
        gain2 = vec[6:7]
        normed = zhat2 * gain2 + vec[7:8]
        valid = (lax.broadcasted_iota(jnp.int32, (SLOT, 1), 0) < ids[s]).astype(f32)
        keep = ids[4 + s] == 0
        layer_out[...] = (jnp.where(keep, normed, x) * valid).astype(bf16)
        dy = joined(c_in).astype(f32) * jnp.where(keep, valid, 0.0)
        vec_grad[1:2] += col_sum(dy * zhat2)
        vec_grad[2:3] += col_sum(dy)
        d_sum2 = norm_back(dy, zhat2, r2, gain2)
        d_branch = d_sum2.astype(bf16)
        d_branches[s] = d_branch
        vec_grad[0:1] += col_sum(d_branch.astype(f32))
        d_hidden = d_sum2
        for n in range(FF_STEPS):
            cols = slice(n * FF_STEP, (n + 1) * FF_STEP)
            d_act = mm_nt(d_branch, outer_rows(n))
            d_inner = (d_act * slope[:, cols].astype(f32)).astype(bf16)
            d_inners[s, n] = d_inner
            bias_grad[0:1, cols] += col_sum(d_inner.astype(f32))
            d_hidden += mm_nt(d_inner, inner_columns(n))
        vec_grad[3:4] += col_sum(d_hidden * zhat1)
        vec_grad[4:5] += col_sum(d_hidden)
        d_sum1 = norm_back(d_hidden, zhat1, r1, vec[3:4])
        dsum_out[...] = d_sum1
        d_attn = d_sum1.astype(bf16)
        dattn_out[...] = d_attn
        d_attns[s] = d_attn
        vec_grad[5:6] += col_sum(d_attn.astype(f32))

    @pl.when((s >= SEQ_DEV) & (s < SEQ_DEV + RING))
    def _():
        rows = pl.ds(pl.multiple_of((s - SEQ_DEV) * FF_STEP, FF_STEP), FF_STEP)
        value = mm(act_t[0, rows, :], d_branches[0])
        for i in range(1, SEQ_DEV):
            value += mm(act_t[i, rows, :], d_branches[i])
        cut_cores(ids, value.astype(bf16), outer_away, outer_mine)

    @pl.when((s >= SEQ_DEV + RING) & (s < SEQ_DEV + RING + FF_STEPS))
    def _():
        n = s - SEQ_DEV - RING
        value = mm(hid_t[0], d_inners[0, n])
        for i in range(1, SEQ_DEV):
            value += mm(hid_t[i], d_inners[i, n])
        cut_cores(ids, value.astype(bf16), inner_away, inner_mine)

    @pl.when(s == SEQ_DEV + RING + FF_STEPS)
    def _():
        value = mm(ctx_t[:, :SLOT], d_attns[0])
        for i in range(1, SEQ_DEV):
            value += mm(ctx_t[:, i * SLOT : (i + 1) * SLOT], d_attns[i])
        block = gather_back([vec_grad[i : i + 1] for i in range(6)] + [bias_grad[...]])
        cut_cores(ids, jnp.concatenate([value.astype(bf16), block], axis=1), out_away, out_mine)


def attention_backward(
    ids, dsum, dattn, qkv, exp_in, norm_in, ctxt_in, x_t, c_in, layer_in, p0, p1, p2, p3, p4, p5, p6, p7, i0, i1, i2, i3,
    back_out, attn_away, attn_mine,
    w, w_out, vec_grad, d_qkv, sems, out_sems,
):
    s = pl.program_id(0)

    @pl.when(s == 0)
    def _():
        vec_grad[...] = jnp.zeros_like(vec_grad)
        copies = attention_copies(ids, (p0, p1, p2, p3, p4, p5, p6, p7), w, sems)
        for i, piece in enumerate((i0, i1, i2, i3)):
            c, z_half = half_of(ids, i)
            for d in range(RING):
                x = lax.rem(ids[8] + RING - d, RING)
                source = piece.at[d, :, pl.ds(0, WIDTH)]
                copies.append(pltpu.make_async_copy(source, w_out.at[x, c, z_half], out_sems.at[i, d]))
        for copy in copies:
            copy.start()
        for copy in copies:
            copy.wait()

    @pl.when(s < SEQ_DEV)
    def _():
        d_sum1 = dsum[...]
        dctx_t = mm_nt(dattn[...], w_out[...].reshape(WIDTH, WIDTH)).T
        ctx_t = ctxt_in[...].astype(f32)
        k_t = qkv[:, WIDTH : 2 * WIDTH].T
        scaled = []
        deltas = []
        for h in range(HEADS):
            rows = slice(h * HEAD, (h + 1) * HEAD)
            one = (dctx_t[rows] * norm_in[0, h : h + 1, :]).astype(bf16)
            scaled.append(one)
            deltas.append(col_sum(one.astype(f32) * ctx_t[rows]))
        dctx_t = jnp.concatenate(scaled, axis=0)
        dctx = dctx_t.T
        low = lax.broadcasted_iota(jnp.int32, (SLOT, PAIR), 1) < HEAD
        dq_t = []
        for p in range(0, WIDTH, PAIR):
            cols = slice(p, p + PAIR)
            q_pair = qkv[:, cols]
            v_pair = qkv[:, 2 * WIDTH + p : 2 * WIDTH + p + PAIR]
            dks = []
            dvs = []
            for half in range(2):
                h = p // HEAD + half
                v_one = jnp.where(low if half == 0 else ~low, v_pair, jnp.zeros_like(v_pair))
                d_probs = mm(v_one, dctx_t[cols]) - deltas[h]
                expo = exp_in[0, h]
                d_scores = (expo.astype(f32) * d_probs).astype(bf16)
                dvs.append(mm(expo, dctx[:, cols]))
                dks.append(mm(d_scores, q_pair))
                dq_t.append(mm(k_t[h * HEAD : (h + 1) * HEAD], d_scores))
            d_qkv[s, 1, :, cols] = jnp.where(low, dks[0], dks[1]).astype(bf16)
            d_qkv[s, 2, :, cols] = jnp.where(low, dvs[0], dvs[1]).astype(bf16)
        dq = (jnp.concatenate(dq_t, axis=0).T * HEAD**-0.5).astype(bf16)
        d_qkv[s, 0] = dq
        vec_grad[0:1] += col_sum(dq.astype(f32))
        vec_grad[1:2] += col_sum(d_qkv[s, 2].astype(f32))
        d_in = d_sum1
        for n in range(3):
            d_in += mm_nt(d_qkv[s, n], columns(w, n * WIDTH, (n + 1) * WIDTH))
        valid = (lax.broadcasted_iota(jnp.int32, (SLOT, 1), 0) < ids[s]).astype(f32)
        upstream = joined(c_in).astype(f32) * valid
        keep = ids[4 + s] == 0
        grad = jnp.where(keep, d_in, upstream).astype(bf16)
        back_out[:, 0, 0] = layer_in[...].reshape(GROUP, PIECE, WIDTH)
        back_out[:, 1, 0] = grad.reshape(GROUP, PIECE, WIDTH)

    @pl.when(s == SEQ_DEV)
    def _():
        values = []
        for n in range(3):
            value = mm(x_t[:, :SLOT], d_qkv[0, n])
            for i in range(1, SEQ_DEV):
                value += mm(x_t[:, i * SLOT : (i + 1) * SLOT], d_qkv[i, n])
            values.append(value.astype(bf16))
        values.append(gather_back([vec_grad[0:1], vec_grad[1:2]]))
        cut_cores(ids, jnp.concatenate(values, axis=1), attn_away, attn_mine)


def in_order(values, me):
    ordered = []
    for j in range(RING):
        step = lax.rem(me + RING - j, RING)
        value = values[0]
        for d in (1, 2, 3):
            value = jnp.where(step == d, values[d], value)
        ordered.append(value)
    return ordered


def pack_rows(ids, query, key, value, out, inner, row, packed):
    for i, ref in enumerate((query, key, value, out)):
        block = jnp.concatenate([ref[...].astype(f32), jnp.zeros((2, WIDTH), f32)], axis=0)
        if i == 0:
            line = lax.broadcasted_iota(jnp.int32, (8, WIDTH), 0)
            block = jnp.where(line == 6, row[...].astype(f32), block)
        packed[:, i * WIDTH : (i + 1) * WIDTH] = block.astype(bf16)
    block = jnp.concatenate([inner[...].astype(f32), jnp.zeros((2, FF), f32)], axis=0)
    packed[:, 4 * WIDTH :] = block.astype(bf16)


def merge_rows(ids, own, r1, r2, r3, attn_out, inner_out):
    ordered = in_order([v[...].astype(f32) for v in (own, r1, r2, r3)], ids[12])
    width = 3 * WIDTH
    rows = jnp.concatenate([v[:6] for v in ordered], axis=0).astype(bf16)
    attn_out[:, :width] = rows[:, :width]
    inner_out[...] = rows[:, width:]
    row = jnp.concatenate([v[6:7, :128] for v in ordered], axis=1)
    first = lax.broadcasted_iota(jnp.int32, (24, 4 * 128), 0) == 0
    attn_out[:, width:] = jnp.where(first, jnp.broadcast_to(row, (24, 4 * 128)), 0.0).astype(bf16)


def stack_rows(ids, own, r1, r2, r3, out):
    for d, piece in enumerate((own, r1, r2, r3)):
        out[lax.rem(ids[11] + RING - d, RING)] = piece[...]


def ahead(ids, axis, step):
    return lax.rem(ids[axis] + step, RING)


def sum_of(refs):
    total = refs[0][...].astype(f32)
    for ref in refs[1:]:
        total += ref[...].astype(f32)
    return total


def sum_blocks(ids, *refs):
    *parts, o0, o1, o2, o3, scratch = refs
    start = 0
    for mine, core in zip(parts[::2], parts[1::2]):
        end = start + mine.shape[2]
        scratch[:, start:end] = mine[0].astype(f32) + core[0].astype(f32)
        start = end
    for d, out in enumerate((o0, o1, o2, o3)):
        first = pl.multiple_of(ahead(ids, 11, d) * 24, 8)
        out[0] = scratch[pl.ds(first, 24), :].astype(bf16)


def sum_attention(ids, outer, mine, core, o0, o1, o2, o3, scratch):
    scratch[...] = mine[0].astype(f32) + core[0].astype(f32)
    for d, out in enumerate((o0, o1, o2, o3)):
        z = ahead(ids, 11, d)
        first = pl.multiple_of(z * 24, 8)
        out[0, :, : scratch.shape[1]] = scratch[pl.ds(first, 24), :].astype(bf16)
        out[0, :, scratch.shape[1] :] = outer[0, z]


def sum_outer(ids, mine, core, out):
    total = mine[0].astype(f32) + core[0].astype(f32)
    for z in range(RING):
        for y in range(RING):
            first = 96 * z + 24 * y
            out[y, 0, z] = total[first : first + 24].astype(bf16)


def sum_first(ids, value, out):
    for z in range(RING):
        out[0, z] = sum_of([value.at[y, 0, z] for y in range(RING)]).astype(bf16)


def split_rows(ids, p0, p1, p2, p3, o0, o1, o2, o3, *refs):
    *rest, scratch = refs
    width = o0.shape[2]
    total = sum_of([p.at[0] for p in (p0, p1, p2, p3)])
    if rest:
        rest[0][0] = total[:, width + 128 :].astype(bf16)
    for y in range(RING):
        vectors = total[y : y + 1, width : width + 128]
        row = jnp.concatenate([vectors, jnp.zeros((1, width - 128), f32)], axis=1)
        rows = total[6 * y : 6 * y + 6, :width]
        scratch[y] = jnp.concatenate([rows, row, jnp.zeros((1, width), f32)], axis=0)
    for d, out in enumerate((o0, o1, o2, o3)):
        out[0] = scratch[ahead(ids, 12, d)].astype(bf16)


LAST = FF + WIDTH + 3 * WIDTH + 3 * WIDTH


def join_flows(ids, i0, i1, i2, i3, a0, a1, a2, a3, outer, o0, o1, o2, o3, scratch):
    scratch[:, :, : FF + WIDTH] = sum_of((i0, i1, i2, i3))
    scratch[:, :, FF + WIDTH : FF + 4 * WIDTH] = sum_of((a0, a1, a2, a3))
    for x in range(RING):
        total = outer[x].astype(f32)
        for k in range(3):
            start = FF + (4 + k) * WIDTH
            scratch[x, :, start : start + WIDTH] = total[8 * k : 8 * k + 8]
    for d, out in enumerate((o0, o1, o2, o3)):
        out[...] = scratch[ahead(ids, 8, d)].astype(bf16)


def split_ffn(ids, p0, p1, p2, p3, inner, outer):
    for d, piece in enumerate((p0, p1, p2, p3)):
        inner[d] = piece[:, :MIXED]
        halves = [piece[:, MIXED + i * WIDTH : MIXED + (i + 1) * WIDTH].astype(f32) for i in range(2)]
        outer[d] = jnp.concatenate(halves, axis=0).astype(bf16)


def write_grads(ids, p0, p1, p2, p3, query, key, value, out, inner, outer, vectors):
    total = sum_of((p0, p1, p2, p3))
    inner[...] = total[:6, :FF]
    out[...] = total[:6, FF : FF + WIDTH]
    start = FF + WIDTH
    query[...] = total[:6, start : start + WIDTH]
    key[...] = total[:6, start + WIDTH : start + 2 * WIDTH]
    value[...] = total[:6, start + 2 * WIDTH : start + 3 * WIDTH]
    vectors[...] = jnp.concatenate([total[6:7, :128], total[6:7, start : start + 128]], axis=0)
    start += 3 * WIDTH
    for k in range(3):
        outer[8 * k : 8 * k + 8] = total[:, start + k * WIDTH : start + (k + 1) * WIDTH]


def whole(shape):
    return pl.BlockSpec(shape, lambda s, ids: (0,) * len(shape), pipeline_mode=pl.Buffered(1))


def sequence(s):
    return jnp.minimum(s, SEQ_DEV - 1)


DEALT_SPEC = pl.BlockSpec((GROUP, 1, PIECE, WIDTH), lambda s, ids: (0, sequence(s), 0, 0))


def by_rows(width):
    return pl.BlockSpec((SLOT, width), lambda s, ids: (sequence(s), 0))


def rows_of(width, kind):
    return jax.ShapeDtypeStruct((ROWS, width), kind)


EXP_SPEC = pl.BlockSpec((1, HEADS, SLOT, SLOT), lambda s, ids: (sequence(s), 0, 0, 0))
NORM_SPEC = pl.BlockSpec((1, 16, SLOT), lambda s, ids: (sequence(s), 0, 0))
RETURN_SPEC = pl.BlockSpec((GROUP, 2, 1, PIECE, WIDTH), lambda s, ids: (0, 0, sequence(s), 0, 0))
RETURN_SHAPE = jax.ShapeDtypeStruct((GROUP, 2, SEQ_DEV, PIECE, WIDTH), bf16)


def by_columns(height):
    return pl.BlockSpec((height, SLOT), lambda s, ids: (0, sequence(s)))


def columns_of(height):
    return jax.ShapeDtypeStruct((height, ROWS), bf16)


def run(kernel, grid, ins, outs, operands, name, flops, moved, scratch=()):
    return pl.pallas_call(
        kernel,
        grid_spec=pltpu.PrefetchScalarGridSpec(
            num_scalar_prefetch=1,
            grid=grid,
            in_specs=ins,
            out_specs=[spec for spec, _ in outs],
            scratch_shapes=list(scratch),
        ),
        out_shape=[shape for _, shape in outs],
        compiler_params=pltpu.CompilerParams(
            vmem_limit_bytes=VMEM_LIMIT, dimension_semantics=("arbitrary",) * len(grid)
        ),
        cost_estimate=pl.CostEstimate(flops=flops, bytes_accessed=moved, transcendentals=0),
        name=name,
    )(*operands)


def out_rows(width, kind):
    return (by_rows(width), rows_of(width, kind))


def out_columns(height):
    return (by_columns(height), columns_of(height))


def out_whole(shape):
    return (whole(shape), jax.ShapeDtypeStruct(shape, f32))


ANYWHERE = pl.BlockSpec(memory_space=pl.ANY)
ATTENTION_SCRATCH = [pltpu.VMEM((RING, CORES, 96, PACKED), bf16)]


def call_forward(ids, dealt, weights, perm):
    return run(
        attention_forward,
        (SEQ_DEV,),
        [DEALT_SPEC] + [ANYWHERE] * 8 + [whole((32, 16))],
        [
            out_columns(WIDTH),
            out_rows(3 * WIDTH, bf16),
            (EXP_SPEC, jax.ShapeDtypeStruct((SEQ_DEV, HEADS, SLOT, SLOT), bf16)),
            (NORM_SPEC, jax.ShapeDtypeStruct((SEQ_DEV, 16, SLOT), f32)),
            out_columns(WIDTH),
            out_whole((8, WIDTH)),
            out_whole((1, FF)),
            out_whole((8, 128)),
        ],
        (ids, dealt, *weights, perm),
        "attention_forward",
        22 * 10**9,
        22 * 10**6,
        ATTENTION_SCRATCH + [pltpu.VMEM((32, PACKED - 3 * WIDTH), f32), pltpu.SemaphoreType.DMA((8,))],
    )


def halves(block, shape, where):
    return [(pl.BlockSpec(block, lambda s, ids: where(s)), jax.ShapeDtypeStruct(shape, bf16))] * 2


def call_ffn(ids, dealt, dealt_c, ctx_t, inner, outer, vec, bias_in):
    outer_rows = FF // GROUP
    inner_rows = WIDTH // GROUP
    first = SEQ_DEV
    second = first + RING
    return run(
        feed_forward,
        (second + FF_STEPS + 1,),
        [DEALT_SPEC] * 2
        + [whole((WIDTH, ROWS))]
        + [ANYWHERE] * 8
        + [whole((8, WIDTH)), whole((1, FF))],
        [out_rows(WIDTH, bf16), out_rows(WIDTH, f32), out_rows(WIDTH, bf16)]
        + halves(
            (1, outer_rows, WIDTH), (RING, outer_rows, WIDTH), lambda s: (jnp.clip(s - first, 0, RING - 1), 0, 0)
        )
        + halves(
            (RING, inner_rows, FF_STEP),
            (RING, inner_rows, FF),
            lambda s: (0, 0, jnp.clip(s - second, 0, FF_STEPS - 1)),
        )
        + halves((RING, inner_rows, WIDTH + 128), (RING, inner_rows, WIDTH + 128), lambda s: (0, 0, 0)),
        (ids, dealt, dealt_c, ctx_t, *inner, *outer, vec, bias_in),
        "feed_forward",
        50 * 10**9,
        40 * 10**6,
        [
            pltpu.VMEM((SLOT, FF), bf16),
            pltpu.VMEM((8, WIDTH), f32),
            pltpu.VMEM((1, FF), f32),
            pltpu.VMEM((RING, CORES, 2, 48, MIXED), bf16),
            pltpu.VMEM((RING, CORES, RING, 2, 48, WIDTH), bf16),
            pltpu.VMEM((SEQ_DEV, WIDTH, SLOT), bf16),
            pltpu.VMEM((SEQ_DEV, FF, SLOT), bf16),
            pltpu.VMEM((SEQ_DEV, SLOT, WIDTH), bf16),
            pltpu.VMEM((SEQ_DEV, FF_STEPS, SLOT, FF_STEP), bf16),
            pltpu.VMEM((SEQ_DEV, SLOT, WIDTH), bf16),
            pltpu.SemaphoreType.DMA((RING, RING)),
            pltpu.SemaphoreType.DMA((RING, RING, RING)),
        ],
    )


def call_backward(ids, dsum, dattn, qkv, expo, norm, ctx_t, x_t, dealt_c, layer, weights, inner):
    block = (RING, WIDTH // GROUP, 3 * WIDTH + 128)
    return run(
        attention_backward,
        (SEQ_DEV + 1,),
        [by_rows(WIDTH), by_rows(WIDTH), by_rows(3 * WIDTH), EXP_SPEC, NORM_SPEC, by_columns(WIDTH)]
        + [whole((WIDTH, ROWS)), DEALT_SPEC, by_rows(WIDTH)]
        + [ANYWHERE] * 12,
        [(RETURN_SPEC, RETURN_SHAPE)] + halves(block, block, lambda s: (0, 0, 0)),
        (ids, dsum, dattn, qkv, expo, norm, ctx_t, x_t, dealt_c, layer, *weights, *inner),
        "attention_backward",
        28 * 10**9,
        30 * 10**6,
        ATTENTION_SCRATCH
        + [
            pltpu.VMEM((RING, CORES, 2, 48, WIDTH), bf16),
            pltpu.VMEM((8, WIDTH), f32),
            pltpu.VMEM((SEQ_DEV, 3, SLOT, WIDTH), bf16),
            pltpu.SemaphoreType.DMA((8,)),
            pltpu.SemaphoreType.DMA((RING, RING)),
        ],
    )


def call_by_x(kernel, name, ids, pieces, at, out_shapes, out_at, scratch):
    count = len(out_shapes)

    def every_x(ids, *refs):
        ins, outs, rest = refs[: len(pieces)], refs[len(pieces) :][:count], refs[len(pieces) + count :]
        for x in range(RING):
            one = (pl.ds(x, 1),)
            kernel(
                ids,
                *[ref.at[(slice(None),) * at + one] for ref in ins],
                *[ref.at[(slice(None),) * out_at + one] for ref in outs],
                *rest,
            )

    return call_small(every_x, name, ids, pieces, *out_shapes, scratch=scratch)


def call_small(kernel, name, ids, pieces, *out_shapes, kind=bf16, scratch=()):
    def full(shape):
        return pl.BlockSpec(shape, lambda i, ids: (0,) * len(shape))

    return run(
        kernel,
        (1,),
        [full(piece.shape) for piece in pieces],
        [(full(shape), jax.ShapeDtypeStruct(shape, kind)) for shape in out_shapes],
        (ids, *pieces),
        name,
        10**6,
        6 * 10**6,
        [pltpu.VMEM(shape, f32) for shape in scratch],
    )


def shift(value, axis, step):
    size = CORES if axis == "core" else RING
    return lax.ppermute(value, axis, [(i, (i + step) % size) for i in range(size)])


def swap(value, axis):
    return lax.ppermute(value, axis, [(i, i ^ 1) for i in range(RING)])


def arrivals(value, axis):
    return [value] + [shift(value, axis, step) for step in (1, 2, 3)]


def both_cores(pieces):
    return [part for piece in pieces for part in (piece, shift(piece, "core", 1))]


def paired(value, axis):
    return in_half(value, swap(value, axis), axis)


def in_half(value, other, axis):
    even = lax.rem(lax.axis_index(axis), 2) == 0
    return jnp.where(even, value, other), jnp.where(even, other, value)


def hold(value, *others):
    return lax.optimization_barrier((value, *others))[0]


def send_ring(parts, axis):
    return [parts[0]] + [shift(parts[step], axis, step) for step in (1, 2, 3)]


def over(value, axis):
    return lax.all_to_all(value, axis, split_axis=0, concat_axis=0, tiled=True)


def body(
    tokens,
    cotangent,
    perm,
    lengths,
    drop,
    w_query,
    b_query,
    w_key,
    w_value,
    b_value,
    w_out,
    b_out,
    norm1_gain,
    norm1_bias,
    w_inner,
    b_inner,
    w_outer,
    b_outer,
    norm2_gain,
    norm2_bias,
):
    me_x = lax.axis_index("x")
    me_c = lax.axis_index("core")
    me_z = lax.axis_index("z")
    me_y = lax.axis_index("y")
    first = ((me_z * RING + me_y) * 8 + me_x * CORES + me_c) * SEQ_DEV
    places = jnp.stack([me_x, me_c, first, me_z, me_y]).astype(jnp.int32)
    places = jnp.pad(places, (8, 3))

    vectors = [b_query, b_value, b_out, norm1_gain, norm1_bias, b_outer, norm2_gain, norm2_bias, b_inner]
    vectors += [lengths.astype(bf16), drop.astype(bf16)]
    row = jnp.zeros((WIDTH,), bf16)
    start = 0
    for vector in vectors:
        end = start + vector.shape[0]
        row += jnp.pad(vector, (start, WIDTH - end))
        start = end
    (piece,) = call_small(
        pack_rows, "pack_rows", places, (w_query, w_key, w_value, w_out, w_inner, row[None]), (8, 4 * WIDTH + FF)
    )
    pieces_y = arrivals(piece, "y")
    dp = ("x", "core")
    dealt = (GROUP, SEQ_DEV, PIECE, WIDTH)
    dealt_x = over(tokens.reshape(dealt), dp)
    attn_y, inner_y = call_small(merge_rows, "merge_rows", places, pieces_y, (24, PACKED), (24, MIXED))
    (attn_zy,) = call_small(
        stack_rows, "stack_rows", places, arrivals(attn_y, "z"), (RING, 24, PACKED)
    )

    outer_pair = paired(w_outer, "y")
    ffn_x = arrivals(jnp.concatenate([hold(inner_y, dealt_x), *outer_pair], axis=1), "x")
    ffn_x[0] = hold(ffn_x[0], attn_zy)
    inner_x, outer_x = call_small(
        split_ffn, "split_ffn", places, ffn_x, (RING, 24, MIXED), (RING, 48, WIDTH)
    )
    attn_x = arrivals(hold(attn_zy, dealt_x).reshape(96, PACKED), "x")
    attn_pieces = both_cores(attn_x)
    inner_z = swap(inner_x, "z")
    outer_z = over(jnp.broadcast_to(outer_x[None], (RING, RING, 48, WIDTH)), "z")
    inner_z = jnp.concatenate(in_half(inner_x, hold(inner_z, attn_x[1]), "z"), axis=1)
    inner_far = shift(inner_z, "z", 2)
    outer_z = hold(outer_z, attn_x[1])
    outer_far = shift(outer_z, "y", 2)
    dealt_c = over(hold(cotangent, attn_x[1]).reshape(dealt), dp)

    x_t, qkv, expo, norm, ctx_t, vec, inner_bias, info = call_forward(
        places, dealt_x, attn_pieces, perm.reshape(32, 16)
    )
    ids = jnp.concatenate([info[:, 0].astype(jnp.int32), places[8:]])

    inner_pieces = both_cores([hold(inner_z, ctx_t, dealt_c), hold(inner_far, ctx_t)])
    outer_pieces = both_cores([hold(outer_z, ctx_t), hold(outer_far, ctx_t)])
    (
        layer, d_sum1, d_attn, outer_away, outer_mine, inner_away, inner_mine, out_away, out_mine
    ) = call_ffn(ids, dealt_x, dealt_c, ctx_t, inner_pieces, outer_pieces, vec, inner_bias)

    inner_core = shift(inner_away, "core", 1)
    out_core = shift(out_away, "core", 1)
    outer_core = shift(hold(outer_away, out_core), "core", 1)
    inner_width = FF + WIDTH + 128
    inner_parts = call_by_x(
        sum_blocks, "sum_blocks", places, (inner_mine, inner_core, out_mine, out_core), 0,
        [(RING, 24, inner_width)] * RING, 0, [(96, inner_width)],
    )
    (outer_sum,) = call_by_x(
        sum_outer, "sum_outer", hold(places, inner_parts[0]), (outer_mine, outer_core), 0,
        [(RING, RING, RING, 24, WIDTH)], 1, [],
    )
    inner_parts = send_ring(inner_parts, "z")
    outer_y = over(outer_sum, "y")

    d_sum1, d_attn = lax.optimization_barrier((d_sum1, d_attn, inner_parts[0], outer_sum))[:2]
    back, attn_away, attn_mine = call_backward(
        ids, d_sum1, d_attn, qkv, expo, norm, ctx_t, x_t, dealt_c, layer, attn_pieces, inner_pieces
    )

    attn_core = shift(hold(attn_away, outer_y, *inner_parts[1:]), "core", 1)
    (outer_z,) = call_by_x(
        sum_first, "sum_first", hold(places, attn_away), (hold(outer_y, attn_away),), 1,
        [(RING, RING, 24, WIDTH)], 0, [],
    )
    attn_width = 3 * WIDTH + 128
    attn_parts = call_by_x(
        sum_attention, "sum_attention", places, (outer_z, attn_mine, attn_core), 0,
        [(RING, 24, attn_width + WIDTH)] * RING, 0, [(96, attn_width)],
    )
    attn_first = attn_parts[0]
    attn_parts = send_ring(attn_parts, "z")
    back = over(hold(back, outer_z), dp)

    inner_parts = [hold(p, attn_first) for p in inner_parts]
    inner_parts = call_by_x(
        split_rows, "split_rows", places, inner_parts, 0,
        [(RING, 8, FF + WIDTH)] * RING, 0, [(RING, 8, FF + WIDTH)],
    )
    *attn_parts, outer_z = call_by_x(
        split_rows, "split_rows", hold(places, inner_parts[0]), attn_parts, 0,
        [(RING, 8, 3 * WIDTH)] * RING + [(RING, 24, WIDTH)], 0, [(RING, 8, 3 * WIDTH)],
    )
    inner_parts = send_ring(inner_parts, "y")
    attn_parts = send_ring(attn_parts, "y")
    last = call_small(
        join_flows, "join_flows", places, [*inner_parts, *attn_parts, outer_z], *[(8, LAST)] * 4,
        scratch=[(RING, 8, LAST)],
    )
    back = hold(back, last[0])
    layer_final = back[:, 0].reshape(GROUP * SEQ_DEV, PIECE, WIDTH)
    grad_final = back[:, 1].reshape(GROUP * SEQ_DEV, PIECE, WIDTH)
    square = (6, WIDTH)
    grad_query, grad_key, grad_value, grad_out, grad_inner, grad_outer, vectors = call_small(
        write_grads, "write_grads", hold(places, layer_final), send_ring(last, "x"),
        square, square, square, square, (6, FF), (24, WIDTH), (2, 128), kind=f32,
    )
    ffn_vectors = [vectors[0, 6 * i : 6 * i + 6] for i in range(6)]
    return (
        layer_final,
        grad_final,
        grad_query,
        vectors[1, :6],
        grad_key,
        grad_value,
        vectors[1, 6:12],
        grad_out,
        ffn_vectors[5],
        ffn_vectors[3],
        ffn_vectors[4],
        grad_inner,
        vectors[0, 36:60],
        grad_outer,
        ffn_vectors[0],
        ffn_vectors[1],
        ffn_vectors[2],
    )


def solution(mesh):
    chips = Mesh(mesh.devices.reshape(RING, CORES, RING, RING), ("x", "core", "z", "y"))
    dp = ("x", "core")
    fsdp = ("z", "y")
    every = P(dp + fsdp)
    rows = P(dp + fsdp, None)
    whole_rows = P(fsdp, dp, None)
    return jax.shard_map(
        body,
        mesh=chips,
        in_specs=(
            whole_rows, whole_rows, P(), every, every,
            rows, every, rows, rows, every, rows, every, every, every,
            rows, every, rows, every, every, every,
        ),
        out_specs=(
            whole_rows, whole_rows,
            rows, every, rows, rows, every, rows, every, every, every,
            rows, every, rows, every, every, every,
        ),
        check_vma=False,
    )
```

profile of v0, /device:TPU:0, one launch (start us, length us, event | category | flops | bytes accessed | tf_op | source)
XLA Modules:
  0.0 340.5 jit_solution(9976944922401178292)
XLA Ops:
  0.8 4.5 %all-to-all-start = ((bf16[8,4,32,768]{3,2,1,0:T(8,128)(2,1)}), bf16[8,4,32,768]{3,2,1,0:T(8,128)(2,1)S(1)}, u32[]{:S(2)}, u32[]{:S(2)}) async-start(bf16[8,4,32,768]{3,2,1,0:T(8,128)(2,1)} %bitcast.28), calls=%async_computation | async-start | bytes 3145728 | tf_op jit(solution)/shard_map/all_to_all | solution.py:747
  24.4 4.0 %collective-permute-start.5 = (bf16[24,2816]{1,0:T(8,128)(2,1)}, bf16[24,2816]{1,0:T(8,128)(2,1)S(1)}, u32[]{:S(2)}, u32[]{:S(2)}) collective-permute-start(bf16[24,2816]{1,0:T(8,128)(2,1)} %get-tuple-element.94.own), channel_id=1, source_target_pairs={{0,12},{4,0},{8,4},{12,8},{1,13},{5,1},{9,5},{13,9},{2,14},{6,2},{... | collective-permute-start | bytes 405512 | tf_op jit(solution)/shard_map/ppermute | solution.py:714
  35.6 5.8 %collective-permute-done.4.r2 = bf16[24,2816]{1,0:T(8,128)(2,1)S(1)} collective-permute-done((bf16[24,2816]{1,0:T(8,128)(2,1)}, bf16[24,2816]{1,0:T(8,128)(2,1)S(1)}, u32[]{:S(2)}, u32[]{:S(2)}) %collective-permute-start.4) | collective-permute-done | bytes 135200 | tf_op jit(solution)/shard_map/ppermute | solution.py:714
  58.2 3.5 %all-to-all-start.2 = ((bf16[4,4,48,768]{3,2,1,0:T(8,128)(2,1)}), bf16[4,4,48,768]{3,2,1,0:T(8,128)(2,1)S(1)}, u32[]{:S(2)}, u32[]{:S(2)}) async-start(bf16[4,4,48,768]{3,2,1,0:T(8,128)(2,1)} %broadcast_in_dim.10), calls=%async_computation.2 | async-start | bytes 2359296 | tf_op jit(solution)/shard_map/all_to_all | solution.py:747
  61.8 15.9 %collective-permute-done.7.p2 = bf16[96,2816]{1,0:T(8,128)(2,1)} collective-permute-done((bf16[96,2816]{1,0:T(8,128)(2,1)}, bf16[96,2816]{1,0:T(8,128)(2,1)}, u32[]{:S(2)}, u32[]{:S(2)}) %collective-permute-start.7) | collective-permute-done | bytes 540704 | tf_op jit(solution)/shard_map/ppermute | solution.py:714
  83.3 4.0 %all-to-all-start.1 = ((bf16[8,4,32,768]{3,2,1,0:T(8,128)(2,1)}), bf16[8,4,32,768]{3,2,1,0:T(8,128)(2,1)S(1)}, u32[]{:S(2)}, u32[]{:S(2)}) async-start(bf16[8,4,32,768]{3,2,1,0:T(8,128)(2,1)} %bitcast.7), calls=%async_computation.1 | async-start | bytes 3145728 | tf_op jit(solution)/shard_map/all_to_all | solution.py:747
  87.2 3.5 %collective-permute-start.22 = (bf16[4,4,48,768]{3,2,1,0:T(8,128)(2,1)}, bf16[4,4,48,768]{3,2,1,0:T(8,128)(2,1)}, u32[]{:S(2)}, u32[]{:S(2)}) collective-permute-start(bf16[4,4,48,768]{3,2,1,0:T(8,128)(2,1)} %copy-done.7), channel_id=1, source_target_pairs={{0,2},{1,3},{2,0},{3,1},{4,6},{5,7},{6,4},{7,5},{8,10},{9,11},{10,... | collective-permute-start | bytes 3538952 | tf_op jit(solution)/shard_map/ppermute | solution.py:714
  90.7 23.7 %attention_forward.1 = (bf16[768,1024]{1,0:T(8,128)(2,1)}, bf16[1024,2304]{1,0:T(8,128)(2,1)}, bf16[4,12,256,256]{3,2,1,0:T(8,128)(2,1)}, f32[4,16,256]{2,1,0:T(...) custom-call(s32[16]{0:T(128)} %pad.48.ids, ...), custom_call_target="tpu_custom_call" | custom-call | flops 22000001024 | bytes 22000000 | tf_op jit(solution)/shard_map/attention_forward/pallas_call | solution.py:550
  123.7 65.8 %feed_forward.1 = (bf16[1024,768]{1,0:T(8,128)(2,1)}, f32[1024,768]{1,0:T(8,128)}, bf16[1024,768]{1,0:T(8,128)(2,1)}, bf16[4,384,768]{2,1,0:T(8,128)(2,1)}, bf16...) custom-call(s32[16]{0:T(128)} %pad_add_fusion.1.ids, ...), custom_call_target="tpu_custom_call" | custom-call | flops 49999998976 | bytes 40000000 | tf_op jit(solution)/shard_map/feed_forward/pallas_call | solution.py:550
  192.1 3.2 collective-permute-done.24.refs_1_
  196.8 6.4 %sum_blocks.1 = (bf16[4,24,3968]{2,1,0:T(8,128)(2,1)}, bf16[4,24,3968]{2,1,0:T(8,128)(2,1)}, bf16[4,24,3968]{2,1,0:T(8,128)(2,1)}, bf16[4,24,3968]{2,1,0:T(8,128)(2,1)}) custom-call(s32[16]{0:T(128)} %pad.48.ids, bf16[4,96,3072]{2,1,0:T(8,128)(2,1)} %get-tuple-element.114.refs_0_, bf16[4,96,3072]{2,1,0:T(8,128)(2,1)} %copy-done.2, ...), custom_call_target="tpu_custom_call" | custom-call | flops 1000000 | bytes 6000000 | tf_op jit(solution)/shard_map/sum_blocks/pallas_call | solution.py:550
  209.8 5.0 %sum_outer.1 = bf16[4,4,4,24,768]{4,3,2,1,0:T(8,128)(2,1)} custom-call(s32[16]{0:T(128)} %pad.48.ids, bf16[4,384,768]{2,1,0:T(8,128)(2,1)} %get-tuple-element.120.refs_0_, bf16[4,384,768]{2,1,0:T(8,128)(2,1)} %copy-done.1), custom_call_target="tpu_custom_call" | custom-call | flops 1000000 | bytes 6000000 | tf_op jit(solution)/shard_map/sum_outer/pallas_call | solution.py:550
  214.8 4.4 %all-to-all-start.3 = ((bf16[4,4,4,24,768]{4,3,2,1,0:T(8,128)(2,1)}), bf16[4,4,4,24,768]{4,3,2,1,0:T(8,128)(2,1)S(1)}, u32[]{:S(2)}, u32[]{:S(2)}) async-start(bf16[4,4,4,24,768]{4,3,2,1,0:T(8,128)(2,1)} %sum_outer.1), calls=%async_computation.3 | async-start | bytes 4718592 | tf_op jit(solution)/shard_map/all_to_all | solution.py:747
  219.3 32.1 %attention_backward.1 = (bf16[8,2,4,32,768]{4,3,2,1,0:T(8,128)(2,1)}, bf16[4,96,2432]{2,1,0:T(8,128)(2,1)}, bf16[4,96,2432]{2,1,0:T(8,128)(2,1)}) custom-call(s32[16]{0:T(128)} %pad_add_fusion.1.ids, f32[1024,768]{1,0:T(8,128)} %get-tuple-element.123.dsum, bf16[1024,768]{1,0:T(8,128)(2,1)} %get-tuple-element.124.dattn, ...), custom_call_target="tpu_custom_call" | custom-call | flops 28000000000 | bytes 30000000 | tf_op jit(solution)/shard_map/attention_backward/pallas_call | solution.py:550
  252.8 3.4 %sum_first.1.refs_0_ = bf16[4,4,24,768]{3,2,1,0:T(8,128)(2,1)} custom-call(s32[16]{0:T(128)} %pad.48.ids, bf16[4,4,4,24,768]{4,3,2,1,0:T(8,128)(2,1)} %copy-done), custom_call_target="tpu_custom_call" | custom-call | flops 1000000 | bytes 6000000 | tf_op jit(solution)/shard_map/sum_first/pallas_call | solution.py:550
  256.2 3.7 %all-to-all-start.4 = ((bf16[8,2,4,32,768]{4,3,2,1,0:T(8,128)(2,1)}), bf16[8,2,4,32,768]{4,3,2,1,0:T(8,128)(2,1)S(1)}, u32[]{:S(2)}, u32[]{:S(2)}) async-start(bf16[8,2,4,32,768]{4,3,2,1,0:T(8,128)(2,1)} %get-tuple-element.134), calls=%async_computation.4 | async-start | bytes 6291456 | tf_op jit(solution)/shard_map/all_to_all | solution.py:747
  260.6 4.0 %collective-permute-done.30.refs_2_ = bf16[4,96,2432]{2,1,0:T(8,128)(2,1)S(1)} collective-permute-done((bf16[4,96,2432]{2,1,0:T(8,128)(2,1)}, bf16[4,96,2432]{2,1,0:T(8,128)(2,1)S(1)}, u32[]{:S(2)}, u32[]{:S(2)}) %collective-permute-start.30) | collective-permute-done | bytes 1867808 | tf_op jit(solution)/shard_map/ppermute | solution.py:714
  265.8 5.2 %sum_attention.1 = (bf16[4,24,3200]{2,1,0:T(8,128)(2,1)}, bf16[4,24,3200]{2,1,0:T(8,128)(2,1)}, bf16[4,24,3200]{2,1,0:T(8,128)(2,1)}, bf16[4,24,3200]{2,1,0:T(8,128)(2,1)}) custom-call(s32[16]{0:T(128)} %pad.48.ids, bf16[4,4,24,768]{3,2,1,0:T(8,128)(2,1)} %sum_first.1.refs_0_, bf16[4,96,2432]{2,1,0:T(8,128)(2,1)} %get-tuple-element.135.refs_1_, ...), custom_call_target="tpu_custom_call" | custom-call | flops 1000000 | bytes 6000000 | tf_op jit(solution)/shard_map/sum_attention/pallas_call | solution.py:550
  275.0 4.3 %split_rows.2 = (bf16[4,8,3840]{2,1,0:T(8,128)(2,1)}, bf16[4,8,3840]{2,1,0:T(8,128)(2,1)}, bf16[4,8,3840]{2,1,0:T(8,128)(2,1)}, bf16[4,8,3840]{2,1,0:T(8,128)(2,1)}) custom-call(s32[16]{0:T(128)} %pad.48.ids, bf16[4,24,3968]{2,1,0:T(8,128)(2,1)} %get-tuple-element.141.refs_0_, bf16[4,24,3968]{2,1,0:T(8,128)(2,1)} %collective-permute-done.27.refs_1_, ...), custom_call_target="tpu_custom_call" | custom-call | flops 1000000 | bytes 6000000 | tf_op jit(solution)/shard_map/split_rows/pallas_call | solution.py:550
  284.1 17.4 %collective-permute-done.34.refs_1_ = bf16[4,24,3200]{2,1,0:T(8,128)(2,1)S(1)} collective-permute-done((bf16[4,24,3200]{2,1,0:T(8,128)(2,1)}, bf16[4,24,3200]{2,1,0:T(8,128)(2,1)S(1)}, u32[]{:S(2)}, u32[]{:S(2)}) %collective-permute-start.34) | collective-permute-done | bytes 614432 | tf_op jit(solution)/shard_map/ppermute | solution.py:714
  301.5 3.2 collective-permute-start.33
  306.4 3.7 %split_rows.3 = (bf16[4,8,2304]{2,1,0:T(8,128)(2,1)}, bf16[4,8,2304]{2,1,0:T(8,128)(2,1)}, bf16[4,8,2304]{2,1,0:T(8,128)(2,1)}, bf16[4,8,2304]{2,1,0:T(8,128)(2,1)}, bf16[4,24,768]{2,1,0:T(8,128)(2,1)}) custom-call(s32[16]{0:T(128)} %pad.48.ids, bf16[4,24,3200]{2,1,0:T(8,128)(2,1)} %get-tuple-element.140.refs_0_, bf16[4,24,3200]{2,1,0:T(8,128)(2,1)} %copy-done.11, ...), custom_call_target="tpu_custom_call" | custom-call | flops 1000000 | bytes 6000000 | tf_op jit(solution)/shard_map/split_rows/pallas_call | solution.py:550
  313.6 5.8 %collective-permute-done.37.a1 = bf16[4,8,2304]{2,1,0:T(8,128)(2,1)S(1)} collective-permute-done((bf16[4,8,2304]{2,1,0:T(8,128)(2,1)}, bf16[4,8,2304]{2,1,0:T(8,128)(2,1)S(1)}, u32[]{:S(2)}, u32[]{:S(2)}) %collective-permute-start.37) | collective-permute-done | bytes 147488 | tf_op jit(solution)/shard_map/ppermute | solution.py:714
  320.7 3.3 join_flows.1
  (199 shorter events, 103.1 us)
Async XLA Ops:
  0.8 27.7 %all-to-all-start = ((bf16[8,4,32,768]{3,2,1,0:T(8,128)(2,1)}), bf16[8,4,32,768]{3,2,1,0:T(8,128)(2,1)S(1)}, u32[]{:S(2)}, u32[]{:S(2)}) async-start(bf16[8,4,32,768]{3,2,1,0:T(8,128)(2,1)} %bitcast.28), calls=%async_computation | async-start | bytes 3145728 | tf_op jit(solution)/shard_map/all_to_all | solution.py:747
  29.6 16.4 %collective-permute-start.16 = (bf16[24,5376]{1,0:T(8,128)(2,1)S(1)}, bf16[24,5376]{1,0:T(8,128)(2,1)S(1)}, u32[]{:S(2)}, u32[]{:S(2)}) collective-permute-start(bf16[24,5376]{1,0:T(8,128)(2,1)S(1)} %pad_maximum_fusion.1.p0), channel_id=1, source_target_pairs={{0,96},{32,0},{64,32},{96,64},{1,97},{33,1},{65,33},{97,65},{2,98}... | collective-permute-start | bytes 774152 | tf_op jit(solution)/shard_map/ppermute | solution.py:714
  32.5 13.5 %collective-permute-start.15 = (bf16[24,5376]{1,0:T(8,128)(2,1)S(1)}, bf16[24,5376]{1,0:T(8,128)(2,1)S(1)}, u32[]{:S(2)}, u32[]{:S(2)}) collective-permute-start(bf16[24,5376]{1,0:T(8,128)(2,1)S(1)} %pad_maximum_fusion.1.p0), channel_id=1, source_target_pairs={{0,64},{32,96},{64,0},{96,32},{1,65},{33,97},{65,1},{97,33},{2,66}... | collective-permute-start | bytes 774152 | tf_op jit(solution)/shard_map/ppermute | solution.py:714
  33.4 13.2 %collective-permute-start.14 = (bf16[24,5376]{1,0:T(8,128)(2,1)S(1)}, bf16[24,5376]{1,0:T(8,128)(2,1)S(1)}, u32[]{:S(2)}, u32[]{:S(2)}) collective-permute-start(bf16[24,5376]{1,0:T(8,128)(2,1)S(1)} %pad_maximum_fusion.1.p0), channel_id=1, source_target_pairs={{0,32},{32,64},{64,96},{96,0},{1,33},{33,65},{65,97},{97,1},{2,34}... | collective-permute-start | bytes 774152 | tf_op jit(solution)/shard_map/ppermute | solution.py:714
  50.5 27.8 %collective-permute-start.17 = (bf16[4,24,3840]{2,1,0:T(8,128)(2,1)}, bf16[4,24,3840]{2,1,0:T(8,128)(2,1)}, u32[]{:S(2)}, u32[]{:S(2)}) collective-permute-start(bf16[4,24,3840]{2,1,0:T(8,128)(2,1)} %get-tuple-element.102), channel_id=1, source_target_pairs={{0,4},{4,0},{8,12},{12,8},{1,5},{5,1},{9,13},{13,9},{2,6},{6,2},{1... | collective-permute-start | bytes 2211848 | tf_op jit(solution)/shard_map/ppermute | solution.py:718
  50.5 27.1 %collective-permute-start.7 = (bf16[96,2816]{1,0:T(8,128)(2,1)}, bf16[96,2816]{1,0:T(8,128)(2,1)}, u32[]{:S(2)}, u32[]{:S(2)}) collective-permute-start(bf16[96,2816]{1,0:T(8,128)(2,1)} %bitcast.31), channel_id=1, source_target_pairs={{0,32},{32,64},{64,96},{96,0},{1,33},{33,65},{65,97},{97,1},{2,34}... | collective-permute-start | bytes 1622024 | tf_op jit(solution)/shard_map/ppermute | solution.py:714
  52.3 25.4 %collective-permute-start.11 = (bf16[96,2816]{1,0:T(8,128)(2,1)}, bf16[96,2816]{1,0:T(8,128)(2,1)}, u32[]{:S(2)}, u32[]{:S(2)}) collective-permute-start(bf16[96,2816]{1,0:T(8,128)(2,1)} %bitcast.32), channel_id=1, source_target_pairs={{0,96},{32,0},{64,32},{96,64},{1,97},{33,1},{65,33},{97,65},{2,98}... | collective-permute-start | bytes 1622024 | tf_op jit(solution)/shard_map/ppermute | solution.py:714
  53.8 24.4 %collective-permute-start.9 = (bf16[96,2816]{1,0:T(8,128)(2,1)}, bf16[96,2816]{1,0:T(8,128)(2,1)}, u32[]{:S(2)}, u32[]{:S(2)}) collective-permute-start(bf16[96,2816]{1,0:T(8,128)(2,1)} %bitcast.33), channel_id=1, source_target_pairs={{0,64},{32,96},{64,0},{96,32},{1,65},{33,97},{65,1},{97,33},{2,66}... | collective-permute-start | bytes 1622024 | tf_op jit(solution)/shard_map/ppermute | solution.py:714
  56.1 31.1 %collective-permute-start.6 = (bf16[96,2816]{1,0:T(8,128)(2,1)}, bf16[96,2816]{1,0:T(8,128)(2,1)}, u32[]{:S(2)}, u32[]{:S(2)}) collective-permute-start(bf16[96,2816]{1,0:T(8,128)(2,1)} %bitcast.34), channel_id=1, source_target_pairs={{0,16},{16,0},{1,17},{17,1},{2,18},{18,2},{3,19},{19,3},{4,20},{20... | collective-permute-start | bytes 1622024 | tf_op jit(solution)/shard_map/ppermute | solution.py:714
  58.2 24.0 %all-to-all-start.2 = ((bf16[4,4,48,768]{3,2,1,0:T(8,128)(2,1)}), bf16[4,4,48,768]{3,2,1,0:T(8,128)(2,1)S(1)}, u32[]{:S(2)}, u32[]{:S(2)}) async-start(bf16[4,4,48,768]{3,2,1,0:T(8,128)(2,1)} %broadcast_in_dim.10), calls=%async_computation.2 | async-start | bytes 2359296 | tf_op jit(solution)/shard_map/all_to_all | solution.py:747
  79.6 36.3 %collective-permute-start.19 = (bf16[4,48,3840]{2,1,0:T(8,128)(2,1)S(1)}, bf16[4,48,3840]{2,1,0:T(8,128)(2,1)}, u32[]{:S(2)}, u32[]{:S(2)}) collective-permute-start(bf16[4,48,3840]{2,1,0:T(8,128)(2,1)S(1)} %pad_maximum_fusion.i0), channel_id=1, source_target_pairs={{0,8},{4,12},{8,0},{12,4},{1,9},{5,13},{9,1},{13,5},{2,10},{6,14},... | collective-permute-start | bytes 4423688 | tf_op jit(solution)/shard_map/ppermute | solution.py:714
  83.3 31.2 %all-to-all-start.1 = ((bf16[8,4,32,768]{3,2,1,0:T(8,128)(2,1)}), bf16[8,4,32,768]{3,2,1,0:T(8,128)(2,1)S(1)}, u32[]{:S(2)}, u32[]{:S(2)}) async-start(bf16[8,4,32,768]{3,2,1,0:T(8,128)(2,1)} %bitcast.7), calls=%async_computation.1 | async-start | bytes 3145728 | tf_op jit(solution)/shard_map/all_to_all | solution.py:747
  87.2 30.4 %collective-permute-start.22 = (bf16[4,4,48,768]{3,2,1,0:T(8,128)(2,1)}, bf16[4,4,48,768]{3,2,1,0:T(8,128)(2,1)}, u32[]{:S(2)}, u32[]{:S(2)}) collective-permute-start(bf16[4,4,48,768]{3,2,1,0:T(8,128)(2,1)} %copy-done.7), channel_id=1, source_target_pairs={{0,2},{1,3},{2,0},{3,1},{4,6},{5,7},{6,4},{7,5},{8,10},{9,11},{10,... | collective-permute-start | bytes 3538952 | tf_op jit(solution)/shard_map/ppermute | solution.py:714
  191.9 16.5 %collective-permute-start.26 = (bf16[4,384,768]{2,1,0:T(8,128)(2,1)}, bf16[4,384,768]{2,1,0:T(8,128)(2,1)S(1)}, u32[]{:S(2)}, u32[]{:S(2)}) collective-permute-start(bf16[4,384,768]{2,1,0:T(8,128)(2,1)} %get-tuple-element.122), channel_id=1, source_target_pairs={{0,16},{16,0},{1,17},{17,1},{2,18},{18,2},{3,19},{19,3},{4,20},{20... | collective-permute-start | bytes 7077896 | tf_op jit(solution)/shard_map/ppermute | solution.py:714
  203.1 56.8 %collective-permute-start.27 = (bf16[4,24,3968]{2,1,0:T(8,128)(2,1)}, bf16[4,24,3968]{2,1,0:T(8,128)(2,1)}, u32[]{:S(2)}, u32[]{:S(2)}) collective-permute-start(bf16[4,24,3968]{2,1,0:T(8,128)(2,1)} %get-tuple-element.136), channel_id=1, source_target_pairs={{0,4},{4,8},{8,12},{12,0},{1,5},{5,9},{9,13},{13,1},{2,6},{6,10},{... | collective-permute-start | bytes 2285576 | tf_op jit(solution)/shard_map/ppermute | solution.py:714
  205.1 54.9 %collective-permute-start.28 = (bf16[4,24,3968]{2,1,0:T(8,128)(2,1)}, bf16[4,24,3968]{2,1,0:T(8,128)(2,1)}, u32[]{:S(2)}, u32[]{:S(2)}) collective-permute-start(bf16[4,24,3968]{2,1,0:T(8,128)(2,1)} %get-tuple-element.137), channel_id=1, source_target_pairs={{0,8},{4,12},{8,0},{12,4},{1,9},{5,13},{9,1},{13,5},{2,10},{6,14},... | collective-permute-start | bytes 2285576 | tf_op jit(solution)/shard_map/ppermute | solution.py:714
  205.8 54.2 %collective-permute-start.29 = (bf16[4,24,3968]{2,1,0:T(8,128)(2,1)}, bf16[4,24,3968]{2,1,0:T(8,128)(2,1)}, u32[]{:S(2)}, u32[]{:S(2)}) collective-permute-start(bf16[4,24,3968]{2,1,0:T(8,128)(2,1)} %get-tuple-element.138), channel_id=1, source_target_pairs={{0,12},{4,0},{8,4},{12,8},{1,13},{5,1},{9,5},{13,9},{2,14},{6,2},{... | collective-permute-start | bytes 2285576 | tf_op jit(solution)/shard_map/ppermute | solution.py:714
  214.8 36.6 %all-to-all-start.3 = ((bf16[4,4,4,24,768]{4,3,2,1,0:T(8,128)(2,1)}), bf16[4,4,4,24,768]{4,3,2,1,0:T(8,128)(2,1)S(1)}, u32[]{:S(2)}, u32[]{:S(2)}) async-start(bf16[4,4,4,24,768]{4,3,2,1,0:T(8,128)(2,1)} %sum_outer.1), calls=%async_computation.3 | async-start | bytes 4718592 | tf_op jit(solution)/shard_map/all_to_all | solution.py:747
  256.2 74.1 %all-to-all-start.4 = ((bf16[8,2,4,32,768]{4,3,2,1,0:T(8,128)(2,1)}), bf16[8,2,4,32,768]{4,3,2,1,0:T(8,128)(2,1)S(1)}, u32[]{:S(2)}, u32[]{:S(2)}) async-start(bf16[8,2,4,32,768]{4,3,2,1,0:T(8,128)(2,1)} %get-tuple-element.134), calls=%async_computation.4 | async-start | bytes 6291456 | tf_op jit(solution)/shard_map/all_to_all | solution.py:747
  271.0 30.5 %collective-permute-start.34 = (bf16[4,24,3200]{2,1,0:T(8,128)(2,1)}, bf16[4,24,3200]{2,1,0:T(8,128)(2,1)S(1)}, u32[]{:S(2)}, u32[]{:S(2)}) collective-permute-start(bf16[4,24,3200]{2,1,0:T(8,128)(2,1)} %get-tuple-element.150), channel_id=1, source_target_pairs={{0,4},{4,8},{8,12},{12,0},{1,5},{5,9},{9,13},{13,1},{2,6},{6,10},{... | collective-permute-start | bytes 1843208 | tf_op jit(solution)/shard_map/ppermute | solution.py:714
  271.0 33.7 %collective-permute-start.35 = (bf16[4,24,3200]{2,1,0:T(8,128)(2,1)}, bf16[4,24,3200]{2,1,0:T(8,128)(2,1)S(1)}, u32[]{:S(2)}, u32[]{:S(2)}) collective-permute-start(bf16[4,24,3200]{2,1,0:T(8,128)(2,1)} %get-tuple-element.151), channel_id=1, source_target_pairs={{0,8},{4,12},{8,0},{12,4},{1,9},{5,13},{9,1},{13,5},{2,10},{6,14},... | collective-permute-start | bytes 1843208 | tf_op jit(solution)/shard_map/ppermute | solution.py:714
  272.5 32.2 %collective-permute-start.36 = (bf16[4,24,3200]{2,1,0:T(8,128)(2,1)}, bf16[4,24,3200]{2,1,0:T(8,128)(2,1)S(1)}, u32[]{:S(2)}, u32[]{:S(2)}) collective-permute-start(bf16[4,24,3200]{2,1,0:T(8,128)(2,1)} %get-tuple-element.152), channel_id=1, source_target_pairs={{0,12},{4,0},{8,4},{12,8},{1,13},{5,1},{9,5},{13,9},{2,14},{6,2},{... | collective-permute-start | bytes 1843208 | tf_op jit(solution)/shard_map/ppermute | solution.py:714
  279.3 33.1 %collective-permute-start.31 = (bf16[4,8,3840]{2,1,0:T(8,128)(2,1)}, bf16[4,8,3840]{2,1,0:T(8,128)(2,1)S(1)}, u32[]{:S(2)}, u32[]{:S(2)}) collective-permute-start(bf16[4,8,3840]{2,1,0:T(8,128)(2,1)} %get-tuple-element.146), channel_id=1, source_target_pairs={{0,1},{1,2},{2,3},{3,0},{4,5},{5,6},{6,7},{7,4},{8,9},{9,10},{10,1... | collective-permute-start | bytes 737288 | tf_op jit(solution)/shard_map/ppermute | solution.py:714
  281.4 32.1 %collective-permute-start.32 = (bf16[4,8,3840]{2,1,0:T(8,128)(2,1)}, bf16[4,8,3840]{2,1,0:T(8,128)(2,1)S(1)}, u32[]{:S(2)}, u32[]{:S(2)}) collective-permute-start(bf16[4,8,3840]{2,1,0:T(8,128)(2,1)} %get-tuple-element.147), channel_id=1, source_target_pairs={{0,2},{1,3},{2,0},{3,1},{4,6},{5,7},{6,4},{7,5},{8,10},{9,11},{10,... | collective-permute-start | bytes 737288 | tf_op jit(solution)/shard_map/ppermute | solution.py:714
  (71 other events, 484.0 us)
where the time goes:
time: 343 us; the launch traced here: 340 us
  Pallas kernels  166 us (48%)
  starting transfers between devices  76.8 us (22%)
  waiting for transfers between devices  71.8 us (21%)
  local copies, waits for them, and re-layouts  20.8 us (6%)
  other arithmetic  3.94 us (1%)
    pallas_call x15, Pallas kernels, run(): pl.pallas_call(kernel, grid_spec=pltpu.PrefetchScalarGridSpec(num_scalar_...  166 us
    ppermute x41, waiting for transfers between devices, shift(): lax.ppermute(value, axis, [(i, (i + step) % size) for i in range(size)])  71.6 us
    ppermute x41, starting transfers between devices, shift(): lax.ppermute(value, axis, [(i, (i + step) % size) for i in range(size)])  54.9 us
    all_to_all x5, starting transfers between devices, over(): return lax.all_to_all(value, axis, split_axis=0, concat_axis=0, tiled=True)  20.2 us
    unnamed x94, local copies, waits for them, and re-layouts  12 us
  transfers between devices with their start and end apart: 48, of which 20 were waited for; matrix products, arithmetic and copies ran while one was open for 3% of the time, Pallas kernels for 28%

commit v1 on v0

--- a/solution.py
+++ b/solution.py
@@ -25,7 +25,7 @@
 epsilon = 1e-05
 bf16 = jnp.bfloat16
 f32 = jnp.float32
-VMEM_LIMIT = 58 * 1024 * 1024
+MIB = 1024 * 1024
 
 TN = (((0,), (0,)), ((), ()))
 NT = (((1,), (1,)), ((), ()))
@@ -546,7 +546,7 @@
     return jax.ShapeDtypeStruct((height, ROWS), bf16)
 
 
-def run(kernel, grid, ins, outs, operands, name, flops, moved, scratch=()):
+def run(kernel, grid, ins, outs, operands, name, flops, moved, scratch, limit):
     return pl.pallas_call(
         kernel,
         grid_spec=pltpu.PrefetchScalarGridSpec(
@@ -558,7 +558,7 @@
         ),
         out_shape=[shape for _, shape in outs],
         compiler_params=pltpu.CompilerParams(
-            vmem_limit_bytes=VMEM_LIMIT, dimension_semantics=("arbitrary",) * len(grid)
+            vmem_limit_bytes=limit * MIB, dimension_semantics=("arbitrary",) * len(grid)
         ),
         cost_estimate=pl.CostEstimate(flops=flops, bytes_accessed=moved, transcendentals=0),
         name=name,
@@ -601,6 +601,7 @@
         22 * 10**9,
         22 * 10**6,
         ATTENTION_SCRATCH + [pltpu.VMEM((32, PACKED - 3 * WIDTH), f32), pltpu.SemaphoreType.DMA((8,))],
+        28,
     )
 
 
@@ -648,6 +649,7 @@
             pltpu.SemaphoreType.DMA((RING, RING)),
             pltpu.SemaphoreType.DMA((RING, RING, RING)),
         ],
+        54,
     )
 
 
@@ -672,6 +674,7 @@
             pltpu.SemaphoreType.DMA((8,)),
             pltpu.SemaphoreType.DMA((RING, RING)),
         ],
+        36,
     )
 
 
@@ -706,6 +709,7 @@
         10**6,
         6 * 10**6,
         [pltpu.VMEM(shape, f32) for shape in scratch],
+        30,
     )
 
 

time: 343 us -> 325 us (0.948)
  Pallas kernels: 166 us -> 135 us
  local copies, waits for them, and re-layouts: 20.8 us -> 29.6 us
  starting transfers between devices: 76.8 us -> 84.8 us
    pallas_call x15, Pallas kernels: 166 us -> 135 us  [run(): pl.pallas_call(kernel, grid_spec=pltpu.PrefetchScalarGridSpec(num_scalar_...]
    unnamed x94 -> x88, local copies, waits for them, and re-layouts: 12 us -> 23.3 us
    ppermute x41, waiting for transfers between devices: 71.6 us -> 65.3 us  [shift(): lax.ppermute(value, axis, [(i, (i + step) % size) for i in range(size)])]
    ppermute x41, starting transfers between devices: 54.9 us -> 59 us  [shift(): lax.ppermute(value, axis, [(i, (i + step) % size) for i in range(size)])]
    all_to_all x5, waiting for transfers between devices: 0.19 us -> 3.7 us  [over(): return lax.all_to_all(value, axis, split_axis=0, concat_axis=0, tiled=True)]
  transfers between devices with their start and end apart: 48 -> 48, of which waited for: 20 -> 18; matrix products, arithmetic and copies ran while one was open for 3% -> 3% of each run, Pallas kernels for 28% -> 21%
where the time goes in v1:
time: 325 us; the launch traced here: 323 us
  Pallas kernels  135 us (42%)
  starting transfers between devices  84.8 us (26%)
  waiting for transfers between devices  69 us (21%)
  local copies, waits for them, and re-layouts  29.6 us (9%)
  other arithmetic  3.27 us (1%)
    pallas_call x15, Pallas kernels, run(): pl.pallas_call(kernel, grid_spec=pltpu.PrefetchScalarGridSpec(num_scalar_...  135 us
    ppermute x41, waiting for transfers between devices, shift(): lax.ppermute(value, axis, [(i, (i + step) % size) for i in range(size)])  65.3 us
    ppermute x41, starting transfers between devices, shift(): lax.ppermute(value, axis, [(i, (i + step) % size) for i in range(size)])  59 us
    unnamed x88, local copies, waits for them, and re-layouts  23.3 us
    all_to_all x5, starting transfers between devices, over(): return lax.all_to_all(value, axis, split_axis=0, concat_axis=0, tiled=True)  22.1 us
  transfers between devices with their start and end apart: 48, of which 18 were waited for; matrix products, arithmetic and copies ran while one was open for 3% of the time, Pallas kernels for 21%

profile of v1, /device:TPU:0, one launch (start us, length us, event | category | flops | bytes accessed | tf_op | source)
XLA Modules:
  0.0 323.5 jit_solution(11520592523206856389)
XLA Ops:
  0.8 4.5 %all-to-all-start = ((bf16[8,4,32,768]{3,2,1,0:T(8,128)(2,1)}), bf16[8,4,32,768]{3,2,1,0:T(8,128)(2,1)S(1)}, u32[]{:S(2)}, u32[]{:S(2)}) async-start(bf16[8,4,32,768]{3,2,1,0:T(8,128)(2,1)} %bitcast.28), calls=%async_computation | async-start | bytes 3145728 | tf_op jit(solution)/shard_map/all_to_all | solution.py:751
  19.1 4.1 %collective-permute-start.5 = (bf16[24,2816]{1,0:T(8,128)(2,1)S(1)}, bf16[24,2816]{1,0:T(8,128)(2,1)S(1)}, u32[]{:S(2)}, u32[]{:S(2)}) collective-permute-start(bf16[24,2816]{1,0:T(8,128)(2,1)S(1)} %get-tuple-element.94.own), channel_id=1, source_target_pairs={{0,12},{4,0},{8,4},{12,8},{1,13},{5,1},{9,5},{13,9},{2,14},{6,2},{... | collective-permute-start | bytes 405512 | tf_op jit(solution)/shard_map/ppermute | solution.py:718
  23.3 3.7 %all-to-all-done.x_in = bf16[8,4,32,768]{3,2,1,0:T(8,128)(2,1)S(1)} async-done(((bf16[8,4,32,768]{3,2,1,0:T(8,128)(2,1)}), bf16[8,4,32,768]{3,2,1,0:T(8,128)(2,1)S(1)}, u32[]{:S(2)}, u32[]{:S(2)}) %all-to-all-start) | async-done | bytes 1572896 | tf_op jit(solution)/shard_map/all_to_all | solution.py:751
  29.7 3.9 %collective-permute-start.4 = (bf16[24,2816]{1,0:T(8,128)(2,1)S(1)}, bf16[24,2816]{1,0:T(8,128)(2,1)S(1)}, u32[]{:S(2)}, u32[]{:S(2)}) collective-permute-start(bf16[24,2816]{1,0:T(8,128)(2,1)S(1)} %get-tuple-element.94.own), channel_id=1, source_target_pairs={{0,8},{4,12},{8,0},{12,4},{1,9},{5,13},{9,1},{13,5},{2,10},{6,14},... | collective-permute-start | bytes 405512 | tf_op jit(solution)/shard_map/ppermute | solution.py:718
  34.6 3.4 %collective-permute-done.4.r2 = bf16[24,2816]{1,0:T(8,128)(2,1)S(1)} collective-permute-done((bf16[24,2816]{1,0:T(8,128)(2,1)S(1)}, bf16[24,2816]{1,0:T(8,128)(2,1)S(1)}, u32[]{:S(2)}, u32[]{:S(2)}) %collective-permute-start.4) | collective-permute-done | bytes 135200 | tf_op jit(solution)/shard_map/ppermute | solution.py:718
  45.3 3.2 collective-permute-start.11
  50.0 4.9 %all-to-all-start.2 = ((bf16[4,4,48,768]{3,2,1,0:T(8,128)(2,1)}), bf16[4,4,48,768]{3,2,1,0:T(8,128)(2,1)}, u32[]{:S(2)}, u32[]{:S(2)}) async-start(bf16[4,4,48,768]{3,2,1,0:T(8,128)(2,1)} %broadcast_in_dim.10), calls=%async_computation.2 | async-start | bytes 2359296 | tf_op jit(solution)/shard_map/all_to_all | solution.py:751
  54.9 17.5 %collective-permute-done.7.p2 = bf16[96,2816]{1,0:T(8,128)(2,1)} collective-permute-done((bf16[96,2816]{1,0:T(8,128)(2,1)}, bf16[96,2816]{1,0:T(8,128)(2,1)}, u32[]{:S(2)}, u32[]{:S(2)}) %collective-permute-start.7) | collective-permute-done | bytes 540704 | tf_op jit(solution)/shard_map/ppermute | solution.py:718
  75.4 3.6 %collective-permute-start.19 = (bf16[4,48,3840]{2,1,0:T(8,128)(2,1)}, bf16[4,48,3840]{2,1,0:T(8,128)(2,1)}, u32[]{:S(2)}, u32[]{:S(2)}) collective-permute-start(bf16[4,48,3840]{2,1,0:T(8,128)(2,1)} %pad_maximum_fusion.i0), channel_id=1, source_target_pairs={{0,8},{4,12},{8,0},{12,4},{1,9},{5,13},{9,1},{13,5},{2,10},{6,14},... | collective-permute-start | bytes 4423688 | tf_op jit(solution)/shard_map/ppermute | solution.py:718
  79.0 4.1 %all-to-all-start.1 = ((bf16[8,4,32,768]{3,2,1,0:T(8,128)(2,1)}), bf16[8,4,32,768]{3,2,1,0:T(8,128)(2,1)S(1)}, u32[]{:S(2)}, u32[]{:S(2)}) async-start(bf16[8,4,32,768]{3,2,1,0:T(8,128)(2,1)} %bitcast.29), calls=%async_computation.1 | async-start | bytes 3145728 | tf_op jit(solution)/shard_map/all_to_all | solution.py:751
  83.2 3.5 %collective-permute-start.22 = (bf16[4,4,48,768]{3,2,1,0:T(8,128)(2,1)}, bf16[4,4,48,768]{3,2,1,0:T(8,128)(2,1)}, u32[]{:S(2)}, u32[]{:S(2)}) collective-permute-start(bf16[4,4,48,768]{3,2,1,0:T(8,128)(2,1)} %all-to-all-done.2.j0), channel_id=1, source_target_pairs={{0,2},{1,3},{2,0},{3,1},{4,6},{5,7},{6,4},{7,5},{8,10},{9,11},{10,... | collective-permute-start | bytes 3538952 | tf_op jit(solution)/shard_map/ppermute | solution.py:718
  86.7 21.6 %attention_forward.1 = (bf16[768,1024]{1,0:T(8,128)(2,1)S(1)}, bf16[1024,2304]{1,0:T(8,128)(2,1)S(1)}, bf16[4,12,256,256]{3,2,1,0:T(8,128)(2,1)S(1)}, f32[4,16,2...) custom-call(s32[16]{0:T(128)S(1)} %pad.48.ids, ...), custom_call_target="tpu_custom_call" | custom-call | flops 22000001024 | bytes 22000000 | tf_op jit(solution)/shard_map/attention_forward/pallas_call | solution.py:550
  118.3 5.5 %collective-permute-done.21.j1 = bf16[4,4,48,768]{3,2,1,0:T(8,128)(2,1)S(1)} collective-permute-done((bf16[4,4,48,768]{3,2,1,0:T(8,128)(2,1)}, bf16[4,4,48,768]{3,2,1,0:T(8,128)(2,1)S(1)}, u32[]{:S(2)}, u32[]{:S(2)}) %collective-permute-start.21) | collective-permute-done | bytes 1179680 | tf_op jit(solution)/shard_map/ppermute | solution.py:718
  127.0 65.8 %feed_forward.1 = (bf16[1024,768]{1,0:T(8,128)(2,1)}, f32[1024,768]{1,0:T(8,128)}, bf16[1024,768]{1,0:T(8,128)(2,1)}, bf16[4,384,768]{2,1,0:T(8,128)(2,1)}, bf16...) custom-call(s32[16]{0:T(128)} %pad_add_fusion.1.ids, ...), custom_call_target="tpu_custom_call" | custom-call | flops 49999998976 | bytes 40000000 | tf_op jit(solution)/shard_map/feed_forward/pallas_call | solution.py:550
  195.4 3.2 collective-permute-done.24.refs_1_
  201.4 3.3 %sum_blocks.1 = (bf16[4,24,3968]{2,1,0:T(8,128)(2,1)S(1)}, bf16[4,24,3968]{2,1,0:T(8,128)(2,1)}, bf16[4,24,3968]{2,1,0:T(8,128)(2,1)}, bf16[4,24,3968]{2,1,0:T(8,128)(2,1)}) custom-call(s32[16]{0:T(128)S(1)} %pad.48.ids, bf16[4,96,3072]{2,1,0:T(8,128)(2,1)S(1)} %copy-done.1, bf16[4,96,3072]{2,1,0:T(8,128)(2,1)S(1)} %collective-permute-done.24.refs_1_, ...), custom_call_target="tpu_custom_call" | custom-call | flops 1000000 | bytes 6000000 | tf_op jit(solution)/shard_map/sum_blocks/pallas_call | solution.py:550
  211.2 3.8 %all-to-all-start.3 = ((bf16[4,4,4,24,768]{4,3,2,1,0:T(8,128)(2,1)}), bf16[4,4,4,24,768]{4,3,2,1,0:T(8,128)(2,1)S(1)}, u32[]{:S(2)}, u32[]{:S(2)}) async-start(bf16[4,4,4,24,768]{4,3,2,1,0:T(8,128)(2,1)} %sum_outer.1), calls=%async_computation.3 | async-start | bytes 4718592 | tf_op jit(solution)/shard_map/all_to_all | solution.py:751
  224.8 30.4 %attention_backward.1 = (bf16[8,2,4,32,768]{4,3,2,1,0:T(8,128)(2,1)}, bf16[4,96,2432]{2,1,0:T(8,128)(2,1)}, bf16[4,96,2432]{2,1,0:T(8,128)(2,1)}) custom-call(s32[16]{0:T(128)S(1)} %copy-done.18, f32[1024,768]{1,0:T(8,128)} %get-tuple-element.123.dsum, bf16[1024,768]{1,0:T(8,128)(2,1)S(1)} %copy-done.26, bf16[1024,2304]{1,0:T(8,128)(2,1)} %copy-done.20, ...), custom_call_target="tpu_custom_call" | custom-call | flops 28000000000 | bytes 30000000 | tf_op jit(solution)/shard_map/attention_backward/pallas_call | solution.py:550
  256.1 4.8 %all-to-all-start.4 = ((bf16[8,2,4,32,768]{4,3,2,1,0:T(8,128)(2,1)}), bf16[8,2,4,32,768]{4,3,2,1,0:T(8,128)(2,1)}, u32[]{:S(2)}, u32[]{:S(2)}) async-start(bf16[8,2,4,32,768]{4,3,2,1,0:T(8,128)(2,1)} %get-tuple-element.134), calls=%async_computation.4 | async-start | bytes 6291456 | tf_op jit(solution)/shard_map/all_to_all | solution.py:751
  261.5 4.0 %collective-permute-done.30.refs_2_ = bf16[4,96,2432]{2,1,0:T(8,128)(2,1)S(1)} collective-permute-done((bf16[4,96,2432]{2,1,0:T(8,128)(2,1)}, bf16[4,96,2432]{2,1,0:T(8,128)(2,1)S(1)}, u32[]{:S(2)}, u32[]{:S(2)}) %collective-permute-start.30) | collective-permute-done | bytes 1867808 | tf_op jit(solution)/shard_map/ppermute | solution.py:718
  280.5 4.1 %collective-permute-done.34.refs_1_ = bf16[4,24,3200]{2,1,0:T(8,128)(2,1)S(1)} collective-permute-done((bf16[4,24,3200]{2,1,0:T(8,128)(2,1)S(1)}, bf16[4,24,3200]{2,1,0:T(8,128)(2,1)S(1)}, u32[]{:S(2)}, u32[]{:S(2)}) %collective-permute-start.34) | collective-permute-done | bytes 614432 | tf_op jit(solution)/shard_map/ppermute | solution.py:718
  287.8 9.5 %collective-permute-done.35.refs_2_ = bf16[4,24,3200]{2,1,0:T(8,128)(2,1)S(1)} collective-permute-done((bf16[4,24,3200]{2,1,0:T(8,128)(2,1)S(1)}, bf16[4,24,3200]{2,1,0:T(8,128)(2,1)S(1)}, u32[]{:S(2)}, u32[]{:S(2)}) %collective-permute-start.35) | collective-permute-done | bytes 614432 | tf_op jit(solution)/shard_map/ppermute | solution.py:718
  306.3 3.5 %collective-permute-done.38.a2 = bf16[4,8,2304]{2,1,0:T(8,128)(2,1)S(1)} collective-permute-done((bf16[4,8,2304]{2,1,0:T(8,128)(2,1)S(1)}, bf16[4,8,2304]{2,1,0:T(8,128)(2,1)S(1)}, u32[]{:S(2)}, u32[]{:S(2)}) %collective-permute-start.38) | collective-permute-done | bytes 147488 | tf_op jit(solution)/shard_map/ppermute | solution.py:718
  316.9 3.8 %fusion = (bf16[8,1,4,32,768]{4,3,2,1,0:T(8,128)(2,1)}, bf16[8,1,4,32,768]{4,3,2,1,0:T(8,128)(2,1)}) fusion(bf16[8,2,4,32,768]{4,3,2,1,0:T(8,128)(2,1)} %all-to-all-done.4), kind=kLoop, calls=%fused_computation.19 | loop fusion | bytes 6291456 | tf_op jit(solution)/shard_map/slice | solution.py:882
  (193 shorter events, 102.4 us)
Async XLA Ops:
  0.8 26.1 %all-to-all-start = ((bf16[8,4,32,768]{3,2,1,0:T(8,128)(2,1)}), bf16[8,4,32,768]{3,2,1,0:T(8,128)(2,1)S(1)}, u32[]{:S(2)}, u32[]{:S(2)}) async-start(bf16[8,4,32,768]{3,2,1,0:T(8,128)(2,1)} %bitcast.28), calls=%async_computation | async-start | bytes 3145728 | tf_op jit(solution)/shard_map/all_to_all | solution.py:751
  19.1 14.4 %collective-permute-start.5 = (bf16[24,2816]{1,0:T(8,128)(2,1)S(1)}, bf16[24,2816]{1,0:T(8,128)(2,1)S(1)}, u32[]{:S(2)}, u32[]{:S(2)}) collective-permute-start(bf16[24,2816]{1,0:T(8,128)(2,1)S(1)} %get-tuple-element.94.own), channel_id=1, source_target_pairs={{0,12},{4,0},{8,4},{12,8},{1,13},{5,1},{9,5},{13,9},{2,14},{6,2},{... | collective-permute-start | bytes 405512 | tf_op jit(solution)/shard_map/ppermute | solution.py:718
  27.0 14.4 %collective-permute-start.16 = (bf16[24,5376]{1,0:T(8,128)(2,1)S(1)}, bf16[24,5376]{1,0:T(8,128)(2,1)S(1)}, u32[]{:S(2)}, u32[]{:S(2)}) collective-permute-start(bf16[24,5376]{1,0:T(8,128)(2,1)S(1)} %pad_maximum_fusion.1.p0), channel_id=1, source_target_pairs={{0,96},{32,0},{64,32},{96,64},{1,97},{33,1},{65,33},{97,65},{2,98}... | collective-permute-start | bytes 774152 | tf_op jit(solution)/shard_map/ppermute | solution.py:718
  43.3 29.6 %collective-permute-start.17 = (bf16[4,24,3840]{2,1,0:T(8,128)(2,1)S(1)}, bf16[4,24,3840]{2,1,0:T(8,128)(2,1)}, u32[]{:S(2)}, u32[]{:S(2)}) collective-permute-start(bf16[4,24,3840]{2,1,0:T(8,128)(2,1)S(1)} %get-tuple-element.102), channel_id=1, source_target_pairs={{0,4},{4,0},{8,12},{12,8},{1,5},{5,1},{9,13},{13,9},{2,6},{6,2},{1... | collective-permute-start | bytes 2211848 | tf_op jit(solution)/shard_map/ppermute | solution.py:722
  45.3 27.0 %collective-permute-start.7 = (bf16[96,2816]{1,0:T(8,128)(2,1)}, bf16[96,2816]{1,0:T(8,128)(2,1)}, u32[]{:S(2)}, u32[]{:S(2)}) collective-permute-start(bf16[96,2816]{1,0:T(8,128)(2,1)} %bitcast.6.p0), channel_id=1, source_target_pairs={{0,32},{32,64},{64,96},{96,0},{1,33},{33,65},{65,97},{97,1},{2,34}... | collective-permute-start | bytes 1622024 | tf_op jit(solution)/shard_map/ppermute | solution.py:718
  45.3 27.0 %collective-permute-start.11 = (bf16[96,2816]{1,0:T(8,128)(2,1)}, bf16[96,2816]{1,0:T(8,128)(2,1)}, u32[]{:S(2)}, u32[]{:S(2)}) collective-permute-start(bf16[96,2816]{1,0:T(8,128)(2,1)} %bitcast.6.p0), channel_id=1, source_target_pairs={{0,96},{32,0},{64,32},{96,64},{1,97},{33,1},{65,33},{97,65},{2,98}... | collective-permute-start | bytes 1622024 | tf_op jit(solution)/shard_map/ppermute | solution.py:718
  48.6 24.3 %collective-permute-start.9 = (bf16[96,2816]{1,0:T(8,128)(2,1)}, bf16[96,2816]{1,0:T(8,128)(2,1)}, u32[]{:S(2)}, u32[]{:S(2)}) collective-permute-start(bf16[96,2816]{1,0:T(8,128)(2,1)} %bitcast.6.p0), channel_id=1, source_target_pairs={{0,64},{32,96},{64,0},{96,32},{1,65},{33,97},{65,1},{97,33},{2,66}... | collective-permute-start | bytes 1622024 | tf_op jit(solution)/shard_map/ppermute | solution.py:718
  48.9 34.2 %collective-permute-start.6 = (bf16[96,2816]{1,0:T(8,128)(2,1)}, bf16[96,2816]{1,0:T(8,128)(2,1)}, u32[]{:S(2)}, u32[]{:S(2)}) collective-permute-start(bf16[96,2816]{1,0:T(8,128)(2,1)} %bitcast.6.p0), channel_id=1, source_target_pairs={{0,16},{16,0},{1,17},{17,1},{2,18},{18,2},{3,19},{19,3},{4,20},{20... | collective-permute-start | bytes 1622024 | tf_op jit(solution)/shard_map/ppermute | solution.py:718
  50.0 29.0 %all-to-all-start.2 = ((bf16[4,4,48,768]{3,2,1,0:T(8,128)(2,1)}), bf16[4,4,48,768]{3,2,1,0:T(8,128)(2,1)}, u32[]{:S(2)}, u32[]{:S(2)}) async-start(bf16[4,4,48,768]{3,2,1,0:T(8,128)(2,1)} %broadcast_in_dim.10), calls=%async_computation.2 | async-start | bytes 2359296 | tf_op jit(solution)/shard_map/all_to_all | solution.py:751
  72.4 14.3 %collective-permute-start.8 = (bf16[96,2816]{1,0:T(8,128)(2,1)}, bf16[96,2816]{1,0:T(8,128)(2,1)}, u32[]{:S(2)}, u32[]{:S(2)}) collective-permute-start(bf16[96,2816]{1,0:T(8,128)(2,1)} %collective-permute-done.7.p2), channel_id=1, source_target_pairs={{0,16},{16,0},{1,17},{17,1},{2,18},{18,2},{3,19},{19,3},{4,20},{20... | collective-permute-start | bytes 1622024 | tf_op jit(solution)/shard_map/ppermute | solution.py:718
  75.4 41.3 %collective-permute-start.19 = (bf16[4,48,3840]{2,1,0:T(8,128)(2,1)}, bf16[4,48,3840]{2,1,0:T(8,128)(2,1)}, u32[]{:S(2)}, u32[]{:S(2)}) collective-permute-start(bf16[4,48,3840]{2,1,0:T(8,128)(2,1)} %pad_maximum_fusion.i0), channel_id=1, source_target_pairs={{0,8},{4,12},{8,0},{12,4},{1,9},{5,13},{9,1},{13,5},{2,10},{6,14},... | collective-permute-start | bytes 4423688 | tf_op jit(solution)/shard_map/ppermute | solution.py:718
  79.0 37.5 %all-to-all-start.1 = ((bf16[8,4,32,768]{3,2,1,0:T(8,128)(2,1)}), bf16[8,4,32,768]{3,2,1,0:T(8,128)(2,1)S(1)}, u32[]{:S(2)}, u32[]{:S(2)}) async-start(bf16[8,4,32,768]{3,2,1,0:T(8,128)(2,1)} %bitcast.29), calls=%async_computation.1 | async-start | bytes 3145728 | tf_op jit(solution)/shard_map/all_to_all | solution.py:751
  83.2 34.0 %collective-permute-start.22 = (bf16[4,4,48,768]{3,2,1,0:T(8,128)(2,1)}, bf16[4,4,48,768]{3,2,1,0:T(8,128)(2,1)}, u32[]{:S(2)}, u32[]{:S(2)}) collective-permute-start(bf16[4,4,48,768]{3,2,1,0:T(8,128)(2,1)} %all-to-all-done.2.j0), channel_id=1, source_target_pairs={{0,2},{1,3},{2,0},{3,1},{4,6},{5,7},{6,4},{7,5},{8,10},{9,11},{10,... | collective-permute-start | bytes 3538952 | tf_op jit(solution)/shard_map/ppermute | solution.py:718
  205.5 55.4 %collective-permute-start.27 = (bf16[4,24,3968]{2,1,0:T(8,128)(2,1)}, bf16[4,24,3968]{2,1,0:T(8,128)(2,1)}, u32[]{:S(2)}, u32[]{:S(2)}) collective-permute-start(bf16[4,24,3968]{2,1,0:T(8,128)(2,1)} %get-tuple-element.136), channel_id=1, source_target_pairs={{0,4},{4,8},{8,12},{12,0},{1,5},{5,9},{9,13},{13,1},{2,6},{6,10},{... | collective-permute-start | bytes 2285576 | tf_op jit(solution)/shard_map/ppermute | solution.py:718
  205.5 55.4 %collective-permute-start.28 = (bf16[4,24,3968]{2,1,0:T(8,128)(2,1)}, bf16[4,24,3968]{2,1,0:T(8,128)(2,1)}, u32[]{:S(2)}, u32[]{:S(2)}) collective-permute-start(bf16[4,24,3968]{2,1,0:T(8,128)(2,1)} %get-tuple-element.137), channel_id=1, source_target_pairs={{0,8},{4,12},{8,0},{12,4},{1,9},{5,13},{9,1},{13,5},{2,10},{6,14},... | collective-permute-start | bytes 2285576 | tf_op jit(solution)/shard_map/ppermute | solution.py:718
  206.4 54.5 %collective-permute-start.29 = (bf16[4,24,3968]{2,1,0:T(8,128)(2,1)}, bf16[4,24,3968]{2,1,0:T(8,128)(2,1)}, u32[]{:S(2)}, u32[]{:S(2)}) collective-permute-start(bf16[4,24,3968]{2,1,0:T(8,128)(2,1)} %get-tuple-element.138), channel_id=1, source_target_pairs={{0,12},{4,0},{8,4},{12,8},{1,13},{5,1},{9,5},{13,9},{2,14},{6,2},{... | collective-permute-start | bytes 2285576 | tf_op jit(solution)/shard_map/ppermute | solution.py:718
  211.2 44.0 %all-to-all-start.3 = ((bf16[4,4,4,24,768]{4,3,2,1,0:T(8,128)(2,1)}), bf16[4,4,4,24,768]{4,3,2,1,0:T(8,128)(2,1)S(1)}, u32[]{:S(2)}, u32[]{:S(2)}) async-start(bf16[4,4,4,24,768]{4,3,2,1,0:T(8,128)(2,1)} %sum_outer.1), calls=%async_computation.3 | async-start | bytes 4718592 | tf_op jit(solution)/shard_map/all_to_all | solution.py:751
  256.1 60.9 %all-to-all-start.4 = ((bf16[8,2,4,32,768]{4,3,2,1,0:T(8,128)(2,1)}), bf16[8,2,4,32,768]{4,3,2,1,0:T(8,128)(2,1)}, u32[]{:S(2)}, u32[]{:S(2)}) async-start(bf16[8,2,4,32,768]{4,3,2,1,0:T(8,128)(2,1)} %get-tuple-element.134), calls=%async_computation.4 | async-start | bytes 6291456 | tf_op jit(solution)/shard_map/all_to_all | solution.py:751
  266.9 17.7 %collective-permute-start.34 = (bf16[4,24,3200]{2,1,0:T(8,128)(2,1)S(1)}, bf16[4,24,3200]{2,1,0:T(8,128)(2,1)S(1)}, u32[]{:S(2)}, u32[]{:S(2)}) collective-permute-start(bf16[4,24,3200]{2,1,0:T(8,128)(2,1)S(1)} %get-tuple-element.150), channel_id=1, source_target_pairs={{0,4},{4,8},{8,12},{12,0},{1,5},{5,9},{9,13},{13,1},{2,6},{6,10},{... | collective-permute-start | bytes 1843208 | tf_op jit(solution)/shard_map/ppermute | solution.py:718
  267.9 29.4 %collective-permute-start.35 = (bf16[4,24,3200]{2,1,0:T(8,128)(2,1)S(1)}, bf16[4,24,3200]{2,1,0:T(8,128)(2,1)S(1)}, u32[]{:S(2)}, u32[]{:S(2)}) collective-permute-start(bf16[4,24,3200]{2,1,0:T(8,128)(2,1)S(1)} %get-tuple-element.151), channel_id=1, source_target_pairs={{0,8},{4,12},{8,0},{12,4},{1,9},{5,13},{9,1},{13,5},{2,10},{6,14},... | collective-permute-start | bytes 1843208 | tf_op jit(solution)/shard_map/ppermute | solution.py:718
  270.0 27.9 %collective-permute-start.36 = (bf16[4,24,3200]{2,1,0:T(8,128)(2,1)S(1)}, bf16[4,24,3200]{2,1,0:T(8,128)(2,1)S(1)}, u32[]{:S(2)}, u32[]{:S(2)}) collective-permute-start(bf16[4,24,3200]{2,1,0:T(8,128)(2,1)S(1)} %get-tuple-element.152), channel_id=1, source_target_pairs={{0,12},{4,0},{8,4},{12,8},{1,13},{5,1},{9,5},{13,9},{2,14},{6,2},{... | collective-permute-start | bytes 1843208 | tf_op jit(solution)/shard_map/ppermute | solution.py:718
  275.6 28.2 %collective-permute-start.31 = (bf16[4,8,3840]{2,1,0:T(8,128)(2,1)S(1)}, bf16[4,8,3840]{2,1,0:T(8,128)(2,1)S(1)}, u32[]{:S(2)}, u32[]{:S(2)}) collective-permute-start(bf16[4,8,3840]{2,1,0:T(8,128)(2,1)S(1)} %get-tuple-element.146), channel_id=1, source_target_pairs={{0,1},{1,2},{2,3},{3,0},{4,5},{5,6},{6,7},{7,4},{8,9},{9,10},{10,1... | collective-permute-start | bytes 737288 | tf_op jit(solution)/shard_map/ppermute | solution.py:718
  277.8 27.4 %collective-permute-start.32 = (bf16[4,8,3840]{2,1,0:T(8,128)(2,1)S(1)}, bf16[4,8,3840]{2,1,0:T(8,128)(2,1)S(1)}, u32[]{:S(2)}, u32[]{:S(2)}) collective-permute-start(bf16[4,8,3840]{2,1,0:T(8,128)(2,1)S(1)} %get-tuple-element.147), channel_id=1, source_target_pairs={{0,2},{1,3},{2,0},{3,1},{4,6},{5,7},{6,4},{7,5},{8,10},{9,11},{10,... | collective-permute-start | bytes 737288 | tf_op jit(solution)/shard_map/ppermute | solution.py:718
  284.6 20.7 %collective-permute-start.33 = (bf16[4,8,3840]{2,1,0:T(8,128)(2,1)S(1)}, bf16[4,8,3840]{2,1,0:T(8,128)(2,1)S(1)}, u32[]{:S(2)}, u32[]{:S(2)}) collective-permute-start(bf16[4,8,3840]{2,1,0:T(8,128)(2,1)S(1)} %get-tuple-element.148), channel_id=1, source_target_pairs={{0,3},{1,0},{2,1},{3,2},{4,7},{5,4},{6,5},{7,6},{8,11},{9,8},{10,9... | collective-permute-start | bytes 737288 | tf_op jit(solution)/shard_map/ppermute | solution.py:718
  (68 other events, 467.6 us)

commit v2 on v1

--- a/solution.py
+++ b/solution.py
@@ -601,7 +601,7 @@
         22 * 10**9,
         22 * 10**6,
         ATTENTION_SCRATCH + [pltpu.VMEM((32, PACKED - 3 * WIDTH), f32), pltpu.SemaphoreType.DMA((8,))],
-        28,
+        58,
     )
 
 
@@ -649,7 +649,7 @@
             pltpu.SemaphoreType.DMA((RING, RING)),
             pltpu.SemaphoreType.DMA((RING, RING, RING)),
         ],
-        54,
+        58,
     )
 
 
@@ -674,7 +674,7 @@
             pltpu.SemaphoreType.DMA((8,)),
             pltpu.SemaphoreType.DMA((RING, RING)),
         ],
-        36,
+        58,
     )
 
 

time: 325 us -> 315 us (0.969)
  local copies, waits for them, and re-layouts: 29.6 us -> 12.2 us
  waiting for transfers between devices: 69 us -> 75.3 us
    unnamed x88 -> x68, local copies, waits for them, and re-layouts: 23.3 us -> 5.25 us
    ppermute x41, waiting for transfers between devices: 65.3 us -> 71.6 us  [shift(): lax.ppermute(value, axis, [(i, (i + step) % size) for i in range(size)])]
  transfers between devices with their start and end apart: 48 -> 48, of which waited for: 18 -> 19; matrix products, arithmetic and copies ran while one was open for 3% -> 3% of each run, Pallas kernels for 21% -> 23%
where the time goes in v2:
time: 315 us; the launch traced here: 314 us
  Pallas kernels  138 us (44%)
  starting transfers between devices  82.5 us (26%)
  waiting for transfers between devices  75.3 us (24%)
  local copies, waits for them, and re-layouts  12.2 us (4%)
  other arithmetic  3.97 us (1%)
    pallas_call x15, Pallas kernels, run(): pl.pallas_call(kernel, grid_spec=pltpu.PrefetchScalarGridSpec(num_scalar_...  138 us
    ppermute x41, waiting for transfers between devices, shift(): lax.ppermute(value, axis, [(i, (i + step) % size) for i in range(size)])  71.6 us
    ppermute x41, starting transfers between devices, shift(): lax.ppermute(value, axis, [(i, (i + step) % size) for i in range(size)])  56.3 us
    all_to_all x5, starting transfers between devices, over(): return lax.all_to_all(value, axis, split_axis=0, concat_axis=0, tiled=True)  22.6 us
  transfers between devices with their start and end apart: 48, of which 19 were waited for; matrix products, arithmetic and copies ran while one was open for 3% of the time, Pallas kernels for 23%

profile of v2, /device:TPU:0, one launch (start us, length us, event | category | flops | bytes accessed | tf_op | source)
XLA Modules:
  0.0 313.7 jit_solution(1466450344700927757)
XLA Ops:
  0.8 4.5 %all-to-all-start = ((bf16[8,4,32,768]{3,2,1,0:T(8,128)(2,1)}), bf16[8,4,32,768]{3,2,1,0:T(8,128)(2,1)S(1)}, u32[]{:S(2)}, u32[]{:S(2)}) async-start(bf16[8,4,32,768]{3,2,1,0:T(8,128)(2,1)} %bitcast.34), calls=%async_computation | async-start | bytes 3145728 | tf_op jit(solution)/shard_map/all_to_all | solution.py:751
  19.2 4.1 %collective-permute-start.5 = (bf16[24,2816]{1,0:T(8,128)(2,1)S(1)}, bf16[24,2816]{1,0:T(8,128)(2,1)S(1)}, u32[]{:S(2)}, u32[]{:S(2)}) collective-permute-start(bf16[24,2816]{1,0:T(8,128)(2,1)S(1)} %get-tuple-element.94.own), channel_id=1, source_target_pairs={{0,12},{4,0},{8,4},{12,8},{1,13},{5,1},{9,5},{13,9},{2,14},{6,2},{... | collective-permute-start | bytes 405512 | tf_op jit(solution)/shard_map/ppermute | solution.py:718
  23.3 3.7 %all-to-all-done.x_in = bf16[8,4,32,768]{3,2,1,0:T(8,128)(2,1)S(1)} async-done(((bf16[8,4,32,768]{3,2,1,0:T(8,128)(2,1)}), bf16[8,4,32,768]{3,2,1,0:T(8,128)(2,1)S(1)}, u32[]{:S(2)}, u32[]{:S(2)}) %all-to-all-start) | async-done | bytes 1572896 | tf_op jit(solution)/shard_map/all_to_all | solution.py:751
  29.7 3.9 %collective-permute-start.4 = (bf16[24,2816]{1,0:T(8,128)(2,1)S(1)}, bf16[24,2816]{1,0:T(8,128)(2,1)S(1)}, u32[]{:S(2)}, u32[]{:S(2)}) collective-permute-start(bf16[24,2816]{1,0:T(8,128)(2,1)S(1)} %get-tuple-element.94.own), channel_id=1, source_target_pairs={{0,8},{4,12},{8,0},{12,4},{1,9},{5,13},{9,1},{13,5},{2,10},{6,14},... | collective-permute-start | bytes 405512 | tf_op jit(solution)/shard_map/ppermute | solution.py:718
  34.6 3.4 %collective-permute-done.4.r2 = bf16[24,2816]{1,0:T(8,128)(2,1)S(1)} collective-permute-done((bf16[24,2816]{1,0:T(8,128)(2,1)S(1)}, bf16[24,2816]{1,0:T(8,128)(2,1)S(1)}, u32[]{:S(2)}, u32[]{:S(2)}) %collective-permute-start.4) | collective-permute-done | bytes 135200 | tf_op jit(solution)/shard_map/ppermute | solution.py:718
  45.3 3.2 %collective-permute-start.11 = (bf16[96,2816]{1,0:T(8,128)(2,1)S(1)}, bf16[96,2816]{1,0:T(8,128)(2,1)}, u32[]{:S(2)}, u32[]{:S(2)}) collective-permute-start(bf16[96,2816]{1,0:T(8,128)(2,1)S(1)} %bitcast.29), channel_id=1, source_target_pairs={{0,96},{32,0},{64,32},{96,64},{1,97},{33,1},{65,33},{97,65},{2,98}... | collective-permute-start | bytes 1622024 | tf_op jit(solution)/shard_map/ppermute | solution.py:718
  50.6 4.9 %all-to-all-start.2 = ((bf16[4,4,48,768]{3,2,1,0:T(8,128)(2,1)}), bf16[4,4,48,768]{3,2,1,0:T(8,128)(2,1)S(1)}, u32[]{:S(2)}, u32[]{:S(2)}) async-start(bf16[4,4,48,768]{3,2,1,0:T(8,128)(2,1)} %broadcast_in_dim.10), calls=%async_computation.2 | async-start | bytes 2359296 | tf_op jit(solution)/shard_map/all_to_all | solution.py:751
  55.5 16.7 %collective-permute-done.7.p2 = bf16[96,2816]{1,0:T(8,128)(2,1)} collective-permute-done((bf16[96,2816]{1,0:T(8,128)(2,1)S(1)}, bf16[96,2816]{1,0:T(8,128)(2,1)}, u32[]{:S(2)}, u32[]{:S(2)}) %collective-permute-start.7) | collective-permute-done | bytes 540704 | tf_op jit(solution)/shard_map/ppermute | solution.py:718
  75.2 3.6 %collective-permute-start.19 = (bf16[4,48,3840]{2,1,0:T(8,128)(2,1)}, bf16[4,48,3840]{2,1,0:T(8,128)(2,1)}, u32[]{:S(2)}, u32[]{:S(2)}) collective-permute-start(bf16[4,48,3840]{2,1,0:T(8,128)(2,1)} %pad_maximum_fusion.i0), channel_id=1, source_target_pairs={{0,8},{4,12},{8,0},{12,4},{1,9},{5,13},{9,1},{13,5},{2,10},{6,14},... | collective-permute-start | bytes 4423688 | tf_op jit(solution)/shard_map/ppermute | solution.py:718
  78.8 4.1 %all-to-all-start.1 = ((bf16[8,4,32,768]{3,2,1,0:T(8,128)(2,1)}), bf16[8,4,32,768]{3,2,1,0:T(8,128)(2,1)S(1)}, u32[]{:S(2)}, u32[]{:S(2)}) async-start(bf16[8,4,32,768]{3,2,1,0:T(8,128)(2,1)} %bitcast.7), calls=%async_computation.1 | async-start | bytes 3145728 | tf_op jit(solution)/shard_map/all_to_all | solution.py:751
  83.0 3.5 %collective-permute-start.22 = (bf16[4,4,48,768]{3,2,1,0:T(8,128)(2,1)S(1)}, bf16[4,4,48,768]{3,2,1,0:T(8,128)(2,1)}, u32[]{:S(2)}, u32[]{:S(2)}) collective-permute-start(bf16[4,4,48,768]{3,2,1,0:T(8,128)(2,1)S(1)} %all-to-all-done.2.j0), channel_id=1, source_target_pairs={{0,2},{1,3},{2,0},{3,1},{4,6},{5,7},{6,4},{7,5},{8,10},{9,11},{10,... | collective-permute-start | bytes 3538952 | tf_op jit(solution)/shard_map/ppermute | solution.py:718
  86.5 23.7 %attention_forward.1 = (bf16[768,1024]{1,0:T(8,128)(2,1)}, bf16[1024,2304]{1,0:T(8,128)(2,1)}, bf16[4,12,256,256]{3,2,1,0:T(8,128)(2,1)}, f32[4,16,256]{2,1,0:T(...) custom-call(s32[16]{0:T(128)} %copy-done.7, ...), custom_call_target="tpu_custom_call" | custom-call | flops 22000001024 | bytes 22000000 | tf_op jit(solution)/shard_map/attention_forward/pallas_call | solution.py:550
  120.8 65.8 %feed_forward.1 = (bf16[1024,768]{1,0:T(8,128)(2,1)}, f32[1024,768]{1,0:T(8,128)}, bf16[1024,768]{1,0:T(8,128)(2,1)}, bf16[4,384,768]{2,1,0:T(8,128)(2,1)}, bf16...) custom-call(s32[16]{0:T(128)} %pad_add_fusion.1.ids, ...), custom_call_target="tpu_custom_call" | custom-call | flops 49999998976 | bytes 40000000 | tf_op jit(solution)/shard_map/feed_forward/pallas_call | solution.py:550
  189.2 3.2 %collective-permute-done.24.refs_1_ = bf16[4,96,3072]{2,1,0:T(8,128)(2,1)S(1)} collective-permute-done((bf16[4,96,3072]{2,1,0:T(8,128)(2,1)}, bf16[4,96,3072]{2,1,0:T(8,128)(2,1)S(1)}, u32[]{:S(2)}, u32[]{:S(2)}) %collective-permute-start.24) | collective-permute-done | bytes 2359328 | tf_op jit(solution)/shard_map/ppermute | solution.py:718
  195.2 3.2 %sum_blocks.1 = (bf16[4,24,3968]{2,1,0:T(8,128)(2,1)S(1)}, bf16[4,24,3968]{2,1,0:T(8,128)(2,1)}, bf16[4,24,3968]{2,1,0:T(8,128)(2,1)}, bf16[4,24,3968]{2,1,0:T(8,128)(2,1)}) custom-call(s32[16]{0:T(128)S(1)} %copy-done.8, bf16[4,96,3072]{2,1,0:T(8,128)(2,1)S(1)} %copy-done.1, bf16[4,96,3072]{2,1,0:T(8,128)(2,1)S(1)} %collective-permute-done.24.refs_1_, ...), custom_call_target="tpu_custom_call" | custom-call | flops 1000000 | bytes 6000000 | tf_op jit(solution)/shard_map/sum_blocks/pallas_call | solution.py:550
  199.5 3.3 %collective-permute-start.28 = (bf16[4,24,3968]{2,1,0:T(8,128)(2,1)}, bf16[4,24,3968]{2,1,0:T(8,128)(2,1)}, u32[]{:S(2)}, u32[]{:S(2)}) collective-permute-start(bf16[4,24,3968]{2,1,0:T(8,128)(2,1)} %get-tuple-element.137), channel_id=1, source_target_pairs={{0,8},{4,12},{8,0},{12,4},{1,9},{5,13},{9,1},{13,5},{2,10},{6,14},... | collective-permute-start | bytes 2285576 | tf_op jit(solution)/shard_map/ppermute | solution.py:718
  207.5 4.5 %all-to-all-start.3 = ((bf16[4,4,4,24,768]{4,3,2,1,0:T(8,128)(2,1)}), bf16[4,4,4,24,768]{4,3,2,1,0:T(8,128)(2,1)S(1)}, u32[]{:S(2)}, u32[]{:S(2)}) async-start(bf16[4,4,4,24,768]{4,3,2,1,0:T(8,128)(2,1)} %sum_outer.1), calls=%async_computation.3 | async-start | bytes 4718592 | tf_op jit(solution)/shard_map/all_to_all | solution.py:751
  211.9 32.1 %attention_backward.1 = (bf16[8,2,4,32,768]{4,3,2,1,0:T(8,128)(2,1)}, bf16[4,96,2432]{2,1,0:T(8,128)(2,1)}, bf16[4,96,2432]{2,1,0:T(8,128)(2,1)}) custom-call(s32[16]{0:T(128)} %pad_add_fusion.1.ids, f32[1024,768]{1,0:T(8,128)} %get-tuple-element.123.dsum, bf16[1024,768]{1,0:T(8,128)(2,1)} %get-tuple-element.124.dattn, ...), custom_call_target="tpu_custom_call" | custom-call | flops 28000000000 | bytes 30000000 | tf_op jit(solution)/shard_map/attention_backward/pallas_call | solution.py:550
  244.9 4.6 %all-to-all-start.4 = ((bf16[8,2,4,32,768]{4,3,2,1,0:T(8,128)(2,1)}), bf16[8,2,4,32,768]{4,3,2,1,0:T(8,128)(2,1)}, u32[]{:S(2)}, u32[]{:S(2)}) async-start(bf16[8,2,4,32,768]{4,3,2,1,0:T(8,128)(2,1)} %get-tuple-element.134), calls=%async_computation.4 | async-start | bytes 6291456 | tf_op jit(solution)/shard_map/all_to_all | solution.py:751
  249.9 4.0 %collective-permute-done.30.refs_2_ = bf16[4,96,2432]{2,1,0:T(8,128)(2,1)S(1)} collective-permute-done((bf16[4,96,2432]{2,1,0:T(8,128)(2,1)}, bf16[4,96,2432]{2,1,0:T(8,128)(2,1)S(1)}, u32[]{:S(2)}, u32[]{:S(2)}) %collective-permute-start.30) | collective-permute-done | bytes 1867808 | tf_op jit(solution)/shard_map/ppermute | solution.py:718
  266.6 19.0 %collective-permute-done.34.refs_1_ = bf16[4,24,3200]{2,1,0:T(8,128)(2,1)S(1)} collective-permute-done((bf16[4,24,3200]{2,1,0:T(8,128)(2,1)S(1)}, bf16[4,24,3200]{2,1,0:T(8,128)(2,1)S(1)}, u32[]{:S(2)}, u32[]{:S(2)}) %collective-permute-start.34) | collective-permute-done | bytes 614432 | tf_op jit(solution)/shard_map/ppermute | solution.py:718
  285.7 3.2 %collective-permute-start.33 = (bf16[4,8,3840]{2,1,0:T(8,128)(2,1)S(1)}, bf16[4,8,3840]{2,1,0:T(8,128)(2,1)S(1)}, u32[]{:S(2)}, u32[]{:S(2)}) collective-permute-start(bf16[4,8,3840]{2,1,0:T(8,128)(2,1)S(1)} %get-tuple-element.148), channel_id=1, source_target_pairs={{0,3},{1,0},{2,1},{3,2},{4,7},{5,4},{6,5},{7,6},{8,11},{9,8},{10,9... | collective-permute-start | bytes 737288 | tf_op jit(solution)/shard_map/ppermute | solution.py:718
  293.7 4.3 %collective-permute-done.33.i3 = bf16[4,8,3840]{2,1,0:T(8,128)(2,1)S(1)} collective-permute-done((bf16[4,8,3840]{2,1,0:T(8,128)(2,1)S(1)}, bf16[4,8,3840]{2,1,0:T(8,128)(2,1)S(1)}, u32[]{:S(2)}, u32[]{:S(2)}) %collective-permute-start.33) | collective-permute-done | bytes 245792 | tf_op jit(solution)/shard_map/ppermute | solution.py:718
  307.2 3.8 %fusion = (bf16[8,1,4,32,768]{4,3,2,1,0:T(8,128)(2,1)}, bf16[8,1,4,32,768]{4,3,2,1,0:T(8,128)(2,1)}) fusion(bf16[8,2,4,32,768]{4,3,2,1,0:T(8,128)(2,1)} %all-to-all-done.4), kind=kLoop, calls=%fused_computation.19 | loop fusion | bytes 6291456 | tf_op jit(solution)/shard_map/slice | solution.py:882
  (173 shorter events, 82.0 us)
Async XLA Ops:
  0.8 26.1 %all-to-all-start = ((bf16[8,4,32,768]{3,2,1,0:T(8,128)(2,1)}), bf16[8,4,32,768]{3,2,1,0:T(8,128)(2,1)S(1)}, u32[]{:S(2)}, u32[]{:S(2)}) async-start(bf16[8,4,32,768]{3,2,1,0:T(8,128)(2,1)} %bitcast.34), calls=%async_computation | async-start | bytes 3145728 | tf_op jit(solution)/shard_map/all_to_all | solution.py:751
  19.2 14.4 %collective-permute-start.5 = (bf16[24,2816]{1,0:T(8,128)(2,1)S(1)}, bf16[24,2816]{1,0:T(8,128)(2,1)S(1)}, u32[]{:S(2)}, u32[]{:S(2)}) collective-permute-start(bf16[24,2816]{1,0:T(8,128)(2,1)S(1)} %get-tuple-element.94.own), channel_id=1, source_target_pairs={{0,12},{4,0},{8,4},{12,8},{1,13},{5,1},{9,5},{13,9},{2,14},{6,2},{... | collective-permute-start | bytes 405512 | tf_op jit(solution)/shard_map/ppermute | solution.py:718
  43.3 29.4 %collective-permute-start.17 = (bf16[4,24,3840]{2,1,0:T(8,128)(2,1)S(1)}, bf16[4,24,3840]{2,1,0:T(8,128)(2,1)}, u32[]{:S(2)}, u32[]{:S(2)}) collective-permute-start(bf16[4,24,3840]{2,1,0:T(8,128)(2,1)S(1)} %get-tuple-element.102), channel_id=1, source_target_pairs={{0,4},{4,0},{8,12},{12,8},{1,5},{5,1},{9,13},{13,9},{2,6},{6,2},{1... | collective-permute-start | bytes 2211848 | tf_op jit(solution)/shard_map/ppermute | solution.py:722
  45.3 26.8 %collective-permute-start.7 = (bf16[96,2816]{1,0:T(8,128)(2,1)S(1)}, bf16[96,2816]{1,0:T(8,128)(2,1)}, u32[]{:S(2)}, u32[]{:S(2)}) collective-permute-start(bf16[96,2816]{1,0:T(8,128)(2,1)S(1)} %bitcast.28), channel_id=1, source_target_pairs={{0,32},{32,64},{64,96},{96,0},{1,33},{33,65},{65,97},{97,1},{2,34}... | collective-permute-start | bytes 1622024 | tf_op jit(solution)/shard_map/ppermute | solution.py:718
  45.3 26.8 %collective-permute-start.11 = (bf16[96,2816]{1,0:T(8,128)(2,1)S(1)}, bf16[96,2816]{1,0:T(8,128)(2,1)}, u32[]{:S(2)}, u32[]{:S(2)}) collective-permute-start(bf16[96,2816]{1,0:T(8,128)(2,1)S(1)} %bitcast.29), channel_id=1, source_target_pairs={{0,96},{32,0},{64,32},{96,64},{1,97},{33,1},{65,33},{97,65},{2,98}... | collective-permute-start | bytes 1622024 | tf_op jit(solution)/shard_map/ppermute | solution.py:718
  48.6 24.1 %collective-permute-start.9 = (bf16[96,2816]{1,0:T(8,128)(2,1)S(1)}, bf16[96,2816]{1,0:T(8,128)(2,1)}, u32[]{:S(2)}, u32[]{:S(2)}) collective-permute-start(bf16[96,2816]{1,0:T(8,128)(2,1)S(1)} %bitcast.30), channel_id=1, source_target_pairs={{0,64},{32,96},{64,0},{96,32},{1,65},{33,97},{65,1},{97,33},{2,66}... | collective-permute-start | bytes 1622024 | tf_op jit(solution)/shard_map/ppermute | solution.py:718
  49.5 33.4 %collective-permute-start.6 = (bf16[96,2816]{1,0:T(8,128)(2,1)S(1)}, bf16[96,2816]{1,0:T(8,128)(2,1)}, u32[]{:S(2)}, u32[]{:S(2)}) collective-permute-start(bf16[96,2816]{1,0:T(8,128)(2,1)S(1)} %bitcast.31), channel_id=1, source_target_pairs={{0,16},{16,0},{1,17},{17,1},{2,18},{18,2},{3,19},{19,3},{4,20},{20... | collective-permute-start | bytes 1622024 | tf_op jit(solution)/shard_map/ppermute | solution.py:718
  50.6 28.2 %all-to-all-start.2 = ((bf16[4,4,48,768]{3,2,1,0:T(8,128)(2,1)}), bf16[4,4,48,768]{3,2,1,0:T(8,128)(2,1)S(1)}, u32[]{:S(2)}, u32[]{:S(2)}) async-start(bf16[4,4,48,768]{3,2,1,0:T(8,128)(2,1)} %broadcast_in_dim.10), calls=%async_computation.2 | async-start | bytes 2359296 | tf_op jit(solution)/shard_map/all_to_all | solution.py:751
  72.2 14.3 %collective-permute-start.8 = (bf16[96,2816]{1,0:T(8,128)(2,1)}, bf16[96,2816]{1,0:T(8,128)(2,1)}, u32[]{:S(2)}, u32[]{:S(2)}) collective-permute-start(bf16[96,2816]{1,0:T(8,128)(2,1)} %collective-permute-done.7.p2), channel_id=1, source_target_pairs={{0,16},{16,0},{1,17},{17,1},{2,18},{18,2},{3,19},{19,3},{4,20},{20... | collective-permute-start | bytes 1622024 | tf_op jit(solution)/shard_map/ppermute | solution.py:718
  72.2 14.3 %collective-permute-start.12 = (bf16[96,2816]{1,0:T(8,128)(2,1)}, bf16[96,2816]{1,0:T(8,128)(2,1)}, u32[]{:S(2)}, u32[]{:S(2)}) collective-permute-start(bf16[96,2816]{1,0:T(8,128)(2,1)} %collective-permute-done.11.p6), channel_id=1, source_target_pairs={{0,16},{16,0},{1,17},{17,1},{2,18},{18,2},{3,19},{19,3},{4,20},{20... | collective-permute-start | bytes 1622024 | tf_op jit(solution)/shard_map/ppermute | solution.py:718
  75.2 36.8 %collective-permute-start.19 = (bf16[4,48,3840]{2,1,0:T(8,128)(2,1)}, bf16[4,48,3840]{2,1,0:T(8,128)(2,1)}, u32[]{:S(2)}, u32[]{:S(2)}) collective-permute-start(bf16[4,48,3840]{2,1,0:T(8,128)(2,1)} %pad_maximum_fusion.i0), channel_id=1, source_target_pairs={{0,8},{4,12},{8,0},{12,4},{1,9},{5,13},{9,1},{13,5},{2,10},{6,14},... | collective-permute-start | bytes 4423688 | tf_op jit(solution)/shard_map/ppermute | solution.py:718
  78.8 31.4 %all-to-all-start.1 = ((bf16[8,4,32,768]{3,2,1,0:T(8,128)(2,1)}), bf16[8,4,32,768]{3,2,1,0:T(8,128)(2,1)S(1)}, u32[]{:S(2)}, u32[]{:S(2)}) async-start(bf16[8,4,32,768]{3,2,1,0:T(8,128)(2,1)} %bitcast.7), calls=%async_computation.1 | async-start | bytes 3145728 | tf_op jit(solution)/shard_map/all_to_all | solution.py:751
  83.0 30.2 %collective-permute-start.22 = (bf16[4,4,48,768]{3,2,1,0:T(8,128)(2,1)S(1)}, bf16[4,4,48,768]{3,2,1,0:T(8,128)(2,1)}, u32[]{:S(2)}, u32[]{:S(2)}) collective-permute-start(bf16[4,4,48,768]{3,2,1,0:T(8,128)(2,1)S(1)} %all-to-all-done.2.j0), channel_id=1, source_target_pairs={{0,2},{1,3},{2,0},{3,1},{4,6},{5,7},{6,4},{7,5},{8,10},{9,11},{10,... | collective-permute-start | bytes 3538952 | tf_op jit(solution)/shard_map/ppermute | solution.py:718
  189.0 16.0 %collective-permute-start.26 = (bf16[4,384,768]{2,1,0:T(8,128)(2,1)}, bf16[4,384,768]{2,1,0:T(8,128)(2,1)S(1)}, u32[]{:S(2)}, u32[]{:S(2)}) collective-permute-start(bf16[4,384,768]{2,1,0:T(8,128)(2,1)} %get-tuple-element.122), channel_id=1, source_target_pairs={{0,16},{16,0},{1,17},{17,1},{2,18},{18,2},{3,19},{19,3},{4,20},{20... | collective-permute-start | bytes 7077896 | tf_op jit(solution)/shard_map/ppermute | solution.py:718
  199.3 50.2 %collective-permute-start.27 = (bf16[4,24,3968]{2,1,0:T(8,128)(2,1)}, bf16[4,24,3968]{2,1,0:T(8,128)(2,1)}, u32[]{:S(2)}, u32[]{:S(2)}) collective-permute-start(bf16[4,24,3968]{2,1,0:T(8,128)(2,1)} %get-tuple-element.136), channel_id=1, source_target_pairs={{0,4},{4,8},{8,12},{12,0},{1,5},{5,9},{9,13},{13,1},{2,6},{6,10},{... | collective-permute-start | bytes 2285576 | tf_op jit(solution)/shard_map/ppermute | solution.py:718
  199.5 50.0 %collective-permute-start.28 = (bf16[4,24,3968]{2,1,0:T(8,128)(2,1)}, bf16[4,24,3968]{2,1,0:T(8,128)(2,1)}, u32[]{:S(2)}, u32[]{:S(2)}) collective-permute-start(bf16[4,24,3968]{2,1,0:T(8,128)(2,1)} %get-tuple-element.137), channel_id=1, source_target_pairs={{0,8},{4,12},{8,0},{12,4},{1,9},{5,13},{9,1},{13,5},{2,10},{6,14},... | collective-permute-start | bytes 2285576 | tf_op jit(solution)/shard_map/ppermute | solution.py:718
  202.7 46.8 %collective-permute-start.29 = (bf16[4,24,3968]{2,1,0:T(8,128)(2,1)}, bf16[4,24,3968]{2,1,0:T(8,128)(2,1)}, u32[]{:S(2)}, u32[]{:S(2)}) collective-permute-start(bf16[4,24,3968]{2,1,0:T(8,128)(2,1)} %get-tuple-element.138), channel_id=1, source_target_pairs={{0,12},{4,0},{8,4},{12,8},{1,13},{5,1},{9,5},{13,9},{2,14},{6,2},{... | collective-permute-start | bytes 2285576 | tf_op jit(solution)/shard_map/ppermute | solution.py:718
  207.5 36.5 %all-to-all-start.3 = ((bf16[4,4,4,24,768]{4,3,2,1,0:T(8,128)(2,1)}), bf16[4,4,4,24,768]{4,3,2,1,0:T(8,128)(2,1)S(1)}, u32[]{:S(2)}, u32[]{:S(2)}) async-start(bf16[4,4,4,24,768]{4,3,2,1,0:T(8,128)(2,1)} %sum_outer.1), calls=%async_computation.3 | async-start | bytes 4718592 | tf_op jit(solution)/shard_map/all_to_all | solution.py:751
  244.9 62.3 %all-to-all-start.4 = ((bf16[8,2,4,32,768]{4,3,2,1,0:T(8,128)(2,1)}), bf16[8,2,4,32,768]{4,3,2,1,0:T(8,128)(2,1)}, u32[]{:S(2)}, u32[]{:S(2)}) async-start(bf16[8,2,4,32,768]{4,3,2,1,0:T(8,128)(2,1)} %get-tuple-element.134), calls=%async_computation.4 | async-start | bytes 6291456 | tf_op jit(solution)/shard_map/all_to_all | solution.py:751
  255.3 30.3 %collective-permute-start.34 = (bf16[4,24,3200]{2,1,0:T(8,128)(2,1)S(1)}, bf16[4,24,3200]{2,1,0:T(8,128)(2,1)S(1)}, u32[]{:S(2)}, u32[]{:S(2)}) collective-permute-start(bf16[4,24,3200]{2,1,0:T(8,128)(2,1)S(1)} %get-tuple-element.150), channel_id=1, source_target_pairs={{0,4},{4,8},{8,12},{12,0},{1,5},{5,9},{9,13},{13,1},{2,6},{6,10},{... | collective-permute-start | bytes 1843208 | tf_op jit(solution)/shard_map/ppermute | solution.py:718
  255.4 33.5 %collective-permute-start.35 = (bf16[4,24,3200]{2,1,0:T(8,128)(2,1)S(1)}, bf16[4,24,3200]{2,1,0:T(8,128)(2,1)S(1)}, u32[]{:S(2)}, u32[]{:S(2)}) collective-permute-start(bf16[4,24,3200]{2,1,0:T(8,128)(2,1)S(1)} %get-tuple-element.151), channel_id=1, source_target_pairs={{0,8},{4,12},{8,0},{12,4},{1,9},{5,13},{9,1},{13,5},{2,10},{6,14},... | collective-permute-start | bytes 1843208 | tf_op jit(solution)/shard_map/ppermute | solution.py:718
  256.9 32.1 %collective-permute-start.36 = (bf16[4,24,3200]{2,1,0:T(8,128)(2,1)S(1)}, bf16[4,24,3200]{2,1,0:T(8,128)(2,1)S(1)}, u32[]{:S(2)}, u32[]{:S(2)}) collective-permute-start(bf16[4,24,3200]{2,1,0:T(8,128)(2,1)S(1)} %get-tuple-element.152), channel_id=1, source_target_pairs={{0,12},{4,0},{8,4},{12,8},{1,13},{5,1},{9,5},{13,9},{2,14},{6,2},{... | collective-permute-start | bytes 1843208 | tf_op jit(solution)/shard_map/ppermute | solution.py:718
  261.7 30.8 %collective-permute-start.31 = (bf16[4,8,3840]{2,1,0:T(8,128)(2,1)S(1)}, bf16[4,8,3840]{2,1,0:T(8,128)(2,1)S(1)}, u32[]{:S(2)}, u32[]{:S(2)}) collective-permute-start(bf16[4,8,3840]{2,1,0:T(8,128)(2,1)S(1)} %get-tuple-element.146), channel_id=1, source_target_pairs={{0,1},{1,2},{2,3},{3,0},{4,5},{5,6},{6,7},{7,4},{8,9},{9,10},{10,1... | collective-permute-start | bytes 737288 | tf_op jit(solution)/shard_map/ppermute | solution.py:718
  264.0 29.7 %collective-permute-start.32 = (bf16[4,8,3840]{2,1,0:T(8,128)(2,1)S(1)}, bf16[4,8,3840]{2,1,0:T(8,128)(2,1)S(1)}, u32[]{:S(2)}, u32[]{:S(2)}) collective-permute-start(bf16[4,8,3840]{2,1,0:T(8,128)(2,1)S(1)} %get-tuple-element.147), channel_id=1, source_target_pairs={{0,2},{1,3},{2,0},{3,1},{4,6},{5,7},{6,4},{7,5},{8,10},{9,11},{10,... | collective-permute-start | bytes 737288 | tf_op jit(solution)/shard_map/ppermute | solution.py:718
  (58 other events, 560.0 us)

commit v3 on v2

--- a/solution.py
+++ b/solution.py
@@ -598,8 +598,8 @@
         ],
         (ids, dealt, *weights, perm),
         "attention_forward",
-        22 * 10**9,
-        22 * 10**6,
+        8 * 10**9,
+        5 * 10**6,
         ATTENTION_SCRATCH + [pltpu.VMEM((32, PACKED - 3 * WIDTH), f32), pltpu.SemaphoreType.DMA((8,))],
         58,
     )
@@ -808,14 +808,14 @@
         split_ffn, "split_ffn", places, ffn_x, (RING, 24, MIXED), (RING, 48, WIDTH)
     )
     attn_x = arrivals(hold(attn_zy, dealt_x).reshape(96, PACKED), "x")
-    attn_pieces = both_cores(attn_x)
     inner_z = swap(inner_x, "z")
     outer_z = over(jnp.broadcast_to(outer_x[None], (RING, RING, 48, WIDTH)), "z")
-    inner_z = jnp.concatenate(in_half(inner_x, hold(inner_z, attn_x[1]), "z"), axis=1)
+    inner_z = jnp.concatenate(in_half(inner_x, inner_z, "z"), axis=1)
+    attn_pieces = both_cores([attn_x[0]] + [hold(p, inner_z) for p in attn_x[1:]])
     inner_far = shift(inner_z, "z", 2)
-    outer_z = hold(outer_z, attn_x[1])
+    outer_z = hold(outer_z, inner_z)
     outer_far = shift(outer_z, "y", 2)
-    dealt_c = over(hold(cotangent, attn_x[1]).reshape(dealt), dp)
+    dealt_c = over(hold(cotangent, inner_z).reshape(dealt), dp)
 
     x_t, qkv, expo, norm, ctx_t, vec, inner_bias, info = call_forward(
         places, dealt_x, attn_pieces, perm.reshape(32, 16)

time: 315 us -> 312 us (level)
  waiting for transfers between devices: 75.3 us -> 70.4 us
    ppermute x41, waiting for transfers between devices: 71.6 us -> 48.3 us  [shift(): lax.ppermute(value, axis, [(i, (i + step) % size) for i in range(size)])]
    all_to_all x5, waiting for transfers between devices: 3.69 us -> 13.4 us  [over(): return lax.all_to_all(value, axis, split_axis=0, concat_axis=0, tiled=True)]
    ppermute x2, waiting for transfers between devices: 0.01 us -> 8.68 us  [swap(): return lax.ppermute(value, axis, [(i, i ^ 1) for i in range(RING)])]
  transfers between devices with their start and end apart: 48 -> 48, of which waited for: 19 -> 20; matrix products, arithmetic and copies ran while one was open for 3% -> 3% of each run, Pallas kernels for 23% -> 23%
where the time goes in v3:
time: 312 us; the launch traced here: 310 us
  Pallas kernels  138 us (44%)
  starting transfers between devices  83.6 us (27%)
  waiting for transfers between devices  70.4 us (23%)
  local copies, waits for them, and re-layouts  12.7 us (4%)
  other arithmetic  3.97 us (1%)
    pallas_call x15, Pallas kernels, run(): pl.pallas_call(kernel, grid_spec=pltpu.PrefetchScalarGridSpec(num_scalar_...  138 us
    ppermute x41, starting transfers between devices, shift(): lax.ppermute(value, axis, [(i, (i + step) % size) for i in range(size)])  58.6 us
    ppermute x41, waiting for transfers between devices, shift(): lax.ppermute(value, axis, [(i, (i + step) % size) for i in range(size)])  48.3 us
    all_to_all x5, starting transfers between devices, over(): return lax.all_to_all(value, axis, split_axis=0, concat_axis=0, tiled=True)  21.3 us
    all_to_all x5, waiting for transfers between devices, over(): return lax.all_to_all(value, axis, split_axis=0, concat_axis=0, tiled=True)  13.4 us
    ppermute x2, waiting for transfers between devices, swap(): return lax.ppermute(value, axis, [(i, i ^ 1) for i in range(RING)])  8.68 us
  transfers between devices with their start and end apart: 48, of which 20 were waited for; matrix products, arithmetic and copies ran while one was open for 3% of the time, Pallas kernels for 23%

profile of v3, /device:TPU:0, one launch (start us, length us, event | category | flops | bytes accessed | tf_op | source)
XLA Modules:
  0.0 310.4 jit_solution(3360267042203054954)
XLA Ops:
  0.8 4.5 %all-to-all-start = ((bf16[8,4,32,768]{3,2,1,0:T(8,128)(2,1)}), bf16[8,4,32,768]{3,2,1,0:T(8,128)(2,1)S(1)}, u32[]{:S(2)}, u32[]{:S(2)}) async-start(bf16[8,4,32,768]{3,2,1,0:T(8,128)(2,1)} %bitcast.34), calls=%async_computation | async-start | bytes 3145728 | tf_op jit(solution)/shard_map/all_to_all | solution.py:751
  19.2 4.1 %collective-permute-start.5 = (bf16[24,2816]{1,0:T(8,128)(2,1)S(1)}, bf16[24,2816]{1,0:T(8,128)(2,1)S(1)}, u32[]{:S(2)}, u32[]{:S(2)}) collective-permute-start(bf16[24,2816]{1,0:T(8,128)(2,1)S(1)} %get-tuple-element.96.own), channel_id=1, source_target_pairs={{0,12},{4,0},{8,4},{12,8},{1,13},{5,1},{9,5},{13,9},{2,14},{6,2},{... | collective-permute-start | bytes 405512 | tf_op jit(solution)/shard_map/ppermute | solution.py:718
  23.3 3.7 %all-to-all-done.x_in = bf16[8,4,32,768]{3,2,1,0:T(8,128)(2,1)S(1)} async-done(((bf16[8,4,32,768]{3,2,1,0:T(8,128)(2,1)}), bf16[8,4,32,768]{3,2,1,0:T(8,128)(2,1)S(1)}, u32[]{:S(2)}, u32[]{:S(2)}) %all-to-all-start) | async-done | bytes 1572896 | tf_op jit(solution)/shard_map/all_to_all | solution.py:751
  29.7 3.9 %collective-permute-start.4 = (bf16[24,2816]{1,0:T(8,128)(2,1)S(1)}, bf16[24,2816]{1,0:T(8,128)(2,1)S(1)}, u32[]{:S(2)}, u32[]{:S(2)}) collective-permute-start(bf16[24,2816]{1,0:T(8,128)(2,1)S(1)} %get-tuple-element.96.own), channel_id=1, source_target_pairs={{0,8},{4,12},{8,0},{12,4},{1,9},{5,13},{9,1},{13,5},{2,10},{6,14},... | collective-permute-start | bytes 405512 | tf_op jit(solution)/shard_map/ppermute | solution.py:718
  34.6 3.4 %collective-permute-done.4.r2 = bf16[24,2816]{1,0:T(8,128)(2,1)S(1)} collective-permute-done((bf16[24,2816]{1,0:T(8,128)(2,1)S(1)}, bf16[24,2816]{1,0:T(8,128)(2,1)S(1)}, u32[]{:S(2)}, u32[]{:S(2)}) %collective-permute-start.4) | collective-permute-done | bytes 135200 | tf_op jit(solution)/shard_map/ppermute | solution.py:718
  49.3 4.9 %all-to-all-start.2 = ((bf16[4,4,48,768]{3,2,1,0:T(8,128)(2,1)}), bf16[4,4,48,768]{3,2,1,0:T(8,128)(2,1)S(1)}, u32[]{:S(2)}, u32[]{:S(2)}) async-start(bf16[4,4,48,768]{3,2,1,0:T(8,128)(2,1)} %broadcast_in_dim.10), calls=%async_computation.2 | async-start | bytes 2359296 | tf_op jit(solution)/shard_map/all_to_all | solution.py:751
  54.2 8.7 %collective-permute-done.12 = bf16[4,24,3840]{2,1,0:T(8,128)(2,1)} collective-permute-done((bf16[4,24,3840]{2,1,0:T(8,128)(2,1)S(1)}, bf16[4,24,3840]{2,1,0:T(8,128)(2,1)}, u32[]{:S(2)}, u32[]{:S(2)}) %collective-permute-start.12) | collective-permute-done | bytes 737312 | tf_op jit(solution)/shard_map/ppermute | solution.py:722
  65.3 3.9 %collective-permute-start.19 = (bf16[4,48,3840]{2,1,0:T(8,128)(2,1)}, bf16[4,48,3840]{2,1,0:T(8,128)(2,1)}, u32[]{:S(2)}, u32[]{:S(2)}) collective-permute-start(bf16[4,48,3840]{2,1,0:T(8,128)(2,1)} %pad_maximum_fusion.i0), channel_id=1, source_target_pairs={{0,8},{4,12},{8,0},{12,4},{1,9},{5,13},{9,1},{13,5},{2,10},{6,14},... | collective-permute-start | bytes 4423688 | tf_op jit(solution)/shard_map/ppermute | solution.py:718
  69.2 9.7 %all-to-all-done.2.j0 = bf16[4,4,48,768]{3,2,1,0:T(8,128)(2,1)S(1)} async-done(((bf16[4,4,48,768]{3,2,1,0:T(8,128)(2,1)}), bf16[4,4,48,768]{3,2,1,0:T(8,128)(2,1)S(1)}, u32[]{:S(2)}, u32[]{:S(2)}) %all-to-all-start.2) | async-done | bytes 1179680 | tf_op jit(solution)/shard_map/all_to_all | solution.py:751
  78.9 3.7 %all-to-all-start.1 = ((bf16[8,4,32,768]{3,2,1,0:T(8,128)(2,1)}), bf16[8,4,32,768]{3,2,1,0:T(8,128)(2,1)S(1)}, u32[]{:S(2)}, u32[]{:S(2)}) async-start(bf16[8,4,32,768]{3,2,1,0:T(8,128)(2,1)} %bitcast.7), calls=%async_computation.1 | async-start | bytes 3145728 | tf_op jit(solution)/shard_map/all_to_all | solution.py:751
  83.6 3.4 %collective-permute-start.22 = (bf16[4,4,48,768]{3,2,1,0:T(8,128)(2,1)S(1)}, bf16[4,4,48,768]{3,2,1,0:T(8,128)(2,1)}, u32[]{:S(2)}, u32[]{:S(2)}) collective-permute-start(bf16[4,4,48,768]{3,2,1,0:T(8,128)(2,1)S(1)} %all-to-all-done.2.j0), channel_id=1, source_target_pairs={{0,2},{1,3},{2,0},{3,1},{4,6},{5,7},{6,4},{7,5},{8,10},{9,11},{10,... | collective-permute-start | bytes 3538952 | tf_op jit(solution)/shard_map/ppermute | solution.py:718
  87.7 23.7 %attention_forward.1 = (bf16[768,1024]{1,0:T(8,128)(2,1)}, bf16[1024,2304]{1,0:T(8,128)(2,1)}, bf16[4,12,256,256]{3,2,1,0:T(8,128)(2,1)}, f32[4,16,256]{2,1,0:T(...) custom-call(s32[16]{0:T(128)} %copy-done.7, ...), custom_call_target="tpu_custom_call" | custom-call | flops 8000000000 | bytes 5000000 | tf_op jit(solution)/shard_map/attention_forward/pallas_call | solution.py:550
  114.8 3.4 %collective-permute-done.21.j1 = bf16[4,4,48,768]{3,2,1,0:T(8,128)(2,1)S(1)} collective-permute-done((bf16[4,4,48,768]{3,2,1,0:T(8,128)(2,1)S(1)}, bf16[4,4,48,768]{3,2,1,0:T(8,128)(2,1)S(1)}, u32[]{:S(2)}, u32[]{:S(2)}) %collective-permute-start.21) | collective-permute-done | bytes 1179680 | tf_op jit(solution)/shard_map/ppermute | solution.py:718
  122.5 65.8 %feed_forward.1 = (bf16[1024,768]{1,0:T(8,128)(2,1)}, f32[1024,768]{1,0:T(8,128)}, bf16[1024,768]{1,0:T(8,128)(2,1)}, bf16[4,384,768]{2,1,0:T(8,128)(2,1)}, bf16...) custom-call(s32[16]{0:T(128)} %pad_add_fusion.1.ids, ...), custom_call_target="tpu_custom_call" | custom-call | flops 49999998976 | bytes 40000000 | tf_op jit(solution)/shard_map/feed_forward/pallas_call | solution.py:550
  190.9 3.2 %collective-permute-done.24.refs_1_ = bf16[4,96,3072]{2,1,0:T(8,128)(2,1)S(1)} collective-permute-done((bf16[4,96,3072]{2,1,0:T(8,128)(2,1)}, bf16[4,96,3072]{2,1,0:T(8,128)(2,1)S(1)}, u32[]{:S(2)}, u32[]{:S(2)}) %collective-permute-start.24) | collective-permute-done | bytes 2359328 | tf_op jit(solution)/shard_map/ppermute | solution.py:718
  196.9 3.2 %sum_blocks.1 = (bf16[4,24,3968]{2,1,0:T(8,128)(2,1)S(1)}, bf16[4,24,3968]{2,1,0:T(8,128)(2,1)}, bf16[4,24,3968]{2,1,0:T(8,128)(2,1)}, bf16[4,24,3968]{2,1,0:T(8,128)(2,1)}) custom-call(s32[16]{0:T(128)S(1)} %copy-done.8, bf16[4,96,3072]{2,1,0:T(8,128)(2,1)S(1)} %copy-done.1, bf16[4,96,3072]{2,1,0:T(8,128)(2,1)S(1)} %collective-permute-done.24.refs_1_, ...), custom_call_target="tpu_custom_call" | custom-call | flops 1000000 | bytes 6000000 | tf_op jit(solution)/shard_map/sum_blocks/pallas_call | solution.py:550
  206.7 3.6 %all-to-all-start.3 = ((bf16[4,4,4,24,768]{4,3,2,1,0:T(8,128)(2,1)}), bf16[4,4,4,24,768]{4,3,2,1,0:T(8,128)(2,1)S(1)}, u32[]{:S(2)}, u32[]{:S(2)}) async-start(bf16[4,4,4,24,768]{4,3,2,1,0:T(8,128)(2,1)} %sum_outer.1), calls=%async_computation.3 | async-start | bytes 4718592 | tf_op jit(solution)/shard_map/all_to_all | solution.py:751
  210.4 32.1 %attention_backward.1 = (bf16[8,2,4,32,768]{4,3,2,1,0:T(8,128)(2,1)}, bf16[4,96,2432]{2,1,0:T(8,128)(2,1)}, bf16[4,96,2432]{2,1,0:T(8,128)(2,1)}) custom-call(s32[16]{0:T(128)} %pad_add_fusion.1.ids, f32[1024,768]{1,0:T(8,128)} %get-tuple-element.127.dsum, bf16[1024,768]{1,0:T(8,128)(2,1)} %get-tuple-element.128.dattn, ...), custom_call_target="tpu_custom_call" | custom-call | flops 28000000000 | bytes 30000000 | tf_op jit(solution)/shard_map/attention_backward/pallas_call | solution.py:550
  243.3 4.6 %all-to-all-start.4 = ((bf16[8,2,4,32,768]{4,3,2,1,0:T(8,128)(2,1)}), bf16[8,2,4,32,768]{4,3,2,1,0:T(8,128)(2,1)}, u32[]{:S(2)}, u32[]{:S(2)}) async-start(bf16[8,2,4,32,768]{4,3,2,1,0:T(8,128)(2,1)} %get-tuple-element.138), calls=%async_computation.4 | async-start | bytes 6291456 | tf_op jit(solution)/shard_map/all_to_all | solution.py:751
  248.5 4.0 %collective-permute-done.30.refs_2_ = bf16[4,96,2432]{2,1,0:T(8,128)(2,1)S(1)} collective-permute-done((bf16[4,96,2432]{2,1,0:T(8,128)(2,1)}, bf16[4,96,2432]{2,1,0:T(8,128)(2,1)S(1)}, u32[]{:S(2)}, u32[]{:S(2)}) %collective-permute-start.30) | collective-permute-done | bytes 1867808 | tf_op jit(solution)/shard_map/ppermute | solution.py:718
  267.5 4.1 %collective-permute-done.34.refs_1_ = bf16[4,24,3200]{2,1,0:T(8,128)(2,1)S(1)} collective-permute-done((bf16[4,24,3200]{2,1,0:T(8,128)(2,1)S(1)}, bf16[4,24,3200]{2,1,0:T(8,128)(2,1)S(1)}, u32[]{:S(2)}, u32[]{:S(2)}) %collective-permute-start.34) | collective-permute-done | bytes 614432 | tf_op jit(solution)/shard_map/ppermute | solution.py:718
  274.8 9.5 %collective-permute-done.35.refs_2_ = bf16[4,24,3200]{2,1,0:T(8,128)(2,1)S(1)} collective-permute-done((bf16[4,24,3200]{2,1,0:T(8,128)(2,1)S(1)}, bf16[4,24,3200]{2,1,0:T(8,128)(2,1)S(1)}, u32[]{:S(2)}, u32[]{:S(2)}) %collective-permute-start.35) | collective-permute-done | bytes 614432 | tf_op jit(solution)/shard_map/ppermute | solution.py:718
  293.3 3.5 %collective-permute-done.38.a2 = bf16[4,8,2304]{2,1,0:T(8,128)(2,1)S(1)} collective-permute-done((bf16[4,8,2304]{2,1,0:T(8,128)(2,1)S(1)}, bf16[4,8,2304]{2,1,0:T(8,128)(2,1)S(1)}, u32[]{:S(2)}, u32[]{:S(2)}) %collective-permute-start.38) | collective-permute-done | bytes 147488 | tf_op jit(solution)/shard_map/ppermute | solution.py:718
  303.9 3.8 %fusion = (bf16[8,1,4,32,768]{4,3,2,1,0:T(8,128)(2,1)}, bf16[8,1,4,32,768]{4,3,2,1,0:T(8,128)(2,1)}) fusion(bf16[8,2,4,32,768]{4,3,2,1,0:T(8,128)(2,1)} %all-to-all-done.4), kind=kLoop, calls=%fused_computation.19 | loop fusion | bytes 6291456 | tf_op jit(solution)/shard_map/slice | solution.py:882
  (173 shorter events, 90.7 us)
Async XLA Ops:
  0.8 26.1 %all-to-all-start = ((bf16[8,4,32,768]{3,2,1,0:T(8,128)(2,1)}), bf16[8,4,32,768]{3,2,1,0:T(8,128)(2,1)S(1)}, u32[]{:S(2)}, u32[]{:S(2)}) async-start(bf16[8,4,32,768]{3,2,1,0:T(8,128)(2,1)} %bitcast.34), calls=%async_computation | async-start | bytes 3145728 | tf_op jit(solution)/shard_map/all_to_all | solution.py:751
  19.2 14.4 %collective-permute-start.5 = (bf16[24,2816]{1,0:T(8,128)(2,1)S(1)}, bf16[24,2816]{1,0:T(8,128)(2,1)S(1)}, u32[]{:S(2)}, u32[]{:S(2)}) collective-permute-start(bf16[24,2816]{1,0:T(8,128)(2,1)S(1)} %get-tuple-element.96.own), channel_id=1, source_target_pairs={{0,12},{4,0},{8,4},{12,8},{1,13},{5,1},{9,5},{13,9},{2,14},{6,2},{... | collective-permute-start | bytes 405512 | tf_op jit(solution)/shard_map/ppermute | solution.py:718
  27.0 13.6 %collective-permute-start.11 = (bf16[24,5376]{1,0:T(8,128)(2,1)S(1)}, bf16[24,5376]{1,0:T(8,128)(2,1)S(1)}, u32[]{:S(2)}, u32[]{:S(2)}) collective-permute-start(bf16[24,5376]{1,0:T(8,128)(2,1)S(1)} %pad_maximum_fusion.1.p0), channel_id=1, source_target_pairs={{0,96},{32,0},{64,32},{96,64},{1,97},{33,1},{65,33},{97,65},{2,98}... | collective-permute-start | bytes 774152 | tf_op jit(solution)/shard_map/ppermute | solution.py:718
  43.3 19.5 %collective-permute-start.12 = (bf16[4,24,3840]{2,1,0:T(8,128)(2,1)S(1)}, bf16[4,24,3840]{2,1,0:T(8,128)(2,1)}, u32[]{:S(2)}, u32[]{:S(2)}) collective-permute-start(bf16[4,24,3840]{2,1,0:T(8,128)(2,1)S(1)} %get-tuple-element.101), channel_id=1, source_target_pairs={{0,4},{4,0},{8,12},{12,8},{1,5},{5,1},{9,13},{13,9},{2,6},{6,2},{1... | collective-permute-start | bytes 2211848 | tf_op jit(solution)/shard_map/ppermute | solution.py:722
  45.3 37.3 %collective-permute-start.16 = (bf16[96,2816]{1,0:T(8,128)(2,1)S(1)}, bf16[96,2816]{1,0:T(8,128)(2,1)}, u32[]{:S(2)}, u32[]{:S(2)}) collective-permute-start(bf16[96,2816]{1,0:T(8,128)(2,1)S(1)} %bitcast.28), channel_id=1, source_target_pairs={{0,96},{32,0},{64,32},{96,64},{1,97},{33,1},{65,33},{97,65},{2,98}... | collective-permute-start | bytes 1622024 | tf_op jit(solution)/shard_map/ppermute | solution.py:718
  45.9 36.7 %collective-permute-start.14 = (bf16[96,2816]{1,0:T(8,128)(2,1)S(1)}, bf16[96,2816]{1,0:T(8,128)(2,1)}, u32[]{:S(2)}, u32[]{:S(2)}) collective-permute-start(bf16[96,2816]{1,0:T(8,128)(2,1)S(1)} %bitcast.29), channel_id=1, source_target_pairs={{0,64},{32,96},{64,0},{96,32},{1,65},{33,97},{65,1},{97,33},{2,66}... | collective-permute-start | bytes 1622024 | tf_op jit(solution)/shard_map/ppermute | solution.py:718
  47.4 35.2 %collective-permute-start.7 = (bf16[96,2816]{1,0:T(8,128)(2,1)S(1)}, bf16[96,2816]{1,0:T(8,128)(2,1)}, u32[]{:S(2)}, u32[]{:S(2)}) collective-permute-start(bf16[96,2816]{1,0:T(8,128)(2,1)S(1)} %bitcast.30), channel_id=1, source_target_pairs={{0,32},{32,64},{64,96},{96,0},{1,33},{33,65},{65,97},{97,1},{2,34}... | collective-permute-start | bytes 1622024 | tf_op jit(solution)/shard_map/ppermute | solution.py:718
  49.3 29.6 %all-to-all-start.2 = ((bf16[4,4,48,768]{3,2,1,0:T(8,128)(2,1)}), bf16[4,4,48,768]{3,2,1,0:T(8,128)(2,1)S(1)}, u32[]{:S(2)}, u32[]{:S(2)}) async-start(bf16[4,4,48,768]{3,2,1,0:T(8,128)(2,1)} %broadcast_in_dim.10), calls=%async_computation.2 | async-start | bytes 2359296 | tf_op jit(solution)/shard_map/all_to_all | solution.py:751
  65.3 46.3 %collective-permute-start.19 = (bf16[4,48,3840]{2,1,0:T(8,128)(2,1)}, bf16[4,48,3840]{2,1,0:T(8,128)(2,1)}, u32[]{:S(2)}, u32[]{:S(2)}) collective-permute-start(bf16[4,48,3840]{2,1,0:T(8,128)(2,1)} %pad_maximum_fusion.i0), channel_id=1, source_target_pairs={{0,8},{4,12},{8,0},{12,4},{1,9},{5,13},{9,1},{13,5},{2,10},{6,14},... | collective-permute-start | bytes 4423688 | tf_op jit(solution)/shard_map/ppermute | solution.py:718
  69.2 14.4 %collective-permute-start.6 = (bf16[96,2816]{1,0:T(8,128)(2,1)S(1)}, bf16[96,2816]{1,0:T(8,128)(2,1)}, u32[]{:S(2)}, u32[]{:S(2)}) collective-permute-start(bf16[96,2816]{1,0:T(8,128)(2,1)S(1)} %bitcast.31), channel_id=1, source_target_pairs={{0,16},{16,0},{1,17},{17,1},{2,18},{18,2},{3,19},{19,3},{4,20},{20... | collective-permute-start | bytes 1622024 | tf_op jit(solution)/shard_map/ppermute | solution.py:718
  78.9 32.6 %all-to-all-start.1 = ((bf16[8,4,32,768]{3,2,1,0:T(8,128)(2,1)}), bf16[8,4,32,768]{3,2,1,0:T(8,128)(2,1)S(1)}, u32[]{:S(2)}, u32[]{:S(2)}) async-start(bf16[8,4,32,768]{3,2,1,0:T(8,128)(2,1)} %bitcast.7), calls=%async_computation.1 | async-start | bytes 3145728 | tf_op jit(solution)/shard_map/all_to_all | solution.py:751
  83.6 29.8 %collective-permute-start.22 = (bf16[4,4,48,768]{3,2,1,0:T(8,128)(2,1)S(1)}, bf16[4,4,48,768]{3,2,1,0:T(8,128)(2,1)}, u32[]{:S(2)}, u32[]{:S(2)}) collective-permute-start(bf16[4,4,48,768]{3,2,1,0:T(8,128)(2,1)S(1)} %all-to-all-done.2.j0), channel_id=1, source_target_pairs={{0,2},{1,3},{2,0},{3,1},{4,6},{5,7},{6,4},{7,5},{8,10},{9,11},{10,... | collective-permute-start | bytes 3538952 | tf_op jit(solution)/shard_map/ppermute | solution.py:718
  190.8 13.5 %collective-permute-start.26 = (bf16[4,384,768]{2,1,0:T(8,128)(2,1)}, bf16[4,384,768]{2,1,0:T(8,128)(2,1)S(1)}, u32[]{:S(2)}, u32[]{:S(2)}) collective-permute-start(bf16[4,384,768]{2,1,0:T(8,128)(2,1)} %get-tuple-element.126), channel_id=1, source_target_pairs={{0,16},{16,0},{1,17},{17,1},{2,18},{18,2},{3,19},{19,3},{4,20},{20... | collective-permute-start | bytes 7077896 | tf_op jit(solution)/shard_map/ppermute | solution.py:718
  201.0 46.9 %collective-permute-start.27 = (bf16[4,24,3968]{2,1,0:T(8,128)(2,1)}, bf16[4,24,3968]{2,1,0:T(8,128)(2,1)}, u32[]{:S(2)}, u32[]{:S(2)}) collective-permute-start(bf16[4,24,3968]{2,1,0:T(8,128)(2,1)} %get-tuple-element.140), channel_id=1, source_target_pairs={{0,4},{4,8},{8,12},{12,0},{1,5},{5,9},{9,13},{13,1},{2,6},{6,10},{... | collective-permute-start | bytes 2285576 | tf_op jit(solution)/shard_map/ppermute | solution.py:718
  201.0 46.9 %collective-permute-start.28 = (bf16[4,24,3968]{2,1,0:T(8,128)(2,1)}, bf16[4,24,3968]{2,1,0:T(8,128)(2,1)}, u32[]{:S(2)}, u32[]{:S(2)}) collective-permute-start(bf16[4,24,3968]{2,1,0:T(8,128)(2,1)} %get-tuple-element.141), channel_id=1, source_target_pairs={{0,8},{4,12},{8,0},{12,4},{1,9},{5,13},{9,1},{13,5},{2,10},{6,14},... | collective-permute-start | bytes 2285576 | tf_op jit(solution)/shard_map/ppermute | solution.py:718
  201.6 46.3 %collective-permute-start.29 = (bf16[4,24,3968]{2,1,0:T(8,128)(2,1)}, bf16[4,24,3968]{2,1,0:T(8,128)(2,1)}, u32[]{:S(2)}, u32[]{:S(2)}) collective-permute-start(bf16[4,24,3968]{2,1,0:T(8,128)(2,1)} %get-tuple-element.142), channel_id=1, source_target_pairs={{0,12},{4,0},{8,4},{12,8},{1,13},{5,1},{9,5},{13,9},{2,14},{6,2},{... | collective-permute-start | bytes 2285576 | tf_op jit(solution)/shard_map/ppermute | solution.py:718
  206.7 35.7 %all-to-all-start.3 = ((bf16[4,4,4,24,768]{4,3,2,1,0:T(8,128)(2,1)}), bf16[4,4,4,24,768]{4,3,2,1,0:T(8,128)(2,1)S(1)}, u32[]{:S(2)}, u32[]{:S(2)}) async-start(bf16[4,4,4,24,768]{4,3,2,1,0:T(8,128)(2,1)} %sum_outer.1), calls=%async_computation.3 | async-start | bytes 4718592 | tf_op jit(solution)/shard_map/all_to_all | solution.py:751
  243.3 60.6 %all-to-all-start.4 = ((bf16[8,2,4,32,768]{4,3,2,1,0:T(8,128)(2,1)}), bf16[8,2,4,32,768]{4,3,2,1,0:T(8,128)(2,1)}, u32[]{:S(2)}, u32[]{:S(2)}) async-start(bf16[8,2,4,32,768]{4,3,2,1,0:T(8,128)(2,1)} %get-tuple-element.138), calls=%async_computation.4 | async-start | bytes 6291456 | tf_op jit(solution)/shard_map/all_to_all | solution.py:751
  253.9 17.7 %collective-permute-start.34 = (bf16[4,24,3200]{2,1,0:T(8,128)(2,1)S(1)}, bf16[4,24,3200]{2,1,0:T(8,128)(2,1)S(1)}, u32[]{:S(2)}, u32[]{:S(2)}) collective-permute-start(bf16[4,24,3200]{2,1,0:T(8,128)(2,1)S(1)} %get-tuple-element.154), channel_id=1, source_target_pairs={{0,4},{4,8},{8,12},{12,0},{1,5},{5,9},{9,13},{13,1},{2,6},{6,10},{... | collective-permute-start | bytes 1843208 | tf_op jit(solution)/shard_map/ppermute | solution.py:718
  254.8 29.4 %collective-permute-start.35 = (bf16[4,24,3200]{2,1,0:T(8,128)(2,1)S(1)}, bf16[4,24,3200]{2,1,0:T(8,128)(2,1)S(1)}, u32[]{:S(2)}, u32[]{:S(2)}) collective-permute-start(bf16[4,24,3200]{2,1,0:T(8,128)(2,1)S(1)} %get-tuple-element.155), channel_id=1, source_target_pairs={{0,8},{4,12},{8,0},{12,4},{1,9},{5,13},{9,1},{13,5},{2,10},{6,14},... | collective-permute-start | bytes 1843208 | tf_op jit(solution)/shard_map/ppermute | solution.py:718
  257.0 27.9 %collective-permute-start.36 = (bf16[4,24,3200]{2,1,0:T(8,128)(2,1)S(1)}, bf16[4,24,3200]{2,1,0:T(8,128)(2,1)S(1)}, u32[]{:S(2)}, u32[]{:S(2)}) collective-permute-start(bf16[4,24,3200]{2,1,0:T(8,128)(2,1)S(1)} %get-tuple-element.156), channel_id=1, source_target_pairs={{0,12},{4,0},{8,4},{12,8},{1,13},{5,1},{9,5},{13,9},{2,14},{6,2},{... | collective-permute-start | bytes 1843208 | tf_op jit(solution)/shard_map/ppermute | solution.py:718
  262.6 28.2 %collective-permute-start.31 = (bf16[4,8,3840]{2,1,0:T(8,128)(2,1)S(1)}, bf16[4,8,3840]{2,1,0:T(8,128)(2,1)S(1)}, u32[]{:S(2)}, u32[]{:S(2)}) collective-permute-start(bf16[4,8,3840]{2,1,0:T(8,128)(2,1)S(1)} %get-tuple-element.150), channel_id=1, source_target_pairs={{0,1},{1,2},{2,3},{3,0},{4,5},{5,6},{6,7},{7,4},{8,9},{9,10},{10,1... | collective-permute-start | bytes 737288 | tf_op jit(solution)/shard_map/ppermute | solution.py:718
  264.8 27.4 %collective-permute-start.32 = (bf16[4,8,3840]{2,1,0:T(8,128)(2,1)S(1)}, bf16[4,8,3840]{2,1,0:T(8,128)(2,1)S(1)}, u32[]{:S(2)}, u32[]{:S(2)}) collective-permute-start(bf16[4,8,3840]{2,1,0:T(8,128)(2,1)S(1)} %get-tuple-element.151), channel_id=1, source_target_pairs={{0,2},{1,3},{2,0},{3,1},{4,6},{5,7},{6,4},{7,5},{8,10},{9,11},{10,... | collective-permute-start | bytes 737288 | tf_op jit(solution)/shard_map/ppermute | solution.py:718
  271.6 20.6 %collective-permute-start.33 = (bf16[4,8,3840]{2,1,0:T(8,128)(2,1)S(1)}, bf16[4,8,3840]{2,1,0:T(8,128)(2,1)S(1)}, u32[]{:S(2)}, u32[]{:S(2)}) collective-permute-start(bf16[4,8,3840]{2,1,0:T(8,128)(2,1)S(1)} %get-tuple-element.152), channel_id=1, source_target_pairs={{0,3},{1,0},{2,1},{3,2},{4,7},{5,4},{6,5},{7,6},{8,11},{9,8},{10,9... | collective-permute-start | bytes 737288 | tf_op jit(solution)/shard_map/ppermute | solution.py:718
  (58 other events, 523.5 us)

commit v4 on v3

--- a/solution.py
+++ b/solution.py
@@ -198,23 +198,28 @@
 ):
     s = pl.program_id(0)
 
-    @pl.when(s == 0)
-    def _():
-        vec_grad[...] = jnp.zeros_like(vec_grad)
-        bias_grad[...] = jnp.zeros_like(bias_grad)
-        copies = []
+    def weight_copies():
+        ins = []
+        outs = []
         for i, (piece, late) in enumerate(zip((i0, i1, i2, i3), (j0, j1, j2, j3))):
             c, z_half = half_of(ids, i)
             y_half = ids[12] // 2 if i // 2 == 0 else 1 - ids[12] // 2
             for d in range(RING):
                 x = lax.rem(ids[8] + RING - d, RING)
-                copies.append(pltpu.make_async_copy(piece.at[d], w_in.at[x, c, z_half], in_sems.at[i, d]))
+                ins.append(pltpu.make_async_copy(piece.at[d], w_in.at[x, c, z_half], in_sems.at[i, d]))
                 for n in range(RING):
                     target = w_out.at[x, c, n, y_half]
-                    copies.append(pltpu.make_async_copy(late.at[n, d], target, out_sems.at[i, d, n]))
-        for copy in copies:
+                    outs.append(pltpu.make_async_copy(late.at[n, d], target, out_sems.at[i, d, n]))
+        return ins, outs
+
+    @pl.when(s == 0)
+    def _():
+        vec_grad[...] = jnp.zeros_like(vec_grad)
+        bias_grad[...] = jnp.zeros_like(bias_grad)
+        ins, outs = weight_copies()
+        for copy in ins + outs:
             copy.start()
-        for copy in copies:
+        for copy in ins:
             copy.wait()
 
     def inner_columns(n):
@@ -232,6 +237,12 @@
         hidden = zhat1 * vec[3:4] + vec[4:5]
         hid_low = hidden.astype(bf16)
         hid_t[s] = hid_low.T
+
+        @pl.when(s == 0)
+        def _():
+            for copy in weight_copies()[1]:
+                copy.wait()
+
         branch = jnp.broadcast_to(vec[5:6], (SLOT, WIDTH))
         for n in range(FF_STEPS):
             cols = slice(n * FF_STEP, (n + 1) * FF_STEP)
@@ -812,8 +823,7 @@
     outer_z = over(jnp.broadcast_to(outer_x[None], (RING, RING, 48, WIDTH)), "z")
     inner_z = jnp.concatenate(in_half(inner_x, inner_z, "z"), axis=1)
     attn_pieces = both_cores([attn_x[0]] + [hold(p, inner_z) for p in attn_x[1:]])
-    inner_far = shift(inner_z, "z", 2)
-    outer_z = hold(outer_z, inner_z)
+    inner_far = shift(hold(inner_z, outer_z), "z", 2)
     outer_far = shift(outer_z, "y", 2)
     dealt_c = over(hold(cotangent, inner_z).reshape(dealt), dp)
 

time: 312 us -> 317 us (1.016)
  waiting for transfers between devices: 70.4 us -> 79.8 us
  starting transfers between devices: 83.6 us -> 77.9 us
    ppermute x41, waiting for transfers between devices: 48.3 us -> 54.8 us  [shift(): lax.ppermute(value, axis, [(i, (i + step) % size) for i in range(size)])]
    ppermute x41, starting transfers between devices: 58.6 us -> 53 us  [shift(): lax.ppermute(value, axis, [(i, (i + step) % size) for i in range(size)])]
  transfers between devices with their start and end apart: 48 -> 48, of which waited for: 20 -> 19; matrix products, arithmetic and copies ran while one was open for 3% -> 3% of each run, Pallas kernels for 23% -> 22%
where the time goes in v4:
time: 317 us; the launch traced here: 315 us
  Pallas kernels  139 us (44%)
  waiting for transfers between devices  79.8 us (25%)
  starting transfers between devices  77.9 us (25%)
  local copies, waits for them, and re-layouts  12.7 us (4%)
  other arithmetic  3.96 us (1%)
    pallas_call x15, Pallas kernels, run(): pl.pallas_call(kernel, grid_spec=pltpu.PrefetchScalarGridSpec(num_scalar_...  139 us
    ppermute x41, waiting for transfers between devices, shift(): lax.ppermute(value, axis, [(i, (i + step) % size) for i in range(size)])  54.8 us
    ppermute x41, starting transfers between devices, shift(): lax.ppermute(value, axis, [(i, (i + step) % size) for i in range(size)])  53 us
    all_to_all x5, starting transfers between devices, over(): return lax.all_to_all(value, axis, split_axis=0, concat_axis=0, tiled=True)  21.3 us
    all_to_all x5, waiting for transfers between devices, over(): return lax.all_to_all(value, axis, split_axis=0, concat_axis=0, tiled=True)  16.3 us
    ppermute x2, waiting for transfers between devices, swap(): return lax.ppermute(value, axis, [(i, i ^ 1) for i in range(RING)])  8.68 us
  transfers between devices with their start and end apart: 48, of which 19 were waited for; matrix products, arithmetic and copies ran while one was open for 3% of the time, Pallas kernels for 22%

profile of v4, /device:TPU:0, one launch (start us, length us, event | category | flops | bytes accessed | tf_op | source)
XLA Modules:
  0.0 315.3 jit_solution(8326534008596846765)
XLA Ops:
  0.8 4.5 %all-to-all-start = ((bf16[8,4,32,768]{3,2,1,0:T(8,128)(2,1)}), bf16[8,4,32,768]{3,2,1,0:T(8,128)(2,1)S(1)}, u32[]{:S(2)}, u32[]{:S(2)}) async-start(bf16[8,4,32,768]{3,2,1,0:T(8,128)(2,1)} %bitcast.34), calls=%async_computation | async-start | bytes 3145728 | tf_op jit(solution)/shard_map/all_to_all | solution.py:762
  19.2 4.1 %collective-permute-start.5 = (bf16[24,2816]{1,0:T(8,128)(2,1)S(1)}, bf16[24,2816]{1,0:T(8,128)(2,1)S(1)}, u32[]{:S(2)}, u32[]{:S(2)}) collective-permute-start(bf16[24,2816]{1,0:T(8,128)(2,1)S(1)} %get-tuple-element.96.own), channel_id=1, source_target_pairs={{0,12},{4,0},{8,4},{12,8},{1,13},{5,1},{9,5},{13,9},{2,14},{6,2},{... | collective-permute-start | bytes 405512 | tf_op jit(solution)/shard_map/ppermute | solution.py:729
  23.3 3.7 %all-to-all-done.x_in = bf16[8,4,32,768]{3,2,1,0:T(8,128)(2,1)S(1)} async-done(((bf16[8,4,32,768]{3,2,1,0:T(8,128)(2,1)}), bf16[8,4,32,768]{3,2,1,0:T(8,128)(2,1)S(1)}, u32[]{:S(2)}, u32[]{:S(2)}) %all-to-all-start) | async-done | bytes 1572896 | tf_op jit(solution)/shard_map/all_to_all | solution.py:762
  29.7 3.9 %collective-permute-start.4 = (bf16[24,2816]{1,0:T(8,128)(2,1)S(1)}, bf16[24,2816]{1,0:T(8,128)(2,1)S(1)}, u32[]{:S(2)}, u32[]{:S(2)}) collective-permute-start(bf16[24,2816]{1,0:T(8,128)(2,1)S(1)} %get-tuple-element.96.own), channel_id=1, source_target_pairs={{0,8},{4,12},{8,0},{12,4},{1,9},{5,13},{9,1},{13,5},{2,10},{6,14},... | collective-permute-start | bytes 405512 | tf_op jit(solution)/shard_map/ppermute | solution.py:729
  34.6 3.4 %collective-permute-done.4.r2 = bf16[24,2816]{1,0:T(8,128)(2,1)S(1)} collective-permute-done((bf16[24,2816]{1,0:T(8,128)(2,1)S(1)}, bf16[24,2816]{1,0:T(8,128)(2,1)S(1)}, u32[]{:S(2)}, u32[]{:S(2)}) %collective-permute-start.4) | collective-permute-done | bytes 135200 | tf_op jit(solution)/shard_map/ppermute | solution.py:729
  49.3 4.9 %all-to-all-start.2 = ((bf16[4,4,48,768]{3,2,1,0:T(8,128)(2,1)}), bf16[4,4,48,768]{3,2,1,0:T(8,128)(2,1)S(1)}, u32[]{:S(2)}, u32[]{:S(2)}) async-start(bf16[4,4,48,768]{3,2,1,0:T(8,128)(2,1)} %broadcast_in_dim.10), calls=%async_computation.2 | async-start | bytes 2359296 | tf_op jit(solution)/shard_map/all_to_all | solution.py:762
  54.2 8.7 %collective-permute-done.12 = bf16[4,24,3840]{2,1,0:T(8,128)(2,1)} collective-permute-done((bf16[4,24,3840]{2,1,0:T(8,128)(2,1)S(1)}, bf16[4,24,3840]{2,1,0:T(8,128)(2,1)}, u32[]{:S(2)}, u32[]{:S(2)}) %collective-permute-start.12) | collective-permute-done | bytes 737312 | tf_op jit(solution)/shard_map/ppermute | solution.py:733
  65.3 12.6 %all-to-all-done.2.j0 = bf16[4,4,48,768]{3,2,1,0:T(8,128)(2,1)S(1)} async-done(((bf16[4,4,48,768]{3,2,1,0:T(8,128)(2,1)}), bf16[4,4,48,768]{3,2,1,0:T(8,128)(2,1)S(1)}, u32[]{:S(2)}, u32[]{:S(2)}) %all-to-all-start.2) | async-done | bytes 1179680 | tf_op jit(solution)/shard_map/all_to_all | solution.py:762
  78.1 3.7 %all-to-all-start.1 = ((bf16[8,4,32,768]{3,2,1,0:T(8,128)(2,1)}), bf16[8,4,32,768]{3,2,1,0:T(8,128)(2,1)S(1)}, u32[]{:S(2)}, u32[]{:S(2)}) async-start(bf16[8,4,32,768]{3,2,1,0:T(8,128)(2,1)} %bitcast.7), calls=%async_computation.1 | async-start | bytes 3145728 | tf_op jit(solution)/shard_map/all_to_all | solution.py:762
  82.8 3.4 %collective-permute-start.22 = (bf16[4,4,48,768]{3,2,1,0:T(8,128)(2,1)S(1)}, bf16[4,4,48,768]{3,2,1,0:T(8,128)(2,1)}, u32[]{:S(2)}, u32[]{:S(2)}) collective-permute-start(bf16[4,4,48,768]{3,2,1,0:T(8,128)(2,1)S(1)} %all-to-all-done.2.j0), channel_id=1, source_target_pairs={{0,2},{1,3},{2,0},{3,1},{4,6},{5,7},{6,4},{7,5},{8,10},{9,11},{10,... | collective-permute-start | bytes 3538952 | tf_op jit(solution)/shard_map/ppermute | solution.py:729
  86.9 23.7 %attention_forward.1 = (bf16[768,1024]{1,0:T(8,128)(2,1)}, bf16[1024,2304]{1,0:T(8,128)(2,1)}, bf16[4,12,256,256]{3,2,1,0:T(8,128)(2,1)}, f32[4,16,256]{2,1,0:T(...) custom-call(s32[16]{0:T(128)} %copy-done.7, ...), custom_call_target="tpu_custom_call" | custom-call | flops 8000000000 | bytes 5000000 | tf_op jit(solution)/shard_map/attention_forward/pallas_call | solution.py:561
  115.1 4.3 %collective-permute-done.21.j1 = bf16[4,4,48,768]{3,2,1,0:T(8,128)(2,1)S(1)} collective-permute-done((bf16[4,4,48,768]{3,2,1,0:T(8,128)(2,1)S(1)}, bf16[4,4,48,768]{3,2,1,0:T(8,128)(2,1)S(1)}, u32[]{:S(2)}, u32[]{:S(2)}) %collective-permute-start.21) | collective-permute-done | bytes 1179680 | tf_op jit(solution)/shard_map/ppermute | solution.py:729
  122.0 66.9 %feed_forward.1 = (bf16[1024,768]{1,0:T(8,128)(2,1)}, f32[1024,768]{1,0:T(8,128)}, bf16[1024,768]{1,0:T(8,128)(2,1)}, bf16[4,384,768]{2,1,0:T(8,128)(2,1)}, bf16...) custom-call(s32[16]{0:T(128)} %pad_add_fusion.1.ids, ...), custom_call_target="tpu_custom_call" | custom-call | flops 49999998976 | bytes 40000000 | tf_op jit(solution)/shard_map/feed_forward/pallas_call | solution.py:561
  191.5 3.2 %collective-permute-done.24.refs_1_ = bf16[4,96,3072]{2,1,0:T(8,128)(2,1)S(1)} collective-permute-done((bf16[4,96,3072]{2,1,0:T(8,128)(2,1)}, bf16[4,96,3072]{2,1,0:T(8,128)(2,1)S(1)}, u32[]{:S(2)}, u32[]{:S(2)}) %collective-permute-start.24) | collective-permute-done | bytes 2359328 | tf_op jit(solution)/shard_map/ppermute | solution.py:729
  197.5 3.2 %sum_blocks.1 = (bf16[4,24,3968]{2,1,0:T(8,128)(2,1)S(1)}, bf16[4,24,3968]{2,1,0:T(8,128)(2,1)}, bf16[4,24,3968]{2,1,0:T(8,128)(2,1)}, bf16[4,24,3968]{2,1,0:T(8,128)(2,1)}) custom-call(s32[16]{0:T(128)S(1)} %copy-done.8, bf16[4,96,3072]{2,1,0:T(8,128)(2,1)S(1)} %copy-done.1, bf16[4,96,3072]{2,1,0:T(8,128)(2,1)S(1)} %collective-permute-done.24.refs_1_, ...), custom_call_target="tpu_custom_call" | custom-call | flops 1000000 | bytes 6000000 | tf_op jit(solution)/shard_map/sum_blocks/pallas_call | solution.py:561
  201.6 3.6 %collective-permute-start.28 = (bf16[4,24,3968]{2,1,0:T(8,128)(2,1)}, bf16[4,24,3968]{2,1,0:T(8,128)(2,1)}, u32[]{:S(2)}, u32[]{:S(2)}) collective-permute-start(bf16[4,24,3968]{2,1,0:T(8,128)(2,1)} %get-tuple-element.141), channel_id=1, source_target_pairs={{0,8},{4,12},{8,0},{12,4},{1,9},{5,13},{9,1},{13,5},{2,10},{6,14},... | collective-permute-start | bytes 2285576 | tf_op jit(solution)/shard_map/ppermute | solution.py:729
  209.9 3.6 %all-to-all-start.3 = ((bf16[4,4,4,24,768]{4,3,2,1,0:T(8,128)(2,1)}), bf16[4,4,4,24,768]{4,3,2,1,0:T(8,128)(2,1)S(1)}, u32[]{:S(2)}, u32[]{:S(2)}) async-start(bf16[4,4,4,24,768]{4,3,2,1,0:T(8,128)(2,1)} %sum_outer.1), calls=%async_computation.3 | async-start | bytes 4718592 | tf_op jit(solution)/shard_map/all_to_all | solution.py:762
  213.5 32.1 %attention_backward.1 = (bf16[8,2,4,32,768]{4,3,2,1,0:T(8,128)(2,1)}, bf16[4,96,2432]{2,1,0:T(8,128)(2,1)}, bf16[4,96,2432]{2,1,0:T(8,128)(2,1)}) custom-call(s32[16]{0:T(128)} %pad_add_fusion.1.ids, f32[1024,768]{1,0:T(8,128)} %get-tuple-element.127.dsum, bf16[1024,768]{1,0:T(8,128)(2,1)} %get-tuple-element.128.dattn, ...), custom_call_target="tpu_custom_call" | custom-call | flops 28000000000 | bytes 30000000 | tf_op jit(solution)/shard_map/attention_backward/pallas_call | solution.py:561
  246.5 4.6 %all-to-all-start.4 = ((bf16[8,2,4,32,768]{4,3,2,1,0:T(8,128)(2,1)}), bf16[8,2,4,32,768]{4,3,2,1,0:T(8,128)(2,1)}, u32[]{:S(2)}, u32[]{:S(2)}) async-start(bf16[8,2,4,32,768]{4,3,2,1,0:T(8,128)(2,1)} %get-tuple-element.138), calls=%async_computation.4 | async-start | bytes 6291456 | tf_op jit(solution)/shard_map/all_to_all | solution.py:762
  251.6 4.0 %collective-permute-done.30.refs_2_ = bf16[4,96,2432]{2,1,0:T(8,128)(2,1)S(1)} collective-permute-done((bf16[4,96,2432]{2,1,0:T(8,128)(2,1)}, bf16[4,96,2432]{2,1,0:T(8,128)(2,1)S(1)}, u32[]{:S(2)}, u32[]{:S(2)}) %collective-permute-start.30) | collective-permute-done | bytes 1867808 | tf_op jit(solution)/shard_map/ppermute | solution.py:729
  268.8 18.6 %collective-permute-done.34.refs_1_ = bf16[4,24,3200]{2,1,0:T(8,128)(2,1)S(1)} collective-permute-done((bf16[4,24,3200]{2,1,0:T(8,128)(2,1)S(1)}, bf16[4,24,3200]{2,1,0:T(8,128)(2,1)S(1)}, u32[]{:S(2)}, u32[]{:S(2)}) %collective-permute-start.34) | collective-permute-done | bytes 614432 | tf_op jit(solution)/shard_map/ppermute | solution.py:729
  287.4 3.2 %collective-permute-start.33 = (bf16[4,8,3840]{2,1,0:T(8,128)(2,1)S(1)}, bf16[4,8,3840]{2,1,0:T(8,128)(2,1)S(1)}, u32[]{:S(2)}, u32[]{:S(2)}) collective-permute-start(bf16[4,8,3840]{2,1,0:T(8,128)(2,1)S(1)} %get-tuple-element.152), channel_id=1, source_target_pairs={{0,3},{1,0},{2,1},{3,2},{4,7},{5,4},{6,5},{7,6},{8,11},{9,8},{10,9... | collective-permute-start | bytes 737288 | tf_op jit(solution)/shard_map/ppermute | solution.py:729
  295.3 4.3 %collective-permute-done.33.i3 = bf16[4,8,3840]{2,1,0:T(8,128)(2,1)S(1)} collective-permute-done((bf16[4,8,3840]{2,1,0:T(8,128)(2,1)S(1)}, bf16[4,8,3840]{2,1,0:T(8,128)(2,1)S(1)}, u32[]{:S(2)}, u32[]{:S(2)}) %collective-permute-start.33) | collective-permute-done | bytes 245792 | tf_op jit(solution)/shard_map/ppermute | solution.py:729
  308.8 3.8 %fusion = (bf16[8,1,4,32,768]{4,3,2,1,0:T(8,128)(2,1)}, bf16[8,1,4,32,768]{4,3,2,1,0:T(8,128)(2,1)}) fusion(bf16[8,2,4,32,768]{4,3,2,1,0:T(8,128)(2,1)} %all-to-all-done.4), kind=kLoop, calls=%fused_computation.19 | loop fusion | bytes 6291456 | tf_op jit(solution)/shard_map/slice | solution.py:892
  (173 shorter events, 81.9 us)
Async XLA Ops:
  0.8 26.1 %all-to-all-start = ((bf16[8,4,32,768]{3,2,1,0:T(8,128)(2,1)}), bf16[8,4,32,768]{3,2,1,0:T(8,128)(2,1)S(1)}, u32[]{:S(2)}, u32[]{:S(2)}) async-start(bf16[8,4,32,768]{3,2,1,0:T(8,128)(2,1)} %bitcast.34), calls=%async_computation | async-start | bytes 3145728 | tf_op jit(solution)/shard_map/all_to_all | solution.py:762
  19.2 14.4 %collective-permute-start.5 = (bf16[24,2816]{1,0:T(8,128)(2,1)S(1)}, bf16[24,2816]{1,0:T(8,128)(2,1)S(1)}, u32[]{:S(2)}, u32[]{:S(2)}) collective-permute-start(bf16[24,2816]{1,0:T(8,128)(2,1)S(1)} %get-tuple-element.96.own), channel_id=1, source_target_pairs={{0,12},{4,0},{8,4},{12,8},{1,13},{5,1},{9,5},{13,9},{2,14},{6,2},{... | collective-permute-start | bytes 405512 | tf_op jit(solution)/shard_map/ppermute | solution.py:729
  27.0 13.6 %collective-permute-start.11 = (bf16[24,5376]{1,0:T(8,128)(2,1)S(1)}, bf16[24,5376]{1,0:T(8,128)(2,1)S(1)}, u32[]{:S(2)}, u32[]{:S(2)}) collective-permute-start(bf16[24,5376]{1,0:T(8,128)(2,1)S(1)} %pad_maximum_fusion.1.p0), channel_id=1, source_target_pairs={{0,96},{32,0},{64,32},{96,64},{1,97},{33,1},{65,33},{97,65},{2,98}... | collective-permute-start | bytes 774152 | tf_op jit(solution)/shard_map/ppermute | solution.py:729
  28.2 12.4 %collective-permute-start.10 = (bf16[24,5376]{1,0:T(8,128)(2,1)S(1)}, bf16[24,5376]{1,0:T(8,128)(2,1)S(1)}, u32[]{:S(2)}, u32[]{:S(2)}) collective-permute-start(bf16[24,5376]{1,0:T(8,128)(2,1)S(1)} %pad_maximum_fusion.1.p0), channel_id=1, source_target_pairs={{0,64},{32,96},{64,0},{96,32},{1,65},{33,97},{65,1},{97,33},{2,66}... | collective-permute-start | bytes 774152 | tf_op jit(solution)/shard_map/ppermute | solution.py:729
  29.7 13.1 %collective-permute-start.9 = (bf16[24,5376]{1,0:T(8,128)(2,1)S(1)}, bf16[24,5376]{1,0:T(8,128)(2,1)S(1)}, u32[]{:S(2)}, u32[]{:S(2)}) collective-permute-start(bf16[24,5376]{1,0:T(8,128)(2,1)S(1)} %pad_maximum_fusion.1.p0), channel_id=1, source_target_pairs={{0,32},{32,64},{64,96},{96,0},{1,33},{33,65},{65,97},{97,1},{2,34}... | collective-permute-start | bytes 774152 | tf_op jit(solution)/shard_map/ppermute | solution.py:729
  43.3 19.5 %collective-permute-start.12 = (bf16[4,24,3840]{2,1,0:T(8,128)(2,1)S(1)}, bf16[4,24,3840]{2,1,0:T(8,128)(2,1)}, u32[]{:S(2)}, u32[]{:S(2)}) collective-permute-start(bf16[4,24,3840]{2,1,0:T(8,128)(2,1)S(1)} %get-tuple-element.101), channel_id=1, source_target_pairs={{0,4},{4,0},{8,12},{12,8},{1,5},{5,1},{9,13},{13,9},{2,6},{6,2},{1... | collective-permute-start | bytes 2211848 | tf_op jit(solution)/shard_map/ppermute | solution.py:733
  45.3 36.5 %collective-permute-start.16 = (bf16[96,2816]{1,0:T(8,128)(2,1)S(1)}, bf16[96,2816]{1,0:T(8,128)(2,1)}, u32[]{:S(2)}, u32[]{:S(2)}) collective-permute-start(bf16[96,2816]{1,0:T(8,128)(2,1)S(1)} %bitcast.28), channel_id=1, source_target_pairs={{0,96},{32,0},{64,32},{96,64},{1,97},{33,1},{65,33},{97,65},{2,98}... | collective-permute-start | bytes 1622024 | tf_op jit(solution)/shard_map/ppermute | solution.py:729
  45.9 35.9 %collective-permute-start.14 = (bf16[96,2816]{1,0:T(8,128)(2,1)S(1)}, bf16[96,2816]{1,0:T(8,128)(2,1)}, u32[]{:S(2)}, u32[]{:S(2)}) collective-permute-start(bf16[96,2816]{1,0:T(8,128)(2,1)S(1)} %bitcast.29), channel_id=1, source_target_pairs={{0,64},{32,96},{64,0},{96,32},{1,65},{33,97},{65,1},{97,33},{2,66}... | collective-permute-start | bytes 1622024 | tf_op jit(solution)/shard_map/ppermute | solution.py:729
  47.4 34.4 %collective-permute-start.7 = (bf16[96,2816]{1,0:T(8,128)(2,1)S(1)}, bf16[96,2816]{1,0:T(8,128)(2,1)}, u32[]{:S(2)}, u32[]{:S(2)}) collective-permute-start(bf16[96,2816]{1,0:T(8,128)(2,1)S(1)} %bitcast.30), channel_id=1, source_target_pairs={{0,32},{32,64},{64,96},{96,0},{1,33},{33,65},{65,97},{97,1},{2,34}... | collective-permute-start | bytes 1622024 | tf_op jit(solution)/shard_map/ppermute | solution.py:729
  49.3 28.6 %all-to-all-start.2 = ((bf16[4,4,48,768]{3,2,1,0:T(8,128)(2,1)}), bf16[4,4,48,768]{3,2,1,0:T(8,128)(2,1)S(1)}, u32[]{:S(2)}, u32[]{:S(2)}) async-start(bf16[4,4,48,768]{3,2,1,0:T(8,128)(2,1)} %broadcast_in_dim.10), calls=%async_computation.2 | async-start | bytes 2359296 | tf_op jit(solution)/shard_map/all_to_all | solution.py:762
  78.0 35.2 %collective-permute-start.19 = (bf16[4,48,3840]{2,1,0:T(8,128)(2,1)}, bf16[4,48,3840]{2,1,0:T(8,128)(2,1)}, u32[]{:S(2)}, u32[]{:S(2)}) collective-permute-start(bf16[4,48,3840]{2,1,0:T(8,128)(2,1)} %pad_maximum_fusion.i0), channel_id=1, source_target_pairs={{0,8},{4,12},{8,0},{12,4},{1,9},{5,13},{9,1},{13,5},{2,10},{6,14},... | collective-permute-start | bytes 4423688 | tf_op jit(solution)/shard_map/ppermute | solution.py:729
  78.1 32.6 %all-to-all-start.1 = ((bf16[8,4,32,768]{3,2,1,0:T(8,128)(2,1)}), bf16[8,4,32,768]{3,2,1,0:T(8,128)(2,1)S(1)}, u32[]{:S(2)}, u32[]{:S(2)}) async-start(bf16[8,4,32,768]{3,2,1,0:T(8,128)(2,1)} %bitcast.7), calls=%async_computation.1 | async-start | bytes 3145728 | tf_op jit(solution)/shard_map/all_to_all | solution.py:762
  82.8 30.8 %collective-permute-start.22 = (bf16[4,4,48,768]{3,2,1,0:T(8,128)(2,1)S(1)}, bf16[4,4,48,768]{3,2,1,0:T(8,128)(2,1)}, u32[]{:S(2)}, u32[]{:S(2)}) collective-permute-start(bf16[4,4,48,768]{3,2,1,0:T(8,128)(2,1)S(1)} %all-to-all-done.2.j0), channel_id=1, source_target_pairs={{0,2},{1,3},{2,0},{3,1},{4,6},{5,7},{6,4},{7,5},{8,10},{9,11},{10,... | collective-permute-start | bytes 3538952 | tf_op jit(solution)/shard_map/ppermute | solution.py:729
  191.3 16.1 %collective-permute-start.26 = (bf16[4,384,768]{2,1,0:T(8,128)(2,1)}, bf16[4,384,768]{2,1,0:T(8,128)(2,1)S(1)}, u32[]{:S(2)}, u32[]{:S(2)}) collective-permute-start(bf16[4,384,768]{2,1,0:T(8,128)(2,1)} %get-tuple-element.126), channel_id=1, source_target_pairs={{0,16},{16,0},{1,17},{17,1},{2,18},{18,2},{3,19},{19,3},{4,20},{20... | collective-permute-start | bytes 7077896 | tf_op jit(solution)/shard_map/ppermute | solution.py:729
  201.6 49.5 %collective-permute-start.27 = (bf16[4,24,3968]{2,1,0:T(8,128)(2,1)}, bf16[4,24,3968]{2,1,0:T(8,128)(2,1)}, u32[]{:S(2)}, u32[]{:S(2)}) collective-permute-start(bf16[4,24,3968]{2,1,0:T(8,128)(2,1)} %get-tuple-element.140), channel_id=1, source_target_pairs={{0,4},{4,8},{8,12},{12,0},{1,5},{5,9},{9,13},{13,1},{2,6},{6,10},{... | collective-permute-start | bytes 2285576 | tf_op jit(solution)/shard_map/ppermute | solution.py:729
  201.6 49.5 %collective-permute-start.28 = (bf16[4,24,3968]{2,1,0:T(8,128)(2,1)}, bf16[4,24,3968]{2,1,0:T(8,128)(2,1)}, u32[]{:S(2)}, u32[]{:S(2)}) collective-permute-start(bf16[4,24,3968]{2,1,0:T(8,128)(2,1)} %get-tuple-element.141), channel_id=1, source_target_pairs={{0,8},{4,12},{8,0},{12,4},{1,9},{5,13},{9,1},{13,5},{2,10},{6,14},... | collective-permute-start | bytes 2285576 | tf_op jit(solution)/shard_map/ppermute | solution.py:729
  205.2 45.9 %collective-permute-start.29 = (bf16[4,24,3968]{2,1,0:T(8,128)(2,1)}, bf16[4,24,3968]{2,1,0:T(8,128)(2,1)}, u32[]{:S(2)}, u32[]{:S(2)}) collective-permute-start(bf16[4,24,3968]{2,1,0:T(8,128)(2,1)} %get-tuple-element.142), channel_id=1, source_target_pairs={{0,12},{4,0},{8,4},{12,8},{1,13},{5,1},{9,5},{13,9},{2,14},{6,2},{... | collective-permute-start | bytes 2285576 | tf_op jit(solution)/shard_map/ppermute | solution.py:729
  209.9 35.7 %all-to-all-start.3 = ((bf16[4,4,4,24,768]{4,3,2,1,0:T(8,128)(2,1)}), bf16[4,4,4,24,768]{4,3,2,1,0:T(8,128)(2,1)S(1)}, u32[]{:S(2)}, u32[]{:S(2)}) async-start(bf16[4,4,4,24,768]{4,3,2,1,0:T(8,128)(2,1)} %sum_outer.1), calls=%async_computation.3 | async-start | bytes 4718592 | tf_op jit(solution)/shard_map/all_to_all | solution.py:762
  246.5 62.4 %all-to-all-start.4 = ((bf16[8,2,4,32,768]{4,3,2,1,0:T(8,128)(2,1)}), bf16[8,2,4,32,768]{4,3,2,1,0:T(8,128)(2,1)}, u32[]{:S(2)}, u32[]{:S(2)}) async-start(bf16[8,2,4,32,768]{4,3,2,1,0:T(8,128)(2,1)} %get-tuple-element.138), calls=%async_computation.4 | async-start | bytes 6291456 | tf_op jit(solution)/shard_map/all_to_all | solution.py:762
  257.0 30.3 %collective-permute-start.34 = (bf16[4,24,3200]{2,1,0:T(8,128)(2,1)S(1)}, bf16[4,24,3200]{2,1,0:T(8,128)(2,1)S(1)}, u32[]{:S(2)}, u32[]{:S(2)}) collective-permute-start(bf16[4,24,3200]{2,1,0:T(8,128)(2,1)S(1)} %get-tuple-element.154), channel_id=1, source_target_pairs={{0,4},{4,8},{8,12},{12,0},{1,5},{5,9},{9,13},{13,1},{2,6},{6,10},{... | collective-permute-start | bytes 1843208 | tf_op jit(solution)/shard_map/ppermute | solution.py:729
  257.1 33.4 %collective-permute-start.35 = (bf16[4,24,3200]{2,1,0:T(8,128)(2,1)S(1)}, bf16[4,24,3200]{2,1,0:T(8,128)(2,1)S(1)}, u32[]{:S(2)}, u32[]{:S(2)}) collective-permute-start(bf16[4,24,3200]{2,1,0:T(8,128)(2,1)S(1)} %get-tuple-element.155), channel_id=1, source_target_pairs={{0,8},{4,12},{8,0},{12,4},{1,9},{5,13},{9,1},{13,5},{2,10},{6,14},... | collective-permute-start | bytes 1843208 | tf_op jit(solution)/shard_map/ppermute | solution.py:729
  258.5 32.0 %collective-permute-start.36 = (bf16[4,24,3200]{2,1,0:T(8,128)(2,1)S(1)}, bf16[4,24,3200]{2,1,0:T(8,128)(2,1)S(1)}, u32[]{:S(2)}, u32[]{:S(2)}) collective-permute-start(bf16[4,24,3200]{2,1,0:T(8,128)(2,1)S(1)} %get-tuple-element.156), channel_id=1, source_target_pairs={{0,12},{4,0},{8,4},{12,8},{1,13},{5,1},{9,5},{13,9},{2,14},{6,2},{... | collective-permute-start | bytes 1843208 | tf_op jit(solution)/shard_map/ppermute | solution.py:729
  263.8 30.3 %collective-permute-start.31 = (bf16[4,8,3840]{2,1,0:T(8,128)(2,1)S(1)}, bf16[4,8,3840]{2,1,0:T(8,128)(2,1)S(1)}, u32[]{:S(2)}, u32[]{:S(2)}) collective-permute-start(bf16[4,8,3840]{2,1,0:T(8,128)(2,1)S(1)} %get-tuple-element.150), channel_id=1, source_target_pairs={{0,1},{1,2},{2,3},{3,0},{4,5},{5,6},{6,7},{7,4},{8,9},{9,10},{10,1... | collective-permute-start | bytes 737288 | tf_op jit(solution)/shard_map/ppermute | solution.py:729
  266.1 29.2 %collective-permute-start.32 = (bf16[4,8,3840]{2,1,0:T(8,128)(2,1)S(1)}, bf16[4,8,3840]{2,1,0:T(8,128)(2,1)S(1)}, u32[]{:S(2)}, u32[]{:S(2)}) collective-permute-start(bf16[4,8,3840]{2,1,0:T(8,128)(2,1)S(1)} %get-tuple-element.151), channel_id=1, source_target_pairs={{0,2},{1,3},{2,0},{3,1},{4,6},{5,7},{6,4},{7,5},{8,10},{9,11},{10,... | collective-permute-start | bytes 737288 | tf_op jit(solution)/shard_map/ppermute | solution.py:729
  (58 other events, 528.7 us)

commit v5 on v3

--- a/solution.py
+++ b/solution.py
@@ -862,7 +862,7 @@
     attn_parts = send_ring(attn_parts, "z")
     back = over(hold(back, outer_z), dp)
 
-    inner_parts = [hold(p, attn_first) for p in inner_parts]
+    inner_parts = [hold(p, attn_away) for p in inner_parts]
     inner_parts = call_by_x(
         split_rows, "split_rows", places, inner_parts, 0,
         [(RING, 8, FF + WIDTH)] * RING, 0, [(RING, 8, FF + WIDTH)],

time: 312 us -> 312 us (level)
  no operation moved by 1% of the time
where the time goes in v5:
time: 312 us; the launch traced here: 310 us
  Pallas kernels  138 us (44%)
  starting transfers between devices  83.6 us (27%)
  waiting for transfers between devices  70.4 us (23%)
  local copies, waits for them, and re-layouts  12.7 us (4%)
  other arithmetic  3.97 us (1%)
    pallas_call x15, Pallas kernels, run(): pl.pallas_call(kernel, grid_spec=pltpu.PrefetchScalarGridSpec(num_scalar_...  138 us
    ppermute x41, starting transfers between devices, shift(): lax.ppermute(value, axis, [(i, (i + step) % size) for i in range(size)])  58.6 us
    ppermute x41, waiting for transfers between devices, shift(): lax.ppermute(value, axis, [(i, (i + step) % size) for i in range(size)])  48.3 us
    all_to_all x5, starting transfers between devices, over(): return lax.all_to_all(value, axis, split_axis=0, concat_axis=0, tiled=True)  21.3 us
    all_to_all x5, waiting for transfers between devices, over(): return lax.all_to_all(value, axis, split_axis=0, concat_axis=0, tiled=True)  13.4 us
    ppermute x2, waiting for transfers between devices, swap(): return lax.ppermute(value, axis, [(i, i ^ 1) for i in range(RING)])  8.68 us
  transfers between devices with their start and end apart: 48, of which 20 were waited for; matrix products, arithmetic and copies ran while one was open for 3% of the time, Pallas kernels for 23%

profile of v5, /device:TPU:0, one launch (start us, length us, event | category | flops | bytes accessed | tf_op | source)
XLA Modules:
  0.0 310.4 jit_solution(9887400388297595957)
XLA Ops:
  0.8 4.5 %all-to-all-start = ((bf16[8,4,32,768]{3,2,1,0:T(8,128)(2,1)}), bf16[8,4,32,768]{3,2,1,0:T(8,128)(2,1)S(1)}, u32[]{:S(2)}, u32[]{:S(2)}) async-start(bf16[8,4,32,768]{3,2,1,0:T(8,128)(2,1)} %bitcast.34), calls=%async_computation | async-start | bytes 3145728 | tf_op jit(solution)/shard_map/all_to_all | solution.py:751
  19.2 4.1 %collective-permute-start.5 = (bf16[24,2816]{1,0:T(8,128)(2,1)S(1)}, bf16[24,2816]{1,0:T(8,128)(2,1)S(1)}, u32[]{:S(2)}, u32[]{:S(2)}) collective-permute-start(bf16[24,2816]{1,0:T(8,128)(2,1)S(1)} %get-tuple-element.96.own), channel_id=1, source_target_pairs={{0,12},{4,0},{8,4},{12,8},{1,13},{5,1},{9,5},{13,9},{2,14},{6,2},{... | collective-permute-start | bytes 405512 | tf_op jit(solution)/shard_map/ppermute | solution.py:718
  23.3 3.7 %all-to-all-done.x_in = bf16[8,4,32,768]{3,2,1,0:T(8,128)(2,1)S(1)} async-done(((bf16[8,4,32,768]{3,2,1,0:T(8,128)(2,1)}), bf16[8,4,32,768]{3,2,1,0:T(8,128)(2,1)S(1)}, u32[]{:S(2)}, u32[]{:S(2)}) %all-to-all-start) | async-done | bytes 1572896 | tf_op jit(solution)/shard_map/all_to_all | solution.py:751
  29.7 3.9 %collective-permute-start.4 = (bf16[24,2816]{1,0:T(8,128)(2,1)S(1)}, bf16[24,2816]{1,0:T(8,128)(2,1)S(1)}, u32[]{:S(2)}, u32[]{:S(2)}) collective-permute-start(bf16[24,2816]{1,0:T(8,128)(2,1)S(1)} %get-tuple-element.96.own), channel_id=1, source_target_pairs={{0,8},{4,12},{8,0},{12,4},{1,9},{5,13},{9,1},{13,5},{2,10},{6,14},... | collective-permute-start | bytes 405512 | tf_op jit(solution)/shard_map/ppermute | solution.py:718
  34.6 3.4 %collective-permute-done.4.r2 = bf16[24,2816]{1,0:T(8,128)(2,1)S(1)} collective-permute-done((bf16[24,2816]{1,0:T(8,128)(2,1)S(1)}, bf16[24,2816]{1,0:T(8,128)(2,1)S(1)}, u32[]{:S(2)}, u32[]{:S(2)}) %collective-permute-start.4) | collective-permute-done | bytes 135200 | tf_op jit(solution)/shard_map/ppermute | solution.py:718
  49.3 4.9 %all-to-all-start.2 = ((bf16[4,4,48,768]{3,2,1,0:T(8,128)(2,1)}), bf16[4,4,48,768]{3,2,1,0:T(8,128)(2,1)S(1)}, u32[]{:S(2)}, u32[]{:S(2)}) async-start(bf16[4,4,48,768]{3,2,1,0:T(8,128)(2,1)} %broadcast_in_dim.10), calls=%async_computation.2 | async-start | bytes 2359296 | tf_op jit(solution)/shard_map/all_to_all | solution.py:751
  54.2 8.7 %collective-permute-done.12 = bf16[4,24,3840]{2,1,0:T(8,128)(2,1)} collective-permute-done((bf16[4,24,3840]{2,1,0:T(8,128)(2,1)S(1)}, bf16[4,24,3840]{2,1,0:T(8,128)(2,1)}, u32[]{:S(2)}, u32[]{:S(2)}) %collective-permute-start.12) | collective-permute-done | bytes 737312 | tf_op jit(solution)/shard_map/ppermute | solution.py:722
  65.3 3.9 %collective-permute-start.19 = (bf16[4,48,3840]{2,1,0:T(8,128)(2,1)}, bf16[4,48,3840]{2,1,0:T(8,128)(2,1)}, u32[]{:S(2)}, u32[]{:S(2)}) collective-permute-start(bf16[4,48,3840]{2,1,0:T(8,128)(2,1)} %pad_maximum_fusion.i0), channel_id=1, source_target_pairs={{0,8},{4,12},{8,0},{12,4},{1,9},{5,13},{9,1},{13,5},{2,10},{6,14},... | collective-permute-start | bytes 4423688 | tf_op jit(solution)/shard_map/ppermute | solution.py:718
  69.2 9.7 %all-to-all-done.2.j0 = bf16[4,4,48,768]{3,2,1,0:T(8,128)(2,1)S(1)} async-done(((bf16[4,4,48,768]{3,2,1,0:T(8,128)(2,1)}), bf16[4,4,48,768]{3,2,1,0:T(8,128)(2,1)S(1)}, u32[]{:S(2)}, u32[]{:S(2)}) %all-to-all-start.2) | async-done | bytes 1179680 | tf_op jit(solution)/shard_map/all_to_all | solution.py:751
  78.9 3.7 %all-to-all-start.1 = ((bf16[8,4,32,768]{3,2,1,0:T(8,128)(2,1)}), bf16[8,4,32,768]{3,2,1,0:T(8,128)(2,1)S(1)}, u32[]{:S(2)}, u32[]{:S(2)}) async-start(bf16[8,4,32,768]{3,2,1,0:T(8,128)(2,1)} %bitcast.7), calls=%async_computation.1 | async-start | bytes 3145728 | tf_op jit(solution)/shard_map/all_to_all | solution.py:751
  83.6 3.4 %collective-permute-start.22 = (bf16[4,4,48,768]{3,2,1,0:T(8,128)(2,1)S(1)}, bf16[4,4,48,768]{3,2,1,0:T(8,128)(2,1)}, u32[]{:S(2)}, u32[]{:S(2)}) collective-permute-start(bf16[4,4,48,768]{3,2,1,0:T(8,128)(2,1)S(1)} %all-to-all-done.2.j0), channel_id=1, source_target_pairs={{0,2},{1,3},{2,0},{3,1},{4,6},{5,7},{6,4},{7,5},{8,10},{9,11},{10,... | collective-permute-start | bytes 3538952 | tf_op jit(solution)/shard_map/ppermute | solution.py:718
  87.7 23.7 %attention_forward.1 = (bf16[768,1024]{1,0:T(8,128)(2,1)}, bf16[1024,2304]{1,0:T(8,128)(2,1)}, bf16[4,12,256,256]{3,2,1,0:T(8,128)(2,1)}, f32[4,16,256]{2,1,0:T(...) custom-call(s32[16]{0:T(128)} %copy-done.7, ...), custom_call_target="tpu_custom_call" | custom-call | flops 8000000000 | bytes 5000000 | tf_op jit(solution)/shard_map/attention_forward/pallas_call | solution.py:550
  114.8 3.4 %collective-permute-done.21.j1 = bf16[4,4,48,768]{3,2,1,0:T(8,128)(2,1)S(1)} collective-permute-done((bf16[4,4,48,768]{3,2,1,0:T(8,128)(2,1)S(1)}, bf16[4,4,48,768]{3,2,1,0:T(8,128)(2,1)S(1)}, u32[]{:S(2)}, u32[]{:S(2)}) %collective-permute-start.21) | collective-permute-done | bytes 1179680 | tf_op jit(solution)/shard_map/ppermute | solution.py:718
  122.5 65.8 %feed_forward.1 = (bf16[1024,768]{1,0:T(8,128)(2,1)}, f32[1024,768]{1,0:T(8,128)}, bf16[1024,768]{1,0:T(8,128)(2,1)}, bf16[4,384,768]{2,1,0:T(8,128)(2,1)}, bf16...) custom-call(s32[16]{0:T(128)} %pad_add_fusion.1.ids, ...), custom_call_target="tpu_custom_call" | custom-call | flops 49999998976 | bytes 40000000 | tf_op jit(solution)/shard_map/feed_forward/pallas_call | solution.py:550
  190.9 3.2 %collective-permute-done.24.refs_1_ = bf16[4,96,3072]{2,1,0:T(8,128)(2,1)S(1)} collective-permute-done((bf16[4,96,3072]{2,1,0:T(8,128)(2,1)}, bf16[4,96,3072]{2,1,0:T(8,128)(2,1)S(1)}, u32[]{:S(2)}, u32[]{:S(2)}) %collective-permute-start.24) | collective-permute-done | bytes 2359328 | tf_op jit(solution)/shard_map/ppermute | solution.py:718
  196.9 3.2 %sum_blocks.1 = (bf16[4,24,3968]{2,1,0:T(8,128)(2,1)S(1)}, bf16[4,24,3968]{2,1,0:T(8,128)(2,1)}, bf16[4,24,3968]{2,1,0:T(8,128)(2,1)}, bf16[4,24,3968]{2,1,0:T(8,128)(2,1)}) custom-call(s32[16]{0:T(128)S(1)} %copy-done.8, bf16[4,96,3072]{2,1,0:T(8,128)(2,1)S(1)} %copy-done.1, bf16[4,96,3072]{2,1,0:T(8,128)(2,1)S(1)} %collective-permute-done.24.refs_1_, ...), custom_call_target="tpu_custom_call" | custom-call | flops 1000000 | bytes 6000000 | tf_op jit(solution)/shard_map/sum_blocks/pallas_call | solution.py:550
  206.7 3.6 %all-to-all-start.3 = ((bf16[4,4,4,24,768]{4,3,2,1,0:T(8,128)(2,1)}), bf16[4,4,4,24,768]{4,3,2,1,0:T(8,128)(2,1)S(1)}, u32[]{:S(2)}, u32[]{:S(2)}) async-start(bf16[4,4,4,24,768]{4,3,2,1,0:T(8,128)(2,1)} %sum_outer.1), calls=%async_computation.3 | async-start | bytes 4718592 | tf_op jit(solution)/shard_map/all_to_all | solution.py:751
  210.4 32.1 %attention_backward.1 = (bf16[8,2,4,32,768]{4,3,2,1,0:T(8,128)(2,1)}, bf16[4,96,2432]{2,1,0:T(8,128)(2,1)}, bf16[4,96,2432]{2,1,0:T(8,128)(2,1)}) custom-call(s32[16]{0:T(128)} %pad_add_fusion.1.ids, f32[1024,768]{1,0:T(8,128)} %get-tuple-element.127.dsum, bf16[1024,768]{1,0:T(8,128)(2,1)} %get-tuple-element.128.dattn, ...), custom_call_target="tpu_custom_call" | custom-call | flops 28000000000 | bytes 30000000 | tf_op jit(solution)/shard_map/attention_backward/pallas_call | solution.py:550
  243.3 4.6 %all-to-all-start.4 = ((bf16[8,2,4,32,768]{4,3,2,1,0:T(8,128)(2,1)}), bf16[8,2,4,32,768]{4,3,2,1,0:T(8,128)(2,1)}, u32[]{:S(2)}, u32[]{:S(2)}) async-start(bf16[8,2,4,32,768]{4,3,2,1,0:T(8,128)(2,1)} %get-tuple-element.138), calls=%async_computation.4 | async-start | bytes 6291456 | tf_op jit(solution)/shard_map/all_to_all | solution.py:751
  248.5 4.0 %collective-permute-done.33.refs_2_ = bf16[4,96,2432]{2,1,0:T(8,128)(2,1)S(1)} collective-permute-done((bf16[4,96,2432]{2,1,0:T(8,128)(2,1)}, bf16[4,96,2432]{2,1,0:T(8,128)(2,1)S(1)}, u32[]{:S(2)}, u32[]{:S(2)}) %collective-permute-start.33) | collective-permute-done | bytes 1867808 | tf_op jit(solution)/shard_map/ppermute | solution.py:718
  267.5 4.1 %collective-permute-done.34.refs_1_ = bf16[4,24,3200]{2,1,0:T(8,128)(2,1)S(1)} collective-permute-done((bf16[4,24,3200]{2,1,0:T(8,128)(2,1)S(1)}, bf16[4,24,3200]{2,1,0:T(8,128)(2,1)S(1)}, u32[]{:S(2)}, u32[]{:S(2)}) %collective-permute-start.34) | collective-permute-done | bytes 614432 | tf_op jit(solution)/shard_map/ppermute | solution.py:718
  274.8 9.5 %collective-permute-done.35.refs_2_ = bf16[4,24,3200]{2,1,0:T(8,128)(2,1)S(1)} collective-permute-done((bf16[4,24,3200]{2,1,0:T(8,128)(2,1)S(1)}, bf16[4,24,3200]{2,1,0:T(8,128)(2,1)S(1)}, u32[]{:S(2)}, u32[]{:S(2)}) %collective-permute-start.35) | collective-permute-done | bytes 614432 | tf_op jit(solution)/shard_map/ppermute | solution.py:718
  293.3 3.5 %collective-permute-done.38.a2 = bf16[4,8,2304]{2,1,0:T(8,128)(2,1)S(1)} collective-permute-done((bf16[4,8,2304]{2,1,0:T(8,128)(2,1)S(1)}, bf16[4,8,2304]{2,1,0:T(8,128)(2,1)S(1)}, u32[]{:S(2)}, u32[]{:S(2)}) %collective-permute-start.38) | collective-permute-done | bytes 147488 | tf_op jit(solution)/shard_map/ppermute | solution.py:718
  303.9 3.8 %fusion = (bf16[8,1,4,32,768]{4,3,2,1,0:T(8,128)(2,1)}, bf16[8,1,4,32,768]{4,3,2,1,0:T(8,128)(2,1)}) fusion(bf16[8,2,4,32,768]{4,3,2,1,0:T(8,128)(2,1)} %all-to-all-done.4), kind=kLoop, calls=%fused_computation.19 | loop fusion | bytes 6291456 | tf_op jit(solution)/shard_map/slice | solution.py:882
  (173 shorter events, 90.7 us)
Async XLA Ops:
  0.8 26.1 %all-to-all-start = ((bf16[8,4,32,768]{3,2,1,0:T(8,128)(2,1)}), bf16[8,4,32,768]{3,2,1,0:T(8,128)(2,1)S(1)}, u32[]{:S(2)}, u32[]{:S(2)}) async-start(bf16[8,4,32,768]{3,2,1,0:T(8,128)(2,1)} %bitcast.34), calls=%async_computation | async-start | bytes 3145728 | tf_op jit(solution)/shard_map/all_to_all | solution.py:751
  19.2 14.4 %collective-permute-start.5 = (bf16[24,2816]{1,0:T(8,128)(2,1)S(1)}, bf16[24,2816]{1,0:T(8,128)(2,1)S(1)}, u32[]{:S(2)}, u32[]{:S(2)}) collective-permute-start(bf16[24,2816]{1,0:T(8,128)(2,1)S(1)} %get-tuple-element.96.own), channel_id=1, source_target_pairs={{0,12},{4,0},{8,4},{12,8},{1,13},{5,1},{9,5},{13,9},{2,14},{6,2},{... | collective-permute-start | bytes 405512 | tf_op jit(solution)/shard_map/ppermute | solution.py:718
  27.0 13.6 %collective-permute-start.11 = (bf16[24,5376]{1,0:T(8,128)(2,1)S(1)}, bf16[24,5376]{1,0:T(8,128)(2,1)S(1)}, u32[]{:S(2)}, u32[]{:S(2)}) collective-permute-start(bf16[24,5376]{1,0:T(8,128)(2,1)S(1)} %pad_maximum_fusion.1.p0), channel_id=1, source_target_pairs={{0,96},{32,0},{64,32},{96,64},{1,97},{33,1},{65,33},{97,65},{2,98}... | collective-permute-start | bytes 774152 | tf_op jit(solution)/shard_map/ppermute | solution.py:718
  43.3 19.5 %collective-permute-start.12 = (bf16[4,24,3840]{2,1,0:T(8,128)(2,1)S(1)}, bf16[4,24,3840]{2,1,0:T(8,128)(2,1)}, u32[]{:S(2)}, u32[]{:S(2)}) collective-permute-start(bf16[4,24,3840]{2,1,0:T(8,128)(2,1)S(1)} %get-tuple-element.101), channel_id=1, source_target_pairs={{0,4},{4,0},{8,12},{12,8},{1,5},{5,1},{9,13},{13,9},{2,6},{6,2},{1... | collective-permute-start | bytes 2211848 | tf_op jit(solution)/shard_map/ppermute | solution.py:722
  45.3 37.3 %collective-permute-start.16 = (bf16[96,2816]{1,0:T(8,128)(2,1)S(1)}, bf16[96,2816]{1,0:T(8,128)(2,1)}, u32[]{:S(2)}, u32[]{:S(2)}) collective-permute-start(bf16[96,2816]{1,0:T(8,128)(2,1)S(1)} %bitcast.28), channel_id=1, source_target_pairs={{0,96},{32,0},{64,32},{96,64},{1,97},{33,1},{65,33},{97,65},{2,98}... | collective-permute-start | bytes 1622024 | tf_op jit(solution)/shard_map/ppermute | solution.py:718
  45.9 36.7 %collective-permute-start.14 = (bf16[96,2816]{1,0:T(8,128)(2,1)S(1)}, bf16[96,2816]{1,0:T(8,128)(2,1)}, u32[]{:S(2)}, u32[]{:S(2)}) collective-permute-start(bf16[96,2816]{1,0:T(8,128)(2,1)S(1)} %bitcast.29), channel_id=1, source_target_pairs={{0,64},{32,96},{64,0},{96,32},{1,65},{33,97},{65,1},{97,33},{2,66}... | collective-permute-start | bytes 1622024 | tf_op jit(solution)/shard_map/ppermute | solution.py:718
  47.4 35.2 %collective-permute-start.7 = (bf16[96,2816]{1,0:T(8,128)(2,1)S(1)}, bf16[96,2816]{1,0:T(8,128)(2,1)}, u32[]{:S(2)}, u32[]{:S(2)}) collective-permute-start(bf16[96,2816]{1,0:T(8,128)(2,1)S(1)} %bitcast.30), channel_id=1, source_target_pairs={{0,32},{32,64},{64,96},{96,0},{1,33},{33,65},{65,97},{97,1},{2,34}... | collective-permute-start | bytes 1622024 | tf_op jit(solution)/shard_map/ppermute | solution.py:718
  49.3 29.6 %all-to-all-start.2 = ((bf16[4,4,48,768]{3,2,1,0:T(8,128)(2,1)}), bf16[4,4,48,768]{3,2,1,0:T(8,128)(2,1)S(1)}, u32[]{:S(2)}, u32[]{:S(2)}) async-start(bf16[4,4,48,768]{3,2,1,0:T(8,128)(2,1)} %broadcast_in_dim.10), calls=%async_computation.2 | async-start | bytes 2359296 | tf_op jit(solution)/shard_map/all_to_all | solution.py:751
  65.3 46.3 %collective-permute-start.19 = (bf16[4,48,3840]{2,1,0:T(8,128)(2,1)}, bf16[4,48,3840]{2,1,0:T(8,128)(2,1)}, u32[]{:S(2)}, u32[]{:S(2)}) collective-permute-start(bf16[4,48,3840]{2,1,0:T(8,128)(2,1)} %pad_maximum_fusion.i0), channel_id=1, source_target_pairs={{0,8},{4,12},{8,0},{12,4},{1,9},{5,13},{9,1},{13,5},{2,10},{6,14},... | collective-permute-start | bytes 4423688 | tf_op jit(solution)/shard_map/ppermute | solution.py:718
  69.2 14.4 %collective-permute-start.6 = (bf16[96,2816]{1,0:T(8,128)(2,1)S(1)}, bf16[96,2816]{1,0:T(8,128)(2,1)}, u32[]{:S(2)}, u32[]{:S(2)}) collective-permute-start(bf16[96,2816]{1,0:T(8,128)(2,1)S(1)} %bitcast.31), channel_id=1, source_target_pairs={{0,16},{16,0},{1,17},{17,1},{2,18},{18,2},{3,19},{19,3},{4,20},{20... | collective-permute-start | bytes 1622024 | tf_op jit(solution)/shard_map/ppermute | solution.py:718
  78.9 32.6 %all-to-all-start.1 = ((bf16[8,4,32,768]{3,2,1,0:T(8,128)(2,1)}), bf16[8,4,32,768]{3,2,1,0:T(8,128)(2,1)S(1)}, u32[]{:S(2)}, u32[]{:S(2)}) async-start(bf16[8,4,32,768]{3,2,1,0:T(8,128)(2,1)} %bitcast.7), calls=%async_computation.1 | async-start | bytes 3145728 | tf_op jit(solution)/shard_map/all_to_all | solution.py:751
  83.6 29.8 %collective-permute-start.22 = (bf16[4,4,48,768]{3,2,1,0:T(8,128)(2,1)S(1)}, bf16[4,4,48,768]{3,2,1,0:T(8,128)(2,1)}, u32[]{:S(2)}, u32[]{:S(2)}) collective-permute-start(bf16[4,4,48,768]{3,2,1,0:T(8,128)(2,1)S(1)} %all-to-all-done.2.j0), channel_id=1, source_target_pairs={{0,2},{1,3},{2,0},{3,1},{4,6},{5,7},{6,4},{7,5},{8,10},{9,11},{10,... | collective-permute-start | bytes 3538952 | tf_op jit(solution)/shard_map/ppermute | solution.py:718
  190.8 13.5 %collective-permute-start.26 = (bf16[4,384,768]{2,1,0:T(8,128)(2,1)}, bf16[4,384,768]{2,1,0:T(8,128)(2,1)S(1)}, u32[]{:S(2)}, u32[]{:S(2)}) collective-permute-start(bf16[4,384,768]{2,1,0:T(8,128)(2,1)} %get-tuple-element.126), channel_id=1, source_target_pairs={{0,16},{16,0},{1,17},{17,1},{2,18},{18,2},{3,19},{19,3},{4,20},{20... | collective-permute-start | bytes 7077896 | tf_op jit(solution)/shard_map/ppermute | solution.py:718
  201.0 46.9 %collective-permute-start.27 = (bf16[4,24,3968]{2,1,0:T(8,128)(2,1)}, bf16[4,24,3968]{2,1,0:T(8,128)(2,1)}, u32[]{:S(2)}, u32[]{:S(2)}) collective-permute-start(bf16[4,24,3968]{2,1,0:T(8,128)(2,1)} %get-tuple-element.140), channel_id=1, source_target_pairs={{0,4},{4,8},{8,12},{12,0},{1,5},{5,9},{9,13},{13,1},{2,6},{6,10},{... | collective-permute-start | bytes 2285576 | tf_op jit(solution)/shard_map/ppermute | solution.py:718
  201.0 46.9 %collective-permute-start.28 = (bf16[4,24,3968]{2,1,0:T(8,128)(2,1)}, bf16[4,24,3968]{2,1,0:T(8,128)(2,1)}, u32[]{:S(2)}, u32[]{:S(2)}) collective-permute-start(bf16[4,24,3968]{2,1,0:T(8,128)(2,1)} %get-tuple-element.142), channel_id=1, source_target_pairs={{0,8},{4,12},{8,0},{12,4},{1,9},{5,13},{9,1},{13,5},{2,10},{6,14},... | collective-permute-start | bytes 2285576 | tf_op jit(solution)/shard_map/ppermute | solution.py:718
  201.6 46.3 %collective-permute-start.29 = (bf16[4,24,3968]{2,1,0:T(8,128)(2,1)}, bf16[4,24,3968]{2,1,0:T(8,128)(2,1)}, u32[]{:S(2)}, u32[]{:S(2)}) collective-permute-start(bf16[4,24,3968]{2,1,0:T(8,128)(2,1)} %get-tuple-element.144), channel_id=1, source_target_pairs={{0,12},{4,0},{8,4},{12,8},{1,13},{5,1},{9,5},{13,9},{2,14},{6,2},{... | collective-permute-start | bytes 2285576 | tf_op jit(solution)/shard_map/ppermute | solution.py:718
  206.7 35.7 %all-to-all-start.3 = ((bf16[4,4,4,24,768]{4,3,2,1,0:T(8,128)(2,1)}), bf16[4,4,4,24,768]{4,3,2,1,0:T(8,128)(2,1)S(1)}, u32[]{:S(2)}, u32[]{:S(2)}) async-start(bf16[4,4,4,24,768]{4,3,2,1,0:T(8,128)(2,1)} %sum_outer.1), calls=%async_computation.3 | async-start | bytes 4718592 | tf_op jit(solution)/shard_map/all_to_all | solution.py:751
  243.3 60.6 %all-to-all-start.4 = ((bf16[8,2,4,32,768]{4,3,2,1,0:T(8,128)(2,1)}), bf16[8,2,4,32,768]{4,3,2,1,0:T(8,128)(2,1)}, u32[]{:S(2)}, u32[]{:S(2)}) async-start(bf16[8,2,4,32,768]{4,3,2,1,0:T(8,128)(2,1)} %get-tuple-element.138), calls=%async_computation.4 | async-start | bytes 6291456 | tf_op jit(solution)/shard_map/all_to_all | solution.py:751
  253.9 17.7 %collective-permute-start.34 = (bf16[4,24,3200]{2,1,0:T(8,128)(2,1)S(1)}, bf16[4,24,3200]{2,1,0:T(8,128)(2,1)S(1)}, u32[]{:S(2)}, u32[]{:S(2)}) collective-permute-start(bf16[4,24,3200]{2,1,0:T(8,128)(2,1)S(1)} %get-tuple-element.154), channel_id=1, source_target_pairs={{0,4},{4,8},{8,12},{12,0},{1,5},{5,9},{9,13},{13,1},{2,6},{6,10},{... | collective-permute-start | bytes 1843208 | tf_op jit(solution)/shard_map/ppermute | solution.py:718
  254.8 29.4 %collective-permute-start.35 = (bf16[4,24,3200]{2,1,0:T(8,128)(2,1)S(1)}, bf16[4,24,3200]{2,1,0:T(8,128)(2,1)S(1)}, u32[]{:S(2)}, u32[]{:S(2)}) collective-permute-start(bf16[4,24,3200]{2,1,0:T(8,128)(2,1)S(1)} %get-tuple-element.155), channel_id=1, source_target_pairs={{0,8},{4,12},{8,0},{12,4},{1,9},{5,13},{9,1},{13,5},{2,10},{6,14},... | collective-permute-start | bytes 1843208 | tf_op jit(solution)/shard_map/ppermute | solution.py:718
  257.0 27.9 %collective-permute-start.36 = (bf16[4,24,3200]{2,1,0:T(8,128)(2,1)S(1)}, bf16[4,24,3200]{2,1,0:T(8,128)(2,1)S(1)}, u32[]{:S(2)}, u32[]{:S(2)}) collective-permute-start(bf16[4,24,3200]{2,1,0:T(8,128)(2,1)S(1)} %get-tuple-element.156), channel_id=1, source_target_pairs={{0,12},{4,0},{8,4},{12,8},{1,13},{5,1},{9,5},{13,9},{2,14},{6,2},{... | collective-permute-start | bytes 1843208 | tf_op jit(solution)/shard_map/ppermute | solution.py:718
  262.6 28.2 %collective-permute-start.30 = (bf16[4,8,3840]{2,1,0:T(8,128)(2,1)S(1)}, bf16[4,8,3840]{2,1,0:T(8,128)(2,1)S(1)}, u32[]{:S(2)}, u32[]{:S(2)}) collective-permute-start(bf16[4,8,3840]{2,1,0:T(8,128)(2,1)S(1)} %get-tuple-element.147), channel_id=1, source_target_pairs={{0,1},{1,2},{2,3},{3,0},{4,5},{5,6},{6,7},{7,4},{8,9},{9,10},{10,1... | collective-permute-start | bytes 737288 | tf_op jit(solution)/shard_map/ppermute | solution.py:718
  264.8 27.4 %collective-permute-start.31 = (bf16[4,8,3840]{2,1,0:T(8,128)(2,1)S(1)}, bf16[4,8,3840]{2,1,0:T(8,128)(2,1)S(1)}, u32[]{:S(2)}, u32[]{:S(2)}) collective-permute-start(bf16[4,8,3840]{2,1,0:T(8,128)(2,1)S(1)} %get-tuple-element.148), channel_id=1, source_target_pairs={{0,2},{1,3},{2,0},{3,1},{4,6},{5,7},{6,4},{7,5},{8,10},{9,11},{10,... | collective-permute-start | bytes 737288 | tf_op jit(solution)/shard_map/ppermute | solution.py:718
  271.6 20.6 %collective-permute-start.32 = (bf16[4,8,3840]{2,1,0:T(8,128)(2,1)S(1)}, bf16[4,8,3840]{2,1,0:T(8,128)(2,1)S(1)}, u32[]{:S(2)}, u32[]{:S(2)}) collective-permute-start(bf16[4,8,3840]{2,1,0:T(8,128)(2,1)S(1)} %get-tuple-element.149), channel_id=1, source_target_pairs={{0,3},{1,0},{2,1},{3,2},{4,7},{5,4},{6,5},{7,6},{8,11},{9,8},{10,9... | collective-permute-start | bytes 737288 | tf_op jit(solution)/shard_map/ppermute | solution.py:718
  (58 other events, 523.5 us)
